TPU v7x, 512 devices: a whole 4x8x8 slice. The times are simulated.
512 devices in a mesh: dp: 32 (over y, x), tm: 16 (over z, core).
Axes of the slice: x: 4, y: 8, z: 8, core: 2. Of those that a mesh axis runs over, the one named last changes fastest.
Arguments:
- pixels: bfloat16 [32, 16, 32, 192], P('dp', 'tm'), may hold values from -1 to 1
- counts: int32 [16, 32, 32], P('tm'), may hold values from 0 to 2, as said below
- clip_lengths: int32 [32, 4], P('dp'), may hold values from 1 to 17, 64 in all within a row
- in_weight: bfloat16 [3, 3, 3, 3, 128], replicated, may hold values from -0.625 to 0.625
- in_bias: float32 [128], replicated, may hold values from -3 to 3
- norm1_gain: float32 [128], replicated, may hold values from 0.5 to 1.5
- norm1_bias: float32 [128], replicated, may hold values from -3 to 3
- conv1_weight: bfloat16 [3, 3, 3, 128, 128], replicated, may hold values from -0.109375 to 0.109375
- norm2_gain: float32 [128], replicated, may hold values from 0.5 to 1.5
- norm2_bias: float32 [128], replicated, may hold values from -3 to 3
- conv2_weight: bfloat16 [3, 3, 3, 128, 128], replicated, may hold values from -0.109375 to 0.109375
- down_weight: bfloat16 [3, 3, 128, 128], replicated, may hold values from -0.1875 to 0.1875
Outputs:
- latents: bfloat16 [32, 16, 32, 2048], P('dp', 'tm')
Inputs may be any that keep to these rules, and one draw needn't show every extreme that they name: For each time block, every row and every column of counts sums to 32, and every row holds exactly one entry equal to 2. `clip_lengths`: each row sums to 64, and its longest clip has exactly 17 frames.
All inputs are finite; a program needn't handle non-finite values.
Results may differ from a plain program's by a relative error of at most 0.011.
Values may be sent and summed in bfloat16 or wider, within the bound.
No kernel may reach another device: no remote copies, remote signals or barrier semaphores. Data moves between devices by JAX's collectives and lax.ppermute only.
A program may use at most 128 MiB of HBM per device.

v0:
```python
import jax
import jax.numpy as jnp
from jax import lax
from jax.experimental import pallas as pl
from jax.experimental.pallas import tpu as pltpu
from jax.sharding import PartitionSpec as P


F32 = jnp.float32
BF16 = jnp.bfloat16
EPS = 1e-06
NDP = 32
NTM = 16
FT = 4
CLIPS = 4
CH = 128
AREA = 512
FRAME_N = AREA * 4
VMEM_LIMIT = 24 * 1024 * 1024


def iota(shape, dim):
    return lax.broadcasted_iota(jnp.int32, shape, dim)


def onehot(cond):
    return jnp.where(cond, 1.0, 0.0).astype(BF16)


def mm(a, b):
    return jnp.dot(a, b, preferred_element_type=F32)


def pick_lane(values, lane):
    return jnp.sum(jnp.where(iota(values.shape, 1) == lane, values, 0.0), axis=1, keepdims=True)


def pack_kernel(counts_ref, pixels_ref, out_ref):
    station = lax.axis_index("dp")
    table = counts_ref[0].astype(F32)
    sub, lane = iota((NDP, NDP), 0), iota((NDP, NDP), 1)
    row = jnp.sum(jnp.where(sub == station, table, 0.0), axis=0, keepdims=True)
    recv = jnp.sum(jnp.where(sub < station, table, 0.0), axis=0, keepdims=True)
    row8 = jnp.broadcast_to(row, (8, NDP))
    start = mm(row8.astype(BF16), onehot(sub < lane))[0:1]
    spread = (iota((256, NDP), 0) // 8 == iota((256, NDP), 1)).astype(F32)
    count_i = jnp.sum(spread * row, axis=1, keepdims=True)
    start_i = jnp.sum(spread * start, axis=1, keepdims=True)
    recv_i = jnp.sum(spread * recv, axis=1, keepdims=True)
    i, m = iota((256, 128), 0), iota((256, 128), 1)
    slot = ((i // 4) % 2).astype(F32)
    valid = slot < count_i
    unit = (m % 32).astype(F32)
    place = onehot((unit == start_i + slot) & (m // 32 == i % 4) & valid)
    src, dst = iota((192, 128), 0), iota((192, 128), 1)
    t = dst % 32
    wanted = 24 * (dst // 32) - 3 + t
    inside = (t < 30) & (dst < 64) & (wanted >= 0) & (wanted < 48)
    pixels = pixels_ref[0, 0]
    rows = [mm(pixels, onehot((src == 48 * q + wanted) & inside)).astype(BF16) for q in range(4)]
    packed = mm(place, jnp.concatenate(rows, axis=0))
    packed = jnp.where(m == 64, jnp.where(valid, recv_i + slot, 255.0), packed)
    out_ref[...] = packed.astype(BF16)


def spread_kernel(weight_ref, out_ref, taps_ref):
    taps_ref[...] = jnp.zeros_like(taps_ref)
    for a in range(3):
        for b in range(3):
            for c in range(3):
                taps_ref[(a * 3 + b) * 3 + c, 0:3, :] = weight_ref[a, b, c].astype(F32)
    taps = taps_ref[...].reshape(27 * 8, CH).astype(BF16)
    r, j = iota((384, 216), 0), iota((384, 216), 1)
    dyi = (r // 32) % 4
    row_key = jnp.where(dyi < 3, ((2 - r // 128) * 3 + dyi) * 64 + r % 32, -1000)
    tap, color = j // 8, j % 8
    col_key = jnp.where(color < 3, (tap // 3) * 64 + (tap % 3) * 3 + color, -5000)
    diff = row_key - col_key
    for l in range(8):
        out_ref[:, l * CH : (l + 1) * CH] = mm(onehot(diff == 3 * l), taps).astype(BF16)


def clip_ends(lengths_ref):
    ends, total = [], 0
    for c in range(CLIPS):
        total = total + lengths_ref[0, c]
        ends.append(total)
    return ends


def clip_of(ends, frame):
    ident = jnp.int32(0)
    begin = jnp.int32(0)
    for c in range(CLIPS - 1):
        past = frame >= ends[c]
        ident = jnp.where(past, jnp.int32(c + 1), ident)
        begin = jnp.where(past, ends[c], begin)
    return ident, begin


def group_sum(x):
    lane = iota(x.shape, 1)
    x = x + pltpu.roll(x, 127, 1)
    x = x + pltpu.roll(x, 126, 1)
    x = jnp.where(lane % 4 == 0, x, 0.0)
    x = x + pltpu.roll(x, 1, 1)
    return x + pltpu.roll(x, 2, 1)


def shift_k(tile, step):
    moved = pltpu.roll(tile, step % 8, 0)
    return jnp.where(iota(tile.shape, 0) == (0 if step == 1 else 7), 0.0, moved)


def unpack_rows(arrived):
    wide = arrived.astype(F32)
    pos = wide[:, 64:65].astype(jnp.int32)
    i, m = iota((256, 128), 0), iota((256, 128), 1)
    target = (pos // 8) * 32 + (i % 4) * 8 + pos % 8
    select = jnp.where((m == target) & (pos < 32), 1.0, 0.0)
    rows = mm(select.T.astype(BF16), arrived)
    return jnp.where(iota((128, 128), 1) < 64, rows, 0.0)


def base_kernel(lengths_ref, own_ref, prev_ref, matrix_ref, bias_ref, base_ref, stat_ref, x_ref, lhs_ref):
    column = lax.axis_index("tm")
    low = iota((8, 128), 1) < 32
    for block, ref in enumerate((prev_ref, own_ref)):
        rows = unpack_rows(ref[...])
        for f in range(4):
            tiles = [rows[f * 32 + q * 8 : f * 32 + q * 8 + 8] for q in range(4)]
            out = []
            for q in range(4):
                above = tiles[q - 1] if q > 0 else shift_k(tiles[3], 1)
                below = tiles[q + 1] if q < 3 else shift_k(tiles[0], -1)
                for h in range(2):
                    a, b, c = above, tiles[q], below
                    if h:
                        a, b, c = (pltpu.roll(v, 96, 1) for v in (a, b, c))
                    a, b, c = (jnp.where(low, v, 0.0) for v in (a, b, c))
                    out.append(a + pltpu.roll(b, 32, 1) + pltpu.roll(c, 64, 1))
            x_ref[block * 4 + f] = jnp.concatenate(out, axis=0).astype(BF16)
    ends = clip_ends(lengths_ref)
    for o in range(6):
        frame = column * FT - 2 + o
        unused, begin = clip_of(ends, frame)
        for lag in range(3):
            p = jnp.clip(jnp.maximum(frame - lag, begin) - (column * FT - 4), 0, 7)
            lhs_ref[o * 64 : (o + 1) * 64, lag * 128 : (lag + 1) * 128] = x_ref[p]
    bias = bias_ref[...]
    sums = [jnp.zeros((1, CH), F32)] * 4
    for pair in range(4):
        both = mm(lhs_ref[...], matrix_ref[:, pair * 256 : (pair + 1) * 256])
        for half in range(2):
            value = (both[:, half * CH : (half + 1) * CH] + bias).astype(BF16)
            for o in range(6):
                part = value[o * 64 : (o + 1) * 64]
                base_ref[o, pair * 2 + half] = part.reshape(4, 16, CH)
                if o >= 2:
                    sums[o - 2] = sums[o - 2] + jnp.sum(part.astype(F32), axis=0, keepdims=True)
    total = group_sum(jnp.concatenate(sums, axis=0))
    devs = []
    for o in range(4):
        wide = base_ref[o + 2].astype(F32).reshape(AREA, CH) - total[o : o + 1] * (1.0 / FRAME_N)
        devs.append(jnp.sum(wide * wide, axis=0, keepdims=True))
    stats = jnp.concatenate([total, group_sum(jnp.concatenate(devs, axis=0))], axis=0)
    for j in range(NTM):
        stat_ref[j] = stats


def clip_scales(stats, lengths_ref, ends, gain, norm_ref):
    frame = iota((NTM, 8, CH), 0) * FT + iota((NTM, 8, CH), 1) % 4
    is_sum = iota((NTM, 8, CH), 1) < 4
    for c in range(CLIPS):
        inside = frame < ends[c]
        if c:
            inside = inside & (frame >= ends[c - 1])
        size = (lengths_ref[0, c] * FRAME_N).astype(F32)
        kept = jnp.sum(jnp.where(inside & is_sum, stats, 0.0), axis=0)
        mean = jnp.sum(kept, axis=0, keepdims=True) / size
        off = stats * (1.0 / FRAME_N) - mean
        dev = jnp.where(is_sum, FRAME_N * (off * off), stats)
        kept = jnp.sum(jnp.where(inside, dev, 0.0), axis=0)
        var = jnp.sum(kept, axis=0, keepdims=True) / size
        norm_ref[c, 0:1, :] = mean
        norm_ref[c, 1:2, :] = lax.rsqrt(var + EPS) * gain


def store_padded(act_ref, o, place, tiles):
    column = []
    for h in range(2):
        own = [tiles[q][h] for q in range(4)]
        column.append([shift_k(own[3], 1)] + own + [shift_k(own[0], -1)])
    flat = [column[h][q] for q in range(6) for h in range(2)]
    act_ref[o, place] = jnp.concatenate(flat, axis=0).astype(BF16).reshape(6, 16, CH)


def norm_frame(value_of, act_ref, o, mean, scale, bias):
    zero = jnp.zeros((8, CH), F32)
    for l in range(8):
        v = (value_of(l).astype(F32).reshape(64, CH) - mean) * scale + bias
        v = v / (1.0 + jnp.exp(-v))
        tiles = [[v[q * 16 + h * 8 : q * 16 + h * 8 + 8] for h in range(2)] for q in range(4)]
        store_padded(act_ref, o, l + 1, tiles)
        if l == 0:
            store_padded(act_ref, o, 9, [[tiles[q][1], zero] for q in range(4)])
        if l == 7:
            store_padded(act_ref, o, 0, [[zero, tiles[q][0]] for q in range(4)])


def conv_frame(act_ref, weight_ref, picks):
    total = None
    for lag in range(3):
        taps = []
        for row in range(3):
            for col in range(3):
                taps.append(act_ref[picks[lag], col : col + 8, row : row + 4].reshape(AREA, CH))
        matrix = weight_ref[2 - lag].reshape(9 * CH, CH)
        part = mm(jnp.concatenate(taps, axis=1), matrix)
        total = part if total is None else total + part
    return total


def frame_picks(ends, column, o):
    frame = column * FT - 2 + o
    unused, begin = clip_of(ends, frame)
    return [jnp.clip(jnp.maximum(frame - lag, begin) - (column * FT - 2), 0, 5) for lag in range(3)]


def conv1_kernel(
    lengths_ref, base_ref, stats_ref, gain_ref, bias_ref, weight_ref,
    middle_ref, tail_ref, stat_ref, act_ref, norm_ref, own_ref,
):
    column = lax.axis_index("tm")
    ends = clip_ends(lengths_ref)
    clip_scales(stats_ref[...], lengths_ref, ends, gain_ref[...], norm_ref)
    bias = bias_ref[...]

    def norm_step(o, carry):
        ident, unused = clip_of(ends, column * FT - 2 + o)
        norm_frame(lambda l: base_ref[o, l], act_ref, o, norm_ref[ident, 0:1, :], norm_ref[ident, 1:2, :], bias)
        return carry

    lax.fori_loop(0, 6, norm_step, 0)

    def conv_step(f, carry):
        total = conv_frame(act_ref, weight_ref, frame_picks(ends, column, f + 2)).astype(BF16)
        middle_ref[f] = total.reshape(8, 4, 16, CH)
        wide = total.astype(F32)
        sums = group_sum(jnp.broadcast_to(jnp.sum(wide, axis=0, keepdims=True), (8, CH)))
        wide = wide - sums[0:1] * (1.0 / FRAME_N)
        devs = group_sum(jnp.broadcast_to(jnp.sum(wide * wide, axis=0, keepdims=True), (8, CH)))
        own_ref[f] = sums
        own_ref[f + 4] = devs
        return carry

    lax.fori_loop(0, 4, conv_step, 0)
    tail_ref[...] = middle_ref[2:4]
    stats = jnp.concatenate([own_ref[n, 0:1, :] for n in range(8)], axis=0)
    for j in range(NTM):
        stat_ref[j] = stats


def conv2_kernel(
    lengths_ref, counts_ref, base_ref, middle_ref, lead_ref, stats_ref, gain_ref, bias_ref, weight_ref, down_ref,
    out_ref, act_ref, norm_ref, resid_ref, latent_ref,
):
    column = lax.axis_index("tm")
    station = lax.axis_index("dp")
    ends = clip_ends(lengths_ref)
    clip_scales(stats_ref[...], lengths_ref, ends, gain_ref[...], norm_ref)
    bias = bias_ref[...]

    def norm_step(source):
        def step(o, carry):
            ident, unused = clip_of(ends, column * FT - 2 + o)
            value_of = (lambda l: lead_ref[o, l]) if source == 0 else (lambda l: middle_ref[o - 2, l])
            norm_frame(value_of, act_ref, o, norm_ref[ident, 0:1, :], norm_ref[ident, 1:2, :], bias)
            return carry

        return step

    lax.fori_loop(0, 2, norm_step(0), 0)
    lax.fori_loop(2, 6, norm_step(1), 0)
    down = down_ref[...].reshape(9 * CH, CH)

    def conv_step(f, carry):
        total = conv_frame(act_ref, weight_ref, frame_picks(ends, column, f + 2))
        resid = base_ref[f + 2].astype(F32).reshape(AREA, CH) + total
        resid = resid.astype(BF16).astype(F32)
        zero = jnp.zeros((8, CH), F32)

        def put(l, tiles):
            flat = [tiles[q][h] for q in range(4) for h in range(2)]
            flat = flat + [shift_k(tiles[0][h], -1) for h in range(2)]
            resid_ref[l] = jnp.concatenate(flat, axis=0).astype(BF16).reshape(5, 16, CH)

        for l in range(8):
            v = resid[l * 64 : (l + 1) * 64]
            tiles = [[v[q * 16 + h * 8 : q * 16 + h * 8 + 8] for h in range(2)] for q in range(4)]
            put(l, tiles)
            if l == 0:
                put(8, [[tiles[q][1], zero] for q in range(4)])
        taps = []
        for row in range(3):
            for col in range(3):
                parts = [resid_ref[2 * j + col, 2 * par + row] for j in range(4) for par in range(2)]
                taps.append(jnp.concatenate(parts, axis=0))
        latent = mm(jnp.concatenate(taps, axis=1), down)
        for j in range(4):
            for w in range(4):
                latent_ref[w, pl.ds(f * 8, 8), j * CH : (j + 1) * CH] = latent[j * 32 + w * 8 : j * 32 + w * 8 + 8]
        return carry

    lax.fori_loop(0, 4, conv_step, 0)
    table = counts_ref[0].astype(F32).astype(BF16)
    loader, other = iota((256, NDP), 0) // 8, iota((256, NDP), 1)
    count_i = pick_lane(mm(onehot(loader == other), table), station)
    start_i = pick_lane(mm(onehot(other < loader), table), station)
    i, m = iota((256, 128), 0), iota((256, 128), 1)
    slot = ((i // 4) % 2).astype(F32)
    place = onehot(((m % 32).astype(F32) == start_i + slot) & (m // 32 == i % 4) & (slot < count_i))
    out_ref[...] = mm(place, latent_ref[...].reshape(128, 512).astype(BF16)).astype(BF16)


def return_kernel(counts_ref, back_ref, out_ref):
    station = lax.axis_index("dp")
    table = counts_ref[0].astype(F32)
    sub, lane = iota((NDP, NDP), 0), iota((NDP, NDP), 1)
    row = jnp.sum(jnp.where(sub == station, table, 0.0), axis=0, keepdims=True)
    row8 = jnp.broadcast_to(row, (8, NDP)).astype(BF16)
    encoder, other = iota((NDP, 256), 1) // 8, iota((NDP, 256), 0)
    count_i = mm(row8, onehot(encoder == other))[0:1]
    start_i = mm(row8, onehot(other < encoder))[0:1]
    r, i = iota((128, 256), 0), iota((128, 256), 1)
    slot = ((i // 4) % 2).astype(F32)
    select = onehot(((r % 32).astype(F32) == start_i + slot) & (r // 32 == i % 4) & (slot < count_i))
    units = mm(select, back_ref[...]).astype(BF16)
    for w in range(4):
        out_ref[0, 0, :, w * 512 : (w + 1) * 512] = units[w * 32 : (w + 1) * 32]


VMEM = pl.BlockSpec(memory_space=pltpu.VMEM)
SMEM = pl.BlockSpec(memory_space=pltpu.SMEM)


def kernel_call(body, name, in_specs, outs, scratch=(), flops=0, bytes_accessed=1 << 20):
    outs = [jax.ShapeDtypeStruct(shape, dtype) for shape, dtype in outs]
    return pl.pallas_call(
        body,
        name=name,
        in_specs=in_specs,
        out_specs=[VMEM] * len(outs) if len(outs) > 1 else VMEM,
        out_shape=outs if len(outs) > 1 else outs[0],
        scratch_shapes=list(scratch),
        compiler_params=pltpu.CompilerParams(vmem_limit_bytes=VMEM_LIMIT),
        cost_estimate=pl.CostEstimate(flops=flops, bytes_accessed=bytes_accessed, transcendentals=0),
    )


def per_device(
    pixels,
    counts,
    clip_lengths,
    in_weight,
    in_bias,
    norm1_gain,
    norm1_bias,
    conv1_weight,
    norm2_gain,
    norm2_bias,
    conv2_weight,
    down_weight,
):
    row = lambda v: v.reshape(1, CH)
    packed = kernel_call(pack_kernel, "pack", [VMEM] * 2, [((256, 128), BF16)])(counts, pixels)
    arrived = lax.all_to_all(packed, "dp", split_axis=0, concat_axis=0, tiled=True)
    matrix = kernel_call(
        spread_kernel, "spread", [VMEM], [((384, 8 * CH), BF16)], [pltpu.VMEM((27, 8, CH), F32)], flops=1 << 28
    )(in_weight)
    onward = [(source, source + 1) for source in range(NTM - 1)]
    before = lax.ppermute(arrived, "tm", onward)
    base, stats = kernel_call(
        base_kernel,
        "base",
        [SMEM] + [VMEM] * 4,
        [((6, 8, 4, 16, CH), BF16), ((NTM, 8, CH), F32)],
        [pltpu.VMEM((8, 64, 128), BF16), pltpu.VMEM((384, 384), BF16)],
    )(clip_lengths, arrived, before, matrix, row(in_bias))
    stats = lax.all_to_all(stats, "tm", split_axis=0, concat_axis=0, tiled=True)
    act = pltpu.VMEM((6, 10, 6, 16, CH), BF16)
    norm = pltpu.VMEM((CLIPS, 8, CH), F32)
    middle, tail, stats = kernel_call(
        conv1_kernel,
        "conv1",
        [SMEM] + [VMEM] * 5,
        [((4, 8, 4, 16, CH), BF16), ((2, 8, 4, 16, CH), BF16), ((NTM, 8, CH), F32)],
        [act, norm, pltpu.VMEM((8, 8, CH), F32)],
        flops=1 << 31,
    )(clip_lengths, base, stats, row(norm1_gain), row(norm1_bias), conv1_weight)
    lead = lax.ppermute(tail, "tm", onward)
    stats = lax.all_to_all(stats, "tm", split_axis=0, concat_axis=0, tiled=True)
    packed = kernel_call(
        conv2_kernel,
        "conv2",
        [SMEM] + [VMEM] * 9,
        [((256, 512), BF16)],
        [act, norm, pltpu.VMEM((9, 5, 16, CH), BF16), pltpu.VMEM((4, 32, 512), F32)],
        flops=1 << 31,
    )(clip_lengths, counts, base, middle, lead, stats, row(norm2_gain), row(norm2_bias), conv2_weight, down_weight)
    returned = lax.all_to_all(packed, "dp", split_axis=0, concat_axis=0, tiled=True)
    return kernel_call(return_kernel, "place", [VMEM] * 2, [((1, 1, 32, 2048), BF16)])(counts, returned)


def solution(mesh):
    in_specs = (
        P("dp", "tm", None, None),
        P("tm", None, None),
        P("dp", None),
        P(),
        P(),
        P(),
        P(),
        P(),
        P(),
        P(),
        P(),
        P(),
    )
    out_specs = P("dp", "tm", None, None)
    return jax.shard_map(
        per_device, mesh=mesh, in_specs=in_specs, out_specs=out_specs, check_vma=False
    )
```

profile of v0, /device:TPU:1, one launch (start us, length us, event | category | flops | bytes accessed | tf_op | source)
XLA Modules:
  0.0 96.8 jit_solution(7127433580322278541)
XLA Ops:
  0.0 0.0 copy-start
  0.0 0.7 copy-done
  0.7 0.0 copy-start.2
  0.7 0.7 copy-done.2
  1.4 0.4 pack.1
  1.8 0.0 copy-start.8
  1.8 19.1 %all_to_all.32 = bf16[32,8,128]{2,1,0:T(8,128)(2,1)S(1)} all-to-all(bf16[32,8,128]{2,1,0:T(8,128)(2,1)S(1)} %bitcast.13), channel_id=1, replica_groups=mesh['dp'=32,'tm'=16] {'dp'}, dimensions={0} | all-to-all | bytes 131072 | tf_op jit(solution)/shard_map/all_to_all | solution.py:377
  20.9 0.0 copy-start.5
  20.9 6.1 %collective-permute-start = (bf16[256,128]{1,0:T(8,128)(2,1)S(1)}, bf16[256,128]{1,0:T(8,128)(2,1)S(1)}, u32[]{:S(2)}, u32[]{:S(2)}) collective-permute-start(bf16[256,128]{1,0:T(8,128)(2,1)S(1)} %bitcast.10), channel_id=1, source_target_pairs={{0,1},{1,2},{2,3},{3,4},{4,5},{5,6},{6,7},{7,8},{8,9},{9,10},{10,1... | collective-permute-start | bytes 196616 | tf_op jit(solution)/shard_map/ppermute | solution.py:382
  27.1 0.0 copy-done.8
  27.1 0.6 spread.1.matrix_ref
  27.7 0.0 copy-start.3
  27.7 0.0 copy-start.4
  27.7 0.7 collective-permute-done.prev_ref
  28.4 0.0 copy-done.3
  28.4 0.0 copy-done.4
  28.4 2.6 %base.1 = (bf16[6,8,4,16,128]{4,3,2,1,0:T(8,128)(2,1)S(1)}, f32[16,8,128]{2,1,0:T(8,128)S(1)}) custom-call(s32[1,4]{1,0:T(1,128)S(1)} %copy-done.4, bf16[256,128]{1,0:T(8,128)(2,1)S(1)} %bitcast.11, bf16[256,128]{1,0:T(8,128)(2,1)S(1)} %collective-permute-done.prev_ref, bf16[384,1024]{1,0:T(8,128)(2,1)S(1)} %spread.1.matrix_ref, f32[1,128]{1,0:T(1,128)S(1)} %bitcast.14), custom_call_target="tpu_custom_call" | custom-call | bytes 1048576 | tf_op jit(solution)/shard_map/base/pallas_call | solution.py:383
  31.0 19.5 %all_to_all.33.stats_ref = f32[16,8,128]{2,1,0:T(8,128)S(1)} all-to-all(f32[16,8,128]{2,1,0:T(8,128)S(1)} %get-tuple-element.11), channel_id=1, replica_groups=mesh['dp'=32,'tm'=16] {'tm'}, dimensions={0} | all-to-all | bytes 131072 | tf_op jit(solution)/shard_map/all_to_all | solution.py:390
  50.5 0.0 copy-start.9
  50.5 0.0 copy-start.10
  50.5 0.0 copy-done.5
  50.5 0.6 copy-done.9
  51.1 0.0 copy-done.10
  51.2 0.0 copy-start.6
  51.2 0.0 copy-start.7
  51.2 8.3 %conv1.1 = (bf16[4,8,4,16,128]{4,3,2,1,0:T(8,128)(2,1)S(1)}, bf16[2,8,4,16,128]{4,3,2,1,0:T(8,128)(2,1)S(1)}, f32[16,8,128]{2,1,0:T(8,128)S(1)}) custom-call(s32[1,4]{1,0:T(1,128)S(1)} %copy-done.4, bf16[6,8,4,16,128]{4,3,2,1,0:T(8,128)(2,1)S(1)} %get-tuple-element.10.base_ref, f32[16,8,128]{2,1,0:T(8,128)S(1)} %all_to_all.33.stats_ref, ...), custom_call_target="tpu_custom_call" | custom-call | flops 2147483648 | bytes 1048576 | tf_op jit(solution)/shard_map/conv1/pallas_call | solution.py:393
  59.5 2.3 %collective-permute-start.1 = (bf16[2,8,4,16,128]{4,3,2,1,0:T(8,128)(2,1)S(1)}, bf16[2,8,4,16,128]{4,3,2,1,0:T(8,128)(2,1)S(1)}, u32[]{:S(2)}, u32[]{:S(2)}) collective-permute-start(bf16[2,8,4,16,128]{4,3,2,1,0:T(8,128)(2,1)S(1)} %get-tuple-element.13), channel_id=1, source_target_pairs={{0,1},{1,2},{2,3},{3,4},{4,5},{5,6},{6,7},{7,8},{8,9},{9,10},{10,1... | collective-permute-start | bytes 786440 | tf_op jit(solution)/shard_map/ppermute | solution.py:401
  61.7 0.0 copy-start.1
  61.7 11.0 %all_to_all.34.stats_ref = f32[16,8,128]{2,1,0:T(8,128)S(1)} all-to-all(f32[16,8,128]{2,1,0:T(8,128)S(1)} %get-tuple-element.14), channel_id=1, replica_groups=mesh['dp'=32,'tm'=16] {'tm'}, dimensions={0} | all-to-all | bytes 131072 | tf_op jit(solution)/shard_map/all_to_all | solution.py:402
  72.8 0.0 collective-permute-done.1.lead_ref
  72.8 0.0 copy-start.11
  72.8 0.0 copy-start.12
  72.8 0.0 copy-done.6
  72.8 0.0 copy-done.7
  72.8 0.0 copy-done.1
  72.8 0.6 copy-done.11
  73.4 0.0 copy-done.12
  73.4 7.4 %conv2.1 = bf16[256,512]{1,0:T(8,128)(2,1)S(1)} custom-call(s32[1,4]{1,0:T(1,128)S(1)} %copy-done.4, s32[1,32,32]{2,1,0:T(8,128)S(1)} %copy-done.1, bf16[6,8,4,16,128]{4,3,2,1,0:T(8,128)(2,1)S(1)} %get-tuple-element.10.base_ref, bf16[4,8,4,16,128]{4,3,2,1,0:T(8,128)(2,1)S(1)} %get-tuple-element.12.middle_ref, ...), custom_call_target="tpu_custom_call" | custom-call | flops 2147483648 | bytes 1048576 | tf_op jit(solution)/shard_map/conv2/pallas_call | solution.py:403
  80.9 14.9 %all_to_all.35 = bf16[32,8,512]{2,1,0:T(8,128)(2,1)S(1)} all-to-all(bf16[32,8,512]{2,1,0:T(8,128)(2,1)S(1)} %bitcast.12), channel_id=1, replica_groups=mesh['dp'=32,'tm'=16] {'dp'}, dimensions={0} | all-to-all | bytes 524288 | tf_op jit(solution)/shard_map/all_to_all | solution.py:411
  95.8 1.0 place.1
Async XLA Ops:
  0.0 0.7 copy-start
  0.7 0.7 copy-start.2
  1.8 25.3 %copy-start.8 = (bf16[3,3,3,3,128]{4,3,2,1,0:T(4,128)(2,1)S(1)}, bf16[3,3,3,3,128]{4,3,2,1,0:T(4,128)(2,1)}, u32[]{:S(2)}) copy-start(bf16[3,3,3,3,128]{4,3,2,1,0:T(4,128)(2,1)} %weight_ref.3) | copy-start | bytes 62212
  20.9 29.6 %copy-start.5 = (bf16[3,3,3,128,128]{4,3,2,1,0:T(8,128)(2,1)S(1)}, bf16[3,3,3,128,128]{4,3,2,1,0:T(8,128)(2,1)}, u32[]{:S(2)}) copy-start(bf16[3,3,3,128,128]{4,3,2,1,0:T(8,128)(2,1)} %weight_ref.4) | copy-start | bytes 2654212
  20.9 7.4 %collective-permute-start = (bf16[256,128]{1,0:T(8,128)(2,1)S(1)}, bf16[256,128]{1,0:T(8,128)(2,1)S(1)}, u32[]{:S(2)}, u32[]{:S(2)}) collective-permute-start(bf16[256,128]{1,0:T(8,128)(2,1)S(1)} %bitcast.10), channel_id=1, source_target_pairs={{0,1},{1,2},{2,3},{3,4},{4,5},{5,6},{6,7},{7,8},{8,9},{9,10},{10,1... | collective-permute-start | bytes 196616 | tf_op jit(solution)/shard_map/ppermute | solution.py:382
  27.7 0.7 copy-start.3
  27.7 0.7 copy-start.4
  50.5 0.7 copy-start.9
  50.5 0.7 copy-start.10
  51.2 21.6 %copy-start.6 = (bf16[3,3,3,128,128]{4,3,2,1,0:T(8,128)(2,1)S(1)}, bf16[3,3,3,128,128]{4,3,2,1,0:T(8,128)(2,1)}, u32[]{:S(2)}) copy-start(bf16[3,3,3,128,128]{4,3,2,1,0:T(8,128)(2,1)} %weight_ref.5) | copy-start | bytes 2654212
  51.2 21.6 %copy-start.7 = (bf16[3,3,128,128]{3,2,1,0:T(8,128)(2,1)S(1)}, bf16[3,3,128,128]{3,2,1,0:T(8,128)(2,1)}, u32[]{:S(2)}) copy-start(bf16[3,3,128,128]{3,2,1,0:T(8,128)(2,1)} %down_ref.1) | copy-start | bytes 884740
  59.5 13.3 %collective-permute-start.1 = (bf16[2,8,4,16,128]{4,3,2,1,0:T(8,128)(2,1)S(1)}, bf16[2,8,4,16,128]{4,3,2,1,0:T(8,128)(2,1)S(1)}, u32[]{:S(2)}, u32[]{:S(2)}) collective-permute-start(bf16[2,8,4,16,128]{4,3,2,1,0:T(8,128)(2,1)S(1)} %get-tuple-element.13), channel_id=1, source_target_pairs={{0,1},{1,2},{2,3},{3,4},{4,5},{5,6},{6,7},{7,8},{8,9},{9,10},{10,1... | collective-permute-start | bytes 786440 | tf_op jit(solution)/shard_map/ppermute | solution.py:401
  61.7 11.1 %copy-start.1 = (s32[1,32,32]{2,1,0:T(8,128)S(1)}, s32[1,32,32]{2,1,0:T(8,128)}, u32[]{:S(2)}) copy-start(s32[1,32,32]{2,1,0:T(8,128)} %counts_ref.5) | copy-start | bytes 12292
  72.8 0.7 copy-start.11
  72.8 0.7 copy-start.12
where the time goes:
time: 97.3 us; the launch traced here: 96.8 us
  blocking collectives  64.5 us (66%)
  Pallas kernels  20.3 us (21%)
  starting transfers between devices  8.37 us (9%)
  local copies, waits for them, and re-layouts  2.78 us (3%)
    all_to_all x2, blocking collectives, per_device(): lax.all_to_all(packed, 'dp', split_axis=0, concat_axis=0, tiled=True)  34 us
    all_to_all x2, blocking collectives, per_device(): stats = lax.all_to_all(stats, 'tm', split_axis=0, concat_axis=0, tiled=True)  30.5 us
    pallas_call x1, Pallas kernels, per_device(): kernel_call(conv1_kernel, 'conv1', [SMEM] + [VMEM] * 5, [((4, 8, 4, 16, C...  8.28 us
    pallas_call x1, Pallas kernels, per_device(): kernel_call(conv2_kernel, 'conv2', [SMEM] + [VMEM] * 9, [((256, 512), BF1...  7.44 us
    ppermute x1, starting transfers between devices, per_device(): before = lax.ppermute(arrived, 'tm', onward)  6.11 us
    unnamed x26, local copies, waits for them, and re-layouts  2.78 us
    pallas_call x1, Pallas kernels, per_device(): kernel_call(base_kernel, 'base', [SMEM] + [VMEM] * 4, [((6, 8, 4, 16, CH)...  2.63 us
    ppermute x1, starting transfers between devices, per_device(): lead = lax.ppermute(tail, 'tm', onward)  2.26 us
  transfers between devices with their start and end apart: 2, of which 1 were waited for; matrix products, arithmetic and copies ran while one was open for 0% of the time, Pallas kernels for 1%

commit v1 on v0

v1 whole, which is shorter than its diff:
```python
import jax
import jax.numpy as jnp
from jax import lax
from jax.experimental import pallas as pl
from jax.experimental.pallas import tpu as pltpu
from jax.sharding import PartitionSpec as P


F32 = jnp.float32
BF16 = jnp.bfloat16
EPS = 1e-06
NDP = 32
NTM = 16
FT = 4
CLIPS = 4
CH = 128
AREA = 512
FRAME_N = AREA * 4
VMEM_LIMIT = 24 * 1024 * 1024


def iota(shape, dim):
    return lax.broadcasted_iota(jnp.int32, shape, dim)


def onehot(cond):
    return jnp.where(cond, 1.0, 0.0).astype(BF16)


def mm(a, b):
    return jnp.dot(a, b, preferred_element_type=F32)


def pick_lane(values, lane):
    return jnp.sum(jnp.where(iota(values.shape, 1) == lane, values, 0.0), axis=1, keepdims=True)


def pack_kernel(joined_ref, out_ref):
    station = lax.axis_index("dp")
    joined = joined_ref[...]
    table = joined[:, :NDP].astype(F32)
    sub, lane = iota((NDP, NDP), 0), iota((NDP, NDP), 1)
    row = jnp.sum(jnp.where(sub == station, table, 0.0), axis=0, keepdims=True)
    recv = jnp.sum(jnp.where(sub < station, table, 0.0), axis=0, keepdims=True)
    row8 = jnp.broadcast_to(row, (8, NDP))
    start = mm(row8.astype(BF16), onehot(sub < lane))[0:1]
    spread = (iota((256, NDP), 0) // 8 == iota((256, NDP), 1)).astype(F32)
    count_i = jnp.sum(spread * row, axis=1, keepdims=True)
    start_i = jnp.sum(spread * start, axis=1, keepdims=True)
    recv_i = jnp.sum(spread * recv, axis=1, keepdims=True)
    i, m = iota((256, 128), 0), iota((256, 128), 1)
    slot = ((i // 4) % 2).astype(F32)
    valid = slot < count_i
    unit = (m % 32).astype(F32)
    place = onehot((unit == start_i + slot) & (m // 32 == i % 4) & valid)
    src, dst = iota((NDP + 192, 128), 0) - NDP, iota((NDP + 192, 128), 1)
    t = dst % 32
    wanted = 24 * (dst // 32) - 3 + t
    inside = (t < 30) & (dst < 64) & (wanted >= 0) & (wanted < 48)
    rows = [mm(joined, onehot((src == 48 * q + wanted) & inside)).astype(BF16) for q in range(4)]
    packed = mm(place, jnp.concatenate(rows, axis=0))
    packed = jnp.where(m == 64, jnp.where(valid, recv_i + slot, 255.0), packed)
    out_ref[...] = packed.astype(BF16)


def spread_kernel(weight_ref, lengths_ref, *refs):
    vector_refs, (out_ref, vectors_ref, along_ref, taps_ref) = refs[:5], refs[5:]
    along_ref[...] = lengths_ref[...]
    for n, ref in enumerate(vector_refs):
        vectors_ref[n : n + 1, :] = ref[...]
    taps_ref[...] = jnp.zeros_like(taps_ref)
    for a in range(3):
        for b in range(3):
            for c in range(3):
                taps_ref[(a * 3 + b) * 3 + c, 0:3, :] = weight_ref[a, b, c].astype(F32)
    taps = taps_ref[...].reshape(27 * 8, CH).astype(BF16)
    r, j = iota((384, 216), 0), iota((384, 216), 1)
    dyi = (r // 32) % 4
    row_key = jnp.where(dyi < 3, ((2 - r // 128) * 3 + dyi) * 64 + r % 32, -1000)
    tap, color = j // 8, j % 8
    col_key = jnp.where(color < 3, (tap // 3) * 64 + (tap % 3) * 3 + color, -5000)
    diff = row_key - col_key
    for l in range(8):
        out_ref[:, l * CH : (l + 1) * CH] = mm(onehot(diff == 3 * l), taps).astype(BF16)


def clip_ends(lengths_ref):
    ends, total = [], 0
    for c in range(CLIPS):
        total = total + lengths_ref[0, c]
        ends.append(total)
    return ends


def clip_of(ends, frame):
    ident = jnp.int32(0)
    begin = jnp.int32(0)
    for c in range(CLIPS - 1):
        past = frame >= ends[c]
        ident = jnp.where(past, jnp.int32(c + 1), ident)
        begin = jnp.where(past, ends[c], begin)
    return ident, begin


def group_sum(x):
    lane = iota(x.shape, 1)
    x = x + pltpu.roll(x, 127, 1)
    x = x + pltpu.roll(x, 126, 1)
    x = jnp.where(lane % 4 == 0, x, 0.0)
    x = x + pltpu.roll(x, 1, 1)
    return x + pltpu.roll(x, 2, 1)


def shift_k(tile, step):
    moved = pltpu.roll(tile, step % 8, 0)
    return jnp.where(iota(tile.shape, 0) == (0 if step == 1 else 7), 0.0, moved)


class Moments:
    def __init__(self):
        self.pivot = None

    def add(self, rows):
        if self.pivot is None:
            self.pivot = rows[0:1]
            self.first = self.second = jnp.zeros((8, CH), F32)
        off = rows - self.pivot
        square = off * off
        self.first = self.first + fold(off)
        self.second = self.second + fold(square)

    def done(self):
        first = jnp.sum(self.first, axis=0, keepdims=True)
        second = jnp.sum(self.second, axis=0, keepdims=True)
        return first + AREA * self.pivot, second - first * first * (1.0 / AREA)


def fold(rows):
    return tree([rows[n : n + 8] for n in range(0, rows.shape[0], 8)])


def exact_mm(rows, matrix):
    high = rows.astype(BF16).astype(F32)
    middle = (rows - high).astype(BF16).astype(F32)
    low = rows - high - middle
    parts = mm(jnp.concatenate([high, middle, low, low], axis=0).astype(BF16), matrix)
    return parts[0:8] + parts[8:16] + parts[16:24]


def put_stats(pairs, stat_ref):
    sums = jnp.concatenate([p[0] for p in pairs], axis=0)
    devs = jnp.concatenate([p[1] for p in pairs], axis=0)
    off = sums * (1.0 / AREA) - group_sum(sums) * (1.0 / FRAME_N)
    rows = jnp.concatenate([sums, devs + AREA * (off * off)], axis=0)
    narrow = exact_mm(rows, onehot(iota((CH, 128), 0) // 4 == iota((CH, 128), 1) % 32))
    own = jnp.where(iota((8, 128), 0) % FT == iota((8, 128), 1) // 32, narrow, 0.0)
    stats = jnp.concatenate([jnp.sum(own[n : n + 4], axis=0, keepdims=True) for n in (0, 4)], axis=0)
    for j in range(NTM):
        stat_ref[j] = stats


def unpack_rows(arrived):
    wide = arrived.astype(F32)
    pos = wide[:, 64:65].astype(jnp.int32)
    i, m = iota((256, 128), 0), iota((256, 128), 1)
    target = (pos // 8) * 32 + (i % 4) * 8 + pos % 8
    select = jnp.where((m == target) & (pos < 32), 1.0, 0.0)
    rows = mm(select.T.astype(BF16), arrived)
    return jnp.where(iota((128, 128), 1) < 64, rows, 0.0)


def frame_rows(arrived, x_ref, first):
    low = iota((8, 128), 1) < 32
    rows = unpack_rows(arrived)
    for f in range(FT):
        tiles = [rows[f * 32 + q * 8 : f * 32 + q * 8 + 8] for q in range(4)]
        out = []
        for q in range(4):
            above = tiles[q - 1] if q > 0 else shift_k(tiles[3], 1)
            below = tiles[q + 1] if q < 3 else shift_k(tiles[0], -1)
            for h in range(2):
                a, b, c = above, tiles[q], below
                if h:
                    a, b, c = (pltpu.roll(v, 96, 1) for v in (a, b, c))
                a, b, c = (jnp.where(low, v, 0.0) for v in (a, b, c))
                out.append(a + pltpu.roll(b, 32, 1) + pltpu.roll(c, 64, 1))
        x_ref[first + f] = jnp.concatenate(out, axis=0).astype(BF16)


def base_frames(lengths_ref, x_ref, x_first, lhs_ref, matrix_ref, vectors_ref, base_ref, first):
    column = lax.axis_index("tm")
    ends = clip_ends(lengths_ref)
    count = base_ref.shape[0]
    for n in range(count):
        frame = column * FT - 2 + first + n
        unused, begin = clip_of(ends, frame)
        for lag in range(3):
            p = jnp.clip(jnp.maximum(frame - lag, begin) - (column * FT + x_first), 0, x_ref.shape[0] - 1)
            lhs_ref[n * 64 : (n + 1) * 64, lag * 128 : (lag + 1) * 128] = x_ref[p]
    bias = vectors_ref[0:1, :]
    moments = [Moments() for unused in range(count)]
    for pair in range(4):
        both = mm(lhs_ref[...], matrix_ref[:, pair * 256 : (pair + 1) * 256])
        for half in range(2):
            value = (both[:, half * CH : (half + 1) * CH] + bias).astype(BF16)
            for n in range(count):
                part = value[n * 64 : (n + 1) * 64]
                base_ref[n, pair * 2 + half] = part.reshape(4, 16, CH)
                if first + n >= 2:
                    moments[n].add(part.astype(F32))
    return [m.done() for m in moments if m.pivot is not None]


def late_kernel(lengths_ref, own_ref, matrix_ref, vectors_ref, base_ref, x_ref, part_ref, lhs_ref):
    frame_rows(own_ref[...], x_ref, 0)
    pairs = base_frames(lengths_ref, x_ref, 0, lhs_ref, matrix_ref, vectors_ref, base_ref, 4)
    part_ref[...] = jnp.concatenate([p[0] for p in pairs] * 2 + [p[1] for p in pairs] * 2, axis=0)


def early_kernel(
    lengths_ref, prev_ref, own_ref, part_ref, matrix_ref, vectors_ref, base_ref, stat_ref, x_ref, lhs_ref
):
    frame_rows(prev_ref[...], x_ref, 0)
    x_ref[FT:] = own_ref[...]
    pairs = base_frames(lengths_ref, x_ref, -FT, lhs_ref, matrix_ref, vectors_ref, base_ref, 0)
    pairs = pairs + [(part_ref[n : n + 1, :], part_ref[n + 4 : n + 5, :]) for n in range(2)]
    put_stats(pairs, stat_ref)


def clip_scales(stats_ref, lengths_ref, ends, gain, norm_ref):
    sums, devs = stats_ref[:, 0, :], stats_ref[:, 1, :]
    frame = iota((NTM, 128), 0) * FT + iota((NTM, 128), 1) // 32
    inside = [frame < ends[0]] + [(frame >= ends[c - 1]) & (frame < ends[c]) for c in range(1, CLIPS)]
    size = [(lengths_ref[0, c] * FRAME_N).astype(F32) for c in range(CLIPS)]

    def clip_mean(values):
        rows = [
            jnp.sum(jnp.where(inside[c], values[c], 0.0), axis=0, keepdims=True) / size[c] for c in range(CLIPS)
        ]
        rows = jnp.concatenate(rows, axis=0)
        rows = rows + pltpu.roll(rows, 32, 1)
        return rows + pltpu.roll(rows, 64, 1)

    means = clip_mean([sums] * CLIPS)
    offs = [sums * (1.0 / FRAME_N) - means[c : c + 1] for c in range(CLIPS)]
    scales = lax.rsqrt(clip_mean([devs + FRAME_N * (off * off) for off in offs]) + EPS)
    wide = exact_mm(jnp.concatenate([means, scales], axis=0), onehot(iota((128, CH), 0) == iota((128, CH), 1) // 4))
    norm_ref[...] = jnp.where(iota((8, CH), 0) < CLIPS, wide, wide * (0.5 * gain))


def clip_norm(norm_ref, ident):
    return norm_ref[pl.ds(ident, 1), :], norm_ref[pl.ds(ident + CLIPS, 1), :]


def tree(parts):
    while len(parts) > 1:
        parts = [a + b for a, b in zip(parts[0::2], parts[1::2])]
    return parts[0]


def store_padded(places, l, tiles):
    column = []
    for h in range(2):
        own = [tiles[q][h] for q in range(4)]
        column.append([shift_k(own[3], 1)] + own + [shift_k(own[0], -1)])
    flat = [column[h][q] for q in range(6) for h in range(2)]
    padded = jnp.concatenate(flat, axis=0).astype(BF16).reshape(6, 16, CH)
    for act_ref, o in places:
        act_ref[o, l] = padded


def norm_frame(value_of, places, mean, scale, bias):
    zero = jnp.zeros((8, CH), F32)
    for l in range(8):
        v = (value_of(l).astype(F32).reshape(64, CH) - mean) * scale + bias
        v = v + v * jnp.tanh(v)
        tiles = [[v[q * 16 + h * 8 : q * 16 + h * 8 + 8] for h in range(2)] for q in range(4)]
        store_padded(places, l + 1, tiles)
        if l == 0:
            store_padded(places, 9, [[tiles[q][1], zero] for q in range(4)])
        if l == 7:
            store_padded(places, 0, [[zero, tiles[q][0]] for q in range(4)])


class Norm:
    def __init__(self, norm_ref, ends, column, bias):
        self.norm_ref, self.ends, self.column, self.bias = norm_ref, ends, column, 0.5 * bias

    def frame(self, ref, n, o, places):
        ident, unused = clip_of(self.ends, self.column * FT - 2 + o)
        mean, scale = clip_norm(self.norm_ref, ident)
        norm_frame(lambda l: ref[n, l], places, mean, scale, self.bias)

    def loop(self, ref, n, o, count, places):
        def step(i, carry):
            self.frame(ref, n + i, o + i, [(act_ref, first + i) for act_ref, first in places])
            return carry

        lax.fori_loop(0, count, step, 0)


def conv_frames(act_ref, weight_ref, picks):
    taps = [(z, r) for z in range(3) for r in range(3)]

    def rows(first):
        blocks = []
        for pick in picks:
            parts = [
                act_ref[pick[2 - z], first : first + 9 - first // 2, r : r + 4].reshape(-1, CH) for z, r in taps
            ]
            blocks.append(jnp.concatenate(parts, axis=1))
        return jnp.concatenate(blocks, axis=0)

    left, here, right = (jnp.concatenate([weight_ref[z, r, c] for z, r in taps], axis=0) for c in range(3))
    both = mm(rows(0), jnp.concatenate([left, here], axis=1))
    last = mm(rows(2), right)
    totals = []
    for n in range(len(picks)):
        at = n * 576
        totals.append(
            both[at : at + AREA, :CH] + both[at + 64 : at + 576, CH:] + last[n * AREA : (n + 1) * AREA]
        )
    return totals


def frame_picks(ends, column, o, first):
    frame = column * FT - 2 + o
    unused, begin = clip_of(ends, frame)
    return [
        jnp.clip(jnp.maximum(frame - lag, begin) - (column * FT - 2 + first), 0, o - first) for lag in range(3)
    ]


def conv_halves(norm, sources, low_ref, high_ref, weight_ref):
    (a, an), (b, bn), (c, cn) = sources
    norm.loop(a, an, 0, 2, [(low_ref, 0)])
    norm.loop(b, bn, 2, 2, [(low_ref, 2), (high_ref, 0)])
    picks = lambda o, first: frame_picks(norm.ends, norm.column, o, first)
    totals = conv_frames(low_ref, weight_ref, [picks(2, 0), picks(3, 0)])
    norm.frame(c, cn, 4, [(high_ref, 2)])
    norm.frame(c, cn + 1, 5, [(high_ref, 3)])
    yield 0, totals
    yield 2, conv_frames(high_ref, weight_ref, [picks(4, 2), picks(5, 2)])


def conv1_kernel(
    lengths_ref, early_ref, late_ref, stats_ref, vectors_ref, weight_ref,
    middle_ref, tail_ref, stat_ref, low_ref, high_ref, norm_ref,
):
    column = lax.axis_index("tm")
    ends = clip_ends(lengths_ref)
    clip_scales(stats_ref, lengths_ref, ends, vectors_ref[1:2, :], norm_ref)
    norm = Norm(norm_ref, ends, column, vectors_ref[2:3, :])
    pairs = []
    for first, totals in conv_halves(
        norm, [(early_ref, 0), (early_ref, 2), (late_ref, 0)], low_ref, high_ref, weight_ref
    ):
        for f, total in enumerate(totals, first):
            value = total.astype(BF16)
            middle_ref[f] = value.reshape(8, 4, 16, CH)
            if f >= 2:
                tail_ref[f - 2] = value.reshape(8, 4, 16, CH)
            moments = Moments()
            moments.add(value.astype(F32))
            pairs.append(moments.done())
    put_stats(pairs, stat_ref)


def conv2_kernel(
    lengths_ref, counts_ref, early_ref, late_ref, middle_ref, lead_ref, stats_ref, vectors_ref, weight_ref, down_ref,
    out_ref, low_ref, high_ref, norm_ref, resid_ref, later_ref, latent_ref,
):
    column = lax.axis_index("tm")
    station = lax.axis_index("dp")
    ends = clip_ends(lengths_ref)
    clip_scales(stats_ref, lengths_ref, ends, vectors_ref[3:4, :], norm_ref)
    norm = Norm(norm_ref, ends, column, vectors_ref[4:5, :])
    down = down_ref[...].reshape(9 * CH, CH)
    zero = jnp.zeros((8, CH), F32)

    def put(ref, f, l, tiles):
        flat = [tiles[q][h] for q in range(4) for h in range(2)]
        flat = flat + [shift_k(tiles[0][h], -1) for h in range(2)]
        ref[f, l] = jnp.concatenate(flat, axis=0).astype(BF16).reshape(5, 16, CH)

    for first, totals in conv_halves(
        norm, [(lead_ref, 0), (middle_ref, 0), (middle_ref, 2)], low_ref, high_ref, weight_ref
    ):
        half_ref, base_ref = (later_ref, late_ref) if first else (resid_ref, early_ref)
        for f, total in enumerate(totals):
            base = base_ref[f if first else f + 2]
            resid = base.astype(F32).reshape(AREA, CH) + total
            resid = resid.astype(BF16).astype(F32)
            for l in range(8):
                v = resid[l * 64 : (l + 1) * 64]
                tiles = [[v[q * 16 + h * 8 : q * 16 + h * 8 + 8] for h in range(2)] for q in range(4)]
                put(half_ref, f, l, tiles)
                if l == 0:
                    put(half_ref, f, 8, [[tiles[q][1], zero] for q in range(4)])
        taps = []
        for row in range(3):
            for col in range(3):
                parts = [
                    half_ref[f, 2 * j + col, 2 * par + row] for f in range(2) for j in range(4) for par in range(2)
                ]
                taps.append(jnp.concatenate(parts, axis=0))
        latent = mm(jnp.concatenate(taps, axis=1), down)
        for f in range(2):
            for j in range(4):
                for w in range(4):
                    at, to = f * 128 + j * 32 + w * 8, (first + f) * 8
                    latent_ref[w, to : to + 8, j * CH : (j + 1) * CH] = latent[at : at + 8]
    table = counts_ref[0].astype(F32).astype(BF16)
    loader, other = iota((256, NDP), 0) // 8, iota((256, NDP), 1)
    count_i = pick_lane(mm(onehot(loader == other), table), station)
    start_i = pick_lane(mm(onehot(other < loader), table), station)
    i, m = iota((256, 128), 0), iota((256, 128), 1)
    slot = ((i // 4) % 2).astype(F32)
    place = onehot(((m % 32).astype(F32) == start_i + slot) & (m // 32 == i % 4) & (slot < count_i))
    out_ref[...] = mm(place, latent_ref[...].reshape(128, 512).astype(BF16)).astype(BF16)


def return_kernel(counts_ref, back_ref, out_ref):
    station = lax.axis_index("dp")
    table = counts_ref[0].astype(F32)
    sub, lane = iota((NDP, NDP), 0), iota((NDP, NDP), 1)
    row = jnp.sum(jnp.where(sub == station, table, 0.0), axis=0, keepdims=True)
    row8 = jnp.broadcast_to(row, (8, NDP)).astype(BF16)
    encoder, other = iota((NDP, 256), 1) // 8, iota((NDP, 256), 0)
    count_i = mm(row8, onehot(encoder == other))[0:1]
    start_i = mm(row8, onehot(other < encoder))[0:1]
    r, i = iota((128, 256), 0), iota((128, 256), 1)
    slot = ((i // 4) % 2).astype(F32)
    select = onehot(((r % 32).astype(F32) == start_i + slot) & (r // 32 == i % 4) & (slot < count_i))
    units = mm(select, back_ref[...]).astype(BF16)
    for w in range(4):
        out_ref[0, 0, :, w * 512 : (w + 1) * 512] = units[w * 32 : (w + 1) * 32]


VMEM = pl.BlockSpec(memory_space=pltpu.VMEM)
SMEM = pl.BlockSpec(memory_space=pltpu.SMEM)


def kernel_call(body, name, in_specs, outs, scratch=(), flops=0, bytes_accessed=1 << 20, limit=VMEM_LIMIT):
    outs = [jax.ShapeDtypeStruct(shape, dtype) for shape, dtype in outs]
    return pl.pallas_call(
        body,
        name=name,
        in_specs=in_specs,
        out_specs=[VMEM] * len(outs) if len(outs) > 1 else VMEM,
        out_shape=outs if len(outs) > 1 else outs[0],
        scratch_shapes=list(scratch),
        compiler_params=pltpu.CompilerParams(vmem_limit_bytes=limit),
        cost_estimate=pl.CostEstimate(flops=flops, bytes_accessed=bytes_accessed, transcendentals=0),
    )


def per_device(
    pixels,
    counts,
    clip_lengths,
    in_weight,
    in_bias,
    norm1_gain,
    norm1_bias,
    conv1_weight,
    norm2_gain,
    norm2_bias,
    conv2_weight,
    down_weight,
):
    row = lambda v: v.reshape(1, CH)
    joined = jnp.concatenate([counts[0].astype(BF16), pixels[0, 0]], axis=1)
    packed = kernel_call(pack_kernel, "pack", [VMEM], [((256, 128), BF16)])(joined)
    arrived = lax.all_to_all(packed, "dp", split_axis=0, concat_axis=0, tiled=True)
    matrix, vectors, lengths = kernel_call(
        spread_kernel,
        "spread",
        [VMEM] * 7,
        [((384, 8 * CH), BF16), ((8, CH), F32), ((1, CLIPS), jnp.int32)],
        [pltpu.VMEM((27, 8, CH), F32)],
        flops=1 << 28,
    )(in_weight, clip_lengths, row(in_bias), row(norm1_gain), row(norm1_bias), row(norm2_gain), row(norm2_bias))
    onward = [(source, source + 1) for source in range(NTM - 1)]
    before = lax.ppermute(arrived, "tm", onward)
    frames = lambda n: ((n, 8, 4, 16, CH), BF16)
    late, own, part = kernel_call(
        late_kernel,
        "late",
        [SMEM] + [VMEM] * 3,
        [frames(2), ((4, 64, 128), BF16), ((8, CH), F32)],
        [pltpu.VMEM((128, 384), BF16)],
    )(lengths, arrived, matrix, vectors)
    early, stats = kernel_call(
        early_kernel,
        "early",
        [SMEM] + [VMEM] * 5,
        [frames(4), ((NTM, 2, 128), F32)],
        [pltpu.VMEM((8, 64, 128), BF16), pltpu.VMEM((256, 384), BF16)],
    )(lengths, before, own, part, matrix, vectors)
    stats = lax.all_to_all(stats, "tm", split_axis=0, concat_axis=0, tiled=True)
    act = [pltpu.VMEM((4, 10, 6, 16, CH), BF16)] * 2
    norm = pltpu.VMEM((8, CH), F32)
    middle, tail, stats = kernel_call(
        conv1_kernel,
        "conv1",
        [SMEM] + [VMEM] * 5,
        [frames(4), frames(2), ((NTM, 2, 128), F32)],
        act + [norm],
        flops=1 << 31,
    )(lengths, early, late, stats, vectors, conv1_weight)
    lead = lax.ppermute(tail, "tm", onward)
    stats = lax.all_to_all(stats, "tm", split_axis=0, concat_axis=0, tiled=True)
    packed = kernel_call(
        conv2_kernel,
        "conv2",
        [SMEM] + [VMEM] * 9,
        [((256, 512), BF16)],
        act + [norm] + [pltpu.VMEM((2, 9, 5, 16, CH), BF16)] * 2 + [pltpu.VMEM((4, 32, 512), F32)],
        flops=1 << 31,
    )(lengths, counts, early, late, middle, lead, stats, vectors, conv2_weight, down_weight)
    returned = lax.all_to_all(packed, "dp", split_axis=0, concat_axis=0, tiled=True)
    return kernel_call(return_kernel, "place", [VMEM] * 2, [((1, 1, 32, 2048), BF16)])(counts, returned)


def solution(mesh):
    in_specs = (
        P("dp", "tm", None, None),
        P("tm", None, None),
        P("dp", None),
        P(),
        P(),
        P(),
        P(),
        P(),
        P(),
        P(),
        P(),
        P(),
    )
    out_specs = P("dp", "tm", None, None)
    return jax.shard_map(
        per_device, mesh=mesh, in_specs=in_specs, out_specs=out_specs, check_vma=False
    )
```

time: 97.3 us -> 87.6 us (0.900)
  Pallas kernels: 20.3 us -> 15.5 us
  blocking collectives: 64.5 us -> 61.3 us
  local copies, waits for them, and re-layouts: 2.78 us -> 0.71 us
    all_to_all x2, blocking collectives: 30.5 us -> 27.6 us  [per_device(): stats = lax.all_to_all(stats, 'tm', split_axis=0, concat_axis=0, tiled=True)]
    pallas_call x4 -> x5, Pallas kernels: 11.9 us -> 9.17 us  [the longest x1 4.76 us: per_device(): kernel_call(conv1_kernel, 'conv1', [SMEM] + [VMEM] * 5, [frames(4), frame...]
    pallas_call x1, Pallas kernels: 7.44 us -> 5.36 us  [per_device(): kernel_call(conv2_kernel, 'conv2', [SMEM] + [VMEM] * 9, [((256, 512), BF1...]
    unnamed x26 -> x24, local copies, waits for them, and re-layouts: 2.78 us -> 0.71 us
  transfers between devices with their start and end apart: 2 -> 2, of which waited for: 1 -> 0; matrix products, arithmetic and copies ran while one was open for 0% -> 0% of each run, Pallas kernels for 1% -> 2%
where the time goes in v1:
time: 87.6 us; the launch traced here: 86.9 us
  blocking collectives  61.3 us (70%)
  Pallas kernels  15.5 us (18%)
  starting transfers between devices  8.45 us (10%)
    all_to_all x2, blocking collectives, per_device(): lax.all_to_all(packed, 'dp', split_axis=0, concat_axis=0, tiled=True)  33.6 us
    all_to_all x2, blocking collectives, per_device(): stats = lax.all_to_all(stats, 'tm', split_axis=0, concat_axis=0, tiled=True)  27.6 us
    ppermute x1, starting transfers between devices, per_device(): before = lax.ppermute(arrived, 'tm', onward)  5.98 us
    pallas_call x1, Pallas kernels, per_device(): kernel_call(conv2_kernel, 'conv2', [SMEM] + [VMEM] * 9, [((256, 512), BF1...  5.36 us
    pallas_call x1, Pallas kernels, per_device(): kernel_call(conv1_kernel, 'conv1', [SMEM] + [VMEM] * 5, [frames(4), frame...  4.76 us
    ppermute x1, starting transfers between devices, per_device(): lead = lax.ppermute(tail, 'tm', onward)  2.47 us
    pallas_call x1, Pallas kernels, per_device(): kernel_call(early_kernel, 'early', [SMEM] + [VMEM] * 5, [frames(4), ((NTM...  1.99 us
  transfers between devices with their start and end apart: 2, of which 0 were waited for; matrix products, arithmetic and copies ran while one was open for 0% of the time, Pallas kernels for 2%

profile of v1, /device:TPU:1, one launch (start us, length us, event | category | flops | bytes accessed | tf_op | source)
XLA Modules:
  0.0 86.9 jit_solution(2181704344097490158)
XLA Ops:
  0.0 0.0 copy-start.11
  0.0 0.7 convert_bitcast_fusion
  0.7 0.0 copy-done.11
  0.7 0.1 pad_maximum_fusion.joined_ref
  0.8 0.4 pack.1
  1.2 0.0 copy-start.4
  1.2 19.1 %all_to_all.32 = bf16[32,8,128]{2,1,0:T(8,128)(2,1)S(1)} all-to-all(bf16[32,8,128]{2,1,0:T(8,128)(2,1)S(1)} %bitcast.15), channel_id=1, replica_groups=mesh['dp'=32,'tm'=16] {'dp'}, dimensions={0} | all-to-all | bytes 131072 | tf_op jit(solution)/shard_map/all_to_all | solution.py:475
  20.3 6.0 %collective-permute-start = (bf16[256,128]{1,0:T(8,128)(2,1)S(1)}, bf16[256,128]{1,0:T(8,128)(2,1)S(1)}, u32[]{:S(2)}, u32[]{:S(2)}) collective-permute-start(bf16[256,128]{1,0:T(8,128)(2,1)S(1)} %bitcast.13), channel_id=1, source_target_pairs={{0,1},{1,2},{2,3},{3,4},{4,5},{5,6},{6,7},{7,8},{8,9},{9,10},{10,1... | collective-permute-start | bytes 196616 | tf_op jit(solution)/shard_map/ppermute | solution.py:485
  26.3 0.0 copy-start.8
  26.3 0.0 copy-start.9
  26.4 0.0 copy-start.10
  26.4 0.0 copy-start.5
  26.4 0.0 copy-start.6
  26.4 0.0 copy-start.7
  26.4 0.0 copy-done.4
  26.4 0.6 copy-done.8
  27.0 0.0 copy-done.9
  27.0 0.0 copy-done.10
  27.0 0.0 copy-done.5
  27.0 0.0 copy-done.6
  27.0 0.0 copy-done.7
  27.1 0.6 spread.1
  27.7 0.0 copy-start.1
  27.7 1.4 %late.1 = (bf16[2,8,4,16,128]{4,3,2,1,0:T(8,128)(2,1)S(1)}, bf16[4,64,128]{2,1,0:T(8,128)(2,1)S(1)}, f32[8,128]{1,0:T(8,128)S(1)}) custom-call(s32[1,4]{1,0:T(1,128)S(1)} %get-tuple-element.16.lengths_ref, bf16[256,128]{1,0:T(8,128)(2,1)S(1)} %bitcast.14, bf16[384,1024]{1,0:T(8,128)(2,1)S(1)} %get-tuple-element.17.matrix_ref, ...), custom_call_target="tpu_custom_call" | custom-call | bytes 1048576 | tf_op jit(solution)/shard_map/late/pallas_call | solution.py:487
  29.1 0.0 collective-permute-done.prev_ref
  29.1 2.0 %early.1 = (bf16[4,8,4,16,128]{4,3,2,1,0:T(8,128)(2,1)S(1)}, f32[16,2,128]{2,1,0:T(2,128)S(1)}) custom-call(s32[1,4]{1,0:T(1,128)S(1)} %get-tuple-element.16.lengths_ref, bf16[256,128]{1,0:T(8,128)(2,1)S(1)} %collective-permute-done.prev_ref, bf16[4,64,128]{2,1,0:T(8,128)(2,1)S(1)} %get-tuple-element.19.own_ref, f32[8,128]{1,0:T(8,128)S(1)} %get-tuple-element.20.part_ref, ...), custom_call_target="tpu_custom_call" | custom-call | bytes 1048576 | tf_op jit(solution)/shard_map/early/pallas_call | solution.py:494
  31.1 17.5 %all_to_all.33.stats_ref = f32[16,2,128]{2,1,0:T(2,128)S(1)} all-to-all(f32[16,2,128]{2,1,0:T(2,128)S(1)} %get-tuple-element.23), channel_id=1, replica_groups=mesh['dp'=32,'tm'=16] {'tm'}, dimensions={0} | all-to-all | bytes 32768 | tf_op jit(solution)/shard_map/all_to_all | solution.py:501
  48.6 0.0 copy-done.1
  48.6 0.0 copy-start.2
  48.7 0.0 copy-start.3
  48.7 4.8 %conv1.1 = (bf16[4,8,4,16,128]{4,3,2,1,0:T(8,128)(2,1)S(1)}, bf16[2,8,4,16,128]{4,3,2,1,0:T(8,128)(2,1)S(1)}, f32[16,2,128]{2,1,0:T(2,128)S(1)}) custom-call(s32[1,4]{1,0:T(1,128)S(1)} %get-tuple-element.16.lengths_ref, bf16[4,8,4,16,128]{4,3,2,1,0:T(8,128)(2,1)S(1)} %get-tuple-element.21.early_ref, ...), custom_call_target="tpu_custom_call" | custom-call | flops 2147483648 | bytes 1048576 | tf_op jit(solution)/shard_map/conv1/pallas_call | solution.py:504
  53.4 2.5 %collective-permute-start.1 = (bf16[2,8,4,16,128]{4,3,2,1,0:T(8,128)(2,1)S(1)}, bf16[2,8,4,16,128]{4,3,2,1,0:T(8,128)(2,1)S(1)}, u32[]{:S(2)}, u32[]{:S(2)}) collective-permute-start(bf16[2,8,4,16,128]{4,3,2,1,0:T(8,128)(2,1)S(1)} %get-tuple-element.25), channel_id=1, source_target_pairs={{0,1},{1,2},{2,3},{3,4},{4,5},{5,6},{6,7},{7,8},{8,9},{9,10},{10,1... | collective-permute-start | bytes 786440 | tf_op jit(solution)/shard_map/ppermute | solution.py:512
  55.9 0.0 copy-start
  55.9 10.1 %all_to_all.34.stats_ref = f32[16,2,128]{2,1,0:T(2,128)S(1)} all-to-all(f32[16,2,128]{2,1,0:T(2,128)S(1)} %get-tuple-element.26), channel_id=1, replica_groups=mesh['dp'=32,'tm'=16] {'tm'}, dimensions={0} | all-to-all | bytes 32768 | tf_op jit(solution)/shard_map/all_to_all | solution.py:513
  66.0 0.0 collective-permute-done.1.lead_ref
  66.0 0.0 copy-done.2
  66.0 0.0 copy-done.3
  66.0 0.0 copy-done
  66.0 5.4 %conv2.1 = bf16[256,512]{1,0:T(8,128)(2,1)S(1)} custom-call(s32[1,4]{1,0:T(1,128)S(1)} %get-tuple-element.16.lengths_ref, s32[1,32,32]{2,1,0:T(8,128)S(1)} %copy-done, bf16[4,8,4,16,128]{4,3,2,1,0:T(8,128)(2,1)S(1)} %get-tuple-element.21.early_ref, bf16[2,8,4,16,128]{4,3,2,1,0:T(8,128)(2,1)S(1)} %get-tuple-element.22.late_ref, ...), custom_call_target="tpu_custom_call" | custom-call | flops 2147483648 | bytes 1048576 | tf_op jit(solution)/shard_map/conv2/pallas_call | solution.py:514
  71.4 14.5 %all_to_all.35 = bf16[32,8,512]{2,1,0:T(8,128)(2,1)S(1)} all-to-all(bf16[32,8,512]{2,1,0:T(8,128)(2,1)S(1)} %bitcast.16), channel_id=1, replica_groups=mesh['dp'=32,'tm'=16] {'dp'}, dimensions={0} | all-to-all | bytes 524288 | tf_op jit(solution)/shard_map/all_to_all | solution.py:522
  85.9 1.0 %place.1 = bf16[1,1,32,2048]{3,2,1,0:T(8,128)(2,1)} custom-call(s32[1,32,32]{2,1,0:T(8,128)S(1)} %copy-done, bf16[256,512]{1,0:T(8,128)(2,1)S(1)} %bitcast.12), custom_call_target="tpu_custom_call" | custom-call | bytes 1048576 | tf_op jit(solution)/shard_map/place/pallas_call | solution.py:523
Async XLA Ops:
  0.0 0.7 copy-start.11
  1.2 25.2 %copy-start.4 = (bf16[3,3,3,3,128]{4,3,2,1,0:T(4,128)(2,1)S(1)}, bf16[3,3,3,3,128]{4,3,2,1,0:T(4,128)(2,1)}, u32[]{:S(2)}) copy-start(bf16[3,3,3,3,128]{4,3,2,1,0:T(4,128)(2,1)} %weight_ref.3) | copy-start | bytes 62212
  20.3 8.8 %collective-permute-start = (bf16[256,128]{1,0:T(8,128)(2,1)S(1)}, bf16[256,128]{1,0:T(8,128)(2,1)S(1)}, u32[]{:S(2)}, u32[]{:S(2)}) collective-permute-start(bf16[256,128]{1,0:T(8,128)(2,1)S(1)} %bitcast.13), channel_id=1, source_target_pairs={{0,1},{1,2},{2,3},{3,4},{4,5},{5,6},{6,7},{7,8},{8,9},{9,10},{10,1... | collective-permute-start | bytes 196616 | tf_op jit(solution)/shard_map/ppermute | solution.py:485
  26.3 0.7 copy-start.8
  26.3 0.7 copy-start.9
  26.4 0.7 copy-start.10
  26.4 0.7 copy-start.5
  26.4 0.7 copy-start.6
  26.4 0.7 copy-start.7
  27.7 21.0 %copy-start.1 = (bf16[3,3,3,128,128]{4,3,2,1,0:T(8,128)(2,1)S(1)}, bf16[3,3,3,128,128]{4,3,2,1,0:T(8,128)(2,1)}, u32[]{:S(2)}) copy-start(bf16[3,3,3,128,128]{4,3,2,1,0:T(8,128)(2,1)} %weight_ref.4) | copy-start | bytes 2654212
  48.6 17.4 %copy-start.2 = (bf16[3,3,3,128,128]{4,3,2,1,0:T(8,128)(2,1)S(1)}, bf16[3,3,3,128,128]{4,3,2,1,0:T(8,128)(2,1)}, u32[]{:S(2)}) copy-start(bf16[3,3,3,128,128]{4,3,2,1,0:T(8,128)(2,1)} %weight_ref.5) | copy-start | bytes 2654212
  48.7 17.4 %copy-start.3 = (bf16[3,3,128,128]{3,2,1,0:T(8,128)(2,1)S(1)}, bf16[3,3,128,128]{3,2,1,0:T(8,128)(2,1)}, u32[]{:S(2)}) copy-start(bf16[3,3,128,128]{3,2,1,0:T(8,128)(2,1)} %down_ref.1) | copy-start | bytes 884740
  53.4 12.6 %collective-permute-start.1 = (bf16[2,8,4,16,128]{4,3,2,1,0:T(8,128)(2,1)S(1)}, bf16[2,8,4,16,128]{4,3,2,1,0:T(8,128)(2,1)S(1)}, u32[]{:S(2)}, u32[]{:S(2)}) collective-permute-start(bf16[2,8,4,16,128]{4,3,2,1,0:T(8,128)(2,1)S(1)} %get-tuple-element.25), channel_id=1, source_target_pairs={{0,1},{1,2},{2,3},{3,4},{4,5},{5,6},{6,7},{7,8},{8,9},{9,10},{10,1... | collective-permute-start | bytes 786440 | tf_op jit(solution)/shard_map/ppermute | solution.py:512
  55.9 10.1 %copy-start = (s32[1,32,32]{2,1,0:T(8,128)S(1)}, s32[1,32,32]{2,1,0:T(8,128)}, u32[]{:S(2)}) copy-start(s32[1,32,32]{2,1,0:T(8,128)} %counts_ref.3) | copy-start | bytes 12292

commit v2 on v1

--- a/solution.py
+++ b/solution.py
@@ -44,18 +44,18 @@
     recv = jnp.sum(jnp.where(sub < station, table, 0.0), axis=0, keepdims=True)
     row8 = jnp.broadcast_to(row, (8, NDP))
     start = mm(row8.astype(BF16), onehot(sub < lane))[0:1]
-    spread = (iota((256, NDP), 0) // 8 == iota((256, NDP), 1)).astype(F32)
+    spread = (iota((256, NDP), 0) >> 3 == iota((256, NDP), 1)).astype(F32)
     count_i = jnp.sum(spread * row, axis=1, keepdims=True)
     start_i = jnp.sum(spread * start, axis=1, keepdims=True)
     recv_i = jnp.sum(spread * recv, axis=1, keepdims=True)
     i, m = iota((256, 128), 0), iota((256, 128), 1)
-    slot = ((i // 4) % 2).astype(F32)
+    slot = ((i >> 2) & 1).astype(F32)
     valid = slot < count_i
-    unit = (m % 32).astype(F32)
-    place = onehot((unit == start_i + slot) & (m // 32 == i % 4) & valid)
+    unit = (m & 31).astype(F32)
+    place = onehot((unit == start_i + slot) & (m >> 5 == (i & 3)) & valid)
     src, dst = iota((NDP + 192, 128), 0) - NDP, iota((NDP + 192, 128), 1)
-    t = dst % 32
-    wanted = 24 * (dst // 32) - 3 + t
+    t = dst & 31
+    wanted = 24 * (dst >> 5) - 3 + t
     inside = (t < 30) & (dst < 64) & (wanted >= 0) & (wanted < 48)
     rows = [mm(joined, onehot((src == 48 * q + wanted) & inside)).astype(BF16) for q in range(4)]
     packed = mm(place, jnp.concatenate(rows, axis=0))
@@ -74,22 +74,19 @@
             for c in range(3):
                 taps_ref[(a * 3 + b) * 3 + c, 0:3, :] = weight_ref[a, b, c].astype(F32)
     taps = taps_ref[...].reshape(27 * 8, CH).astype(BF16)
-    r, j = iota((384, 216), 0), iota((384, 216), 1)
-    dyi = (r // 32) % 4
-    row_key = jnp.where(dyi < 3, ((2 - r // 128) * 3 + dyi) * 64 + r % 32, -1000)
-    tap, color = j // 8, j % 8
-    col_key = jnp.where(color < 3, (tap // 3) * 64 + (tap % 3) * 3 + color, -5000)
+    r, j = iota((384, 1), 0), iota((1, 216), 1)
+    dyi = (r >> 5) & 3
+    row_key = jnp.where(dyi < 3, ((2 - (r >> 7)) * 3 + dyi) * 64 + (r & 31), -1000)
+    tap, color = j >> 3, j & 7
+    third = (tap * 43) >> 7
+    col_key = jnp.where(color < 3, third * 64 + (tap - 3 * third) * 3 + color, -5000)
     diff = row_key - col_key
     for l in range(8):
         out_ref[:, l * CH : (l + 1) * CH] = mm(onehot(diff == 3 * l), taps).astype(BF16)
 
 
 def clip_ends(lengths_ref):
-    ends, total = [], 0
-    for c in range(CLIPS):
-        total = total + lengths_ref[0, c]
-        ends.append(total)
-    return ends
+    return [jnp.sum(lengths_ref[0:1, 0 : c + 1]) for c in range(CLIPS)]
 
 
 def clip_of(ends, frame):
@@ -106,7 +103,7 @@
     lane = iota(x.shape, 1)
     x = x + pltpu.roll(x, 127, 1)
     x = x + pltpu.roll(x, 126, 1)
-    x = jnp.where(lane % 4 == 0, x, 0.0)
+    x = jnp.where(lane & 3 == 0, x, 0.0)
     x = x + pltpu.roll(x, 1, 1)
     return x + pltpu.roll(x, 2, 1)
 
@@ -152,38 +149,36 @@
     devs = jnp.concatenate([p[1] for p in pairs], axis=0)
     off = sums * (1.0 / AREA) - group_sum(sums) * (1.0 / FRAME_N)
     rows = jnp.concatenate([sums, devs + AREA * (off * off)], axis=0)
-    narrow = exact_mm(rows, onehot(iota((CH, 128), 0) // 4 == iota((CH, 128), 1) % 32))
-    own = jnp.where(iota((8, 128), 0) % FT == iota((8, 128), 1) // 32, narrow, 0.0)
+    narrow = exact_mm(rows, onehot(iota((CH, 128), 0) >> 2 == (iota((CH, 128), 1) & 31)))
+    own = jnp.where(iota((8, 128), 0) & 3 == iota((8, 128), 1) >> 5, narrow, 0.0)
     stats = jnp.concatenate([jnp.sum(own[n : n + 4], axis=0, keepdims=True) for n in (0, 4)], axis=0)
     for j in range(NTM):
         stat_ref[j] = stats
 
 
 def unpack_rows(arrived):
-    wide = arrived.astype(F32)
-    pos = wide[:, 64:65].astype(jnp.int32)
-    i, m = iota((256, 128), 0), iota((256, 128), 1)
-    target = (pos // 8) * 32 + (i % 4) * 8 + pos % 8
-    select = jnp.where((m == target) & (pos < 32), 1.0, 0.0)
-    rows = mm(select.T.astype(BF16), arrived)
-    return jnp.where(iota((128, 128), 1) < 64, rows, 0.0)
+    lane64 = onehot(iota((8, 128), 1) == 64)
+    pos = lax.dot_general(lane64, arrived, (((1,), (1,)), ((), ())), preferred_element_type=F32)[0:1]
+    pos = pos.astype(jnp.int32)
+    q = iota((1, 256), 1) & 3
+    target = jnp.where(pos < 32, (pos >> 3) * 32 + q * 8 + (pos & 7), -1)
+    return mm(onehot(iota((128, 256), 0) == target), arrived)
 
 
 def frame_rows(arrived, x_ref, first):
-    low = iota((8, 128), 1) < 32
     rows = unpack_rows(arrived)
+    lane = iota((8, 128), 1)
     for f in range(FT):
         tiles = [rows[f * 32 + q * 8 : f * 32 + q * 8 + 8] for q in range(4)]
+        above = [shift_k(tiles[3], 1)] + tiles[:3]
+        below = tiles[1:] + [shift_k(tiles[0], -1)]
         out = []
         for q in range(4):
-            above = tiles[q - 1] if q > 0 else shift_k(tiles[3], 1)
-            below = tiles[q + 1] if q < 3 else shift_k(tiles[0], -1)
-            for h in range(2):
-                a, b, c = above, tiles[q], below
-                if h:
-                    a, b, c = (pltpu.roll(v, 96, 1) for v in (a, b, c))
-                a, b, c = (jnp.where(low, v, 0.0) for v in (a, b, c))
-                out.append(a + pltpu.roll(b, 32, 1) + pltpu.roll(c, 64, 1))
+            for a, b, c in ((0, 32, 64), (96, 0, 32)):
+                a, b, c = (
+                    pltpu.roll(v, n, 1) if n else v for v, n in ((above[q], a), (tiles[q], b), (below[q], c))
+                )
+                out.append(jnp.where(lane < 32, a, jnp.where(lane < 64, b, c)))
         x_ref[first + f] = jnp.concatenate(out, axis=0).astype(BF16)
 
 
@@ -229,9 +224,9 @@
 
 def clip_scales(stats_ref, lengths_ref, ends, gain, norm_ref):
     sums, devs = stats_ref[:, 0, :], stats_ref[:, 1, :]
-    frame = iota((NTM, 128), 0) * FT + iota((NTM, 128), 1) // 32
+    frame = iota((NTM, 128), 0) * FT + (iota((NTM, 128), 1) >> 5)
     inside = [frame < ends[0]] + [(frame >= ends[c - 1]) & (frame < ends[c]) for c in range(1, CLIPS)]
-    size = [(lengths_ref[0, c] * FRAME_N).astype(F32) for c in range(CLIPS)]
+    size = [(lengths_ref[0:1, c : c + 1] * FRAME_N).astype(F32) for c in range(CLIPS)]
 
     def clip_mean(values):
         rows = [
@@ -244,7 +239,7 @@
     means = clip_mean([sums] * CLIPS)
     offs = [sums * (1.0 / FRAME_N) - means[c : c + 1] for c in range(CLIPS)]
     scales = lax.rsqrt(clip_mean([devs + FRAME_N * (off * off) for off in offs]) + EPS)
-    wide = exact_mm(jnp.concatenate([means, scales], axis=0), onehot(iota((128, CH), 0) == iota((128, CH), 1) // 4))
+    wide = exact_mm(jnp.concatenate([means, scales], axis=0), onehot(iota((128, CH), 0) == iota((128, CH), 1) >> 2))
     norm_ref[...] = jnp.where(iota((8, CH), 0) < CLIPS, wide, wide * (0.5 * gain))
 
 
@@ -411,12 +406,12 @@
                     at, to = f * 128 + j * 32 + w * 8, (first + f) * 8
                     latent_ref[w, to : to + 8, j * CH : (j + 1) * CH] = latent[at : at + 8]
     table = counts_ref[0].astype(F32).astype(BF16)
-    loader, other = iota((256, NDP), 0) // 8, iota((256, NDP), 1)
+    loader, other = iota((256, NDP), 0) >> 3, iota((256, NDP), 1)
     count_i = pick_lane(mm(onehot(loader == other), table), station)
     start_i = pick_lane(mm(onehot(other < loader), table), station)
     i, m = iota((256, 128), 0), iota((256, 128), 1)
-    slot = ((i // 4) % 2).astype(F32)
-    place = onehot(((m % 32).astype(F32) == start_i + slot) & (m // 32 == i % 4) & (slot < count_i))
+    slot = ((i >> 2) & 1).astype(F32)
+    place = onehot(((m & 31).astype(F32) == start_i + slot) & (m >> 5 == (i & 3)) & (slot < count_i))
     out_ref[...] = mm(place, latent_ref[...].reshape(128, 512).astype(BF16)).astype(BF16)
 
 
@@ -426,19 +421,18 @@
     sub, lane = iota((NDP, NDP), 0), iota((NDP, NDP), 1)
     row = jnp.sum(jnp.where(sub == station, table, 0.0), axis=0, keepdims=True)
     row8 = jnp.broadcast_to(row, (8, NDP)).astype(BF16)
-    encoder, other = iota((NDP, 256), 1) // 8, iota((NDP, 256), 0)
+    encoder, other = iota((NDP, 256), 1) >> 3, iota((NDP, 256), 0)
     count_i = mm(row8, onehot(encoder == other))[0:1]
     start_i = mm(row8, onehot(other < encoder))[0:1]
     r, i = iota((128, 256), 0), iota((128, 256), 1)
-    slot = ((i // 4) % 2).astype(F32)
-    select = onehot(((r % 32).astype(F32) == start_i + slot) & (r // 32 == i % 4) & (slot < count_i))
+    slot = ((i >> 2) & 1).astype(F32)
+    select = onehot(((r & 31).astype(F32) == start_i + slot) & (r >> 5 == (i & 3)) & (slot < count_i))
     units = mm(select, back_ref[...]).astype(BF16)
     for w in range(4):
         out_ref[0, 0, :, w * 512 : (w + 1) * 512] = units[w * 32 : (w + 1) * 32]
 
 
 VMEM = pl.BlockSpec(memory_space=pltpu.VMEM)
-SMEM = pl.BlockSpec(memory_space=pltpu.SMEM)
 
 
 def kernel_call(body, name, in_specs, outs, scratch=(), flops=0, bytes_accessed=1 << 20, limit=VMEM_LIMIT):
@@ -487,14 +481,14 @@
     late, own, part = kernel_call(
         late_kernel,
         "late",
-        [SMEM] + [VMEM] * 3,
+        [VMEM] * 4,
         [frames(2), ((4, 64, 128), BF16), ((8, CH), F32)],
         [pltpu.VMEM((128, 384), BF16)],
     )(lengths, arrived, matrix, vectors)
     early, stats = kernel_call(
         early_kernel,
         "early",
-        [SMEM] + [VMEM] * 5,
+        [VMEM] * 6,
         [frames(4), ((NTM, 2, 128), F32)],
         [pltpu.VMEM((8, 64, 128), BF16), pltpu.VMEM((256, 384), BF16)],
     )(lengths, before, own, part, matrix, vectors)
@@ -504,7 +498,7 @@
     middle, tail, stats = kernel_call(
         conv1_kernel,
         "conv1",
-        [SMEM] + [VMEM] * 5,
+        [VMEM] * 6,
         [frames(4), frames(2), ((NTM, 2, 128), F32)],
         act + [norm],
         flops=1 << 31,
@@ -514,7 +508,7 @@
     packed = kernel_call(
         conv2_kernel,
         "conv2",
-        [SMEM] + [VMEM] * 9,
+        [VMEM] * 10,
         [((256, 512), BF16)],
         act + [norm] + [pltpu.VMEM((2, 9, 5, 16, CH), BF16)] * 2 + [pltpu.VMEM((4, 32, 512), F32)],
         flops=1 << 31,

time: 87.6 us -> 86.1 us (0.983)
  Pallas kernels: 15.5 us -> 13.2 us
    pallas_call x4, Pallas kernels: 13.6 us -> 11.3 us  [the longest x1 4.95 us: per_device(): kernel_call(conv2_kernel, 'conv2', [VMEM] * 10, [((256, 512), BF16)], act...]
where the time goes in v2:
time: 86.1 us; the launch traced here: 85.3 us
  blocking collectives  62 us (72%)
  Pallas kernels  13.2 us (15%)
  starting transfers between devices  8.44 us (10%)
    all_to_all x2, blocking collectives, per_device(): lax.all_to_all(packed, 'dp', split_axis=0, concat_axis=0, tiled=True)  33.6 us
    all_to_all x2, blocking collectives, per_device(): stats = lax.all_to_all(stats, 'tm', split_axis=0, concat_axis=0, tiled=True)  28.4 us
    ppermute x1, starting transfers between devices, per_device(): before = lax.ppermute(arrived, 'tm', onward)  5.98 us
    pallas_call x1, Pallas kernels, per_device(): kernel_call(conv2_kernel, 'conv2', [VMEM] * 10, [((256, 512), BF16)], act...  4.95 us
    pallas_call x1, Pallas kernels, per_device(): kernel_call(conv1_kernel, 'conv1', [VMEM] * 6, [frames(4), frames(2), ((N...  4.35 us
    ppermute x1, starting transfers between devices, per_device(): lead = lax.ppermute(tail, 'tm', onward)  2.46 us
  transfers between devices with their start and end apart: 2, of which 0 were waited for; matrix products, arithmetic and copies ran while one was open for 0% of the time, Pallas kernels for 2%

profile of v2, /device:TPU:1, one launch (start us, length us, event | category | flops | bytes accessed | tf_op | source)
XLA Modules:
  0.0 85.3 jit_solution(13870706695558366774)
XLA Ops:
  0.0 0.0 copy-start.11
  0.0 0.7 convert_bitcast_fusion
  0.7 0.0 copy-done.11
  0.7 0.1 pad_maximum_fusion.joined_ref
  0.8 0.4 pack.1
  1.2 0.0 copy-start.4
  1.2 19.1 %all_to_all.32 = bf16[32,8,128]{2,1,0:T(8,128)(2,1)S(1)} all-to-all(bf16[32,8,128]{2,1,0:T(8,128)(2,1)S(1)} %bitcast.15), channel_id=1, replica_groups=mesh['dp'=32,'tm'=16] {'dp'}, dimensions={0} | all-to-all | bytes 131072 | tf_op jit(solution)/shard_map/all_to_all | solution.py:469
  20.3 6.0 %collective-permute-start = (bf16[256,128]{1,0:T(8,128)(2,1)S(1)}, bf16[256,128]{1,0:T(8,128)(2,1)S(1)}, u32[]{:S(2)}, u32[]{:S(2)}) collective-permute-start(bf16[256,128]{1,0:T(8,128)(2,1)S(1)} %bitcast.13), channel_id=1, source_target_pairs={{0,1},{1,2},{2,3},{3,4},{4,5},{5,6},{6,7},{7,8},{8,9},{9,10},{10,1... | collective-permute-start | bytes 196616 | tf_op jit(solution)/shard_map/ppermute | solution.py:479
  26.3 0.0 copy-start.8
  26.3 0.0 copy-start.9
  26.3 0.0 copy-start.10
  26.4 0.0 copy-start.5
  26.4 0.0 copy-start.6
  26.4 0.0 copy-start.7
  26.4 0.0 copy-done.4
  26.4 0.6 copy-done.8
  27.0 0.0 copy-done.9
  27.0 0.0 copy-done.10
  27.0 0.0 copy-done.5
  27.0 0.0 copy-done.6
  27.0 0.0 copy-done.7
  27.1 0.6 spread.1
  27.7 0.0 copy-start.1
  27.7 0.7 late.1
  28.4 0.0 collective-permute-done.prev_ref
  28.4 1.3 %early.1 = (bf16[4,8,4,16,128]{4,3,2,1,0:T(8,128)(2,1)S(1)}, f32[16,2,128]{2,1,0:T(2,128)S(1)}) custom-call(s32[1,4]{1,0:T(1,128)S(1)} %get-tuple-element.16.lengths_ref, bf16[256,128]{1,0:T(8,128)(2,1)S(1)} %collective-permute-done.prev_ref, bf16[4,64,128]{2,1,0:T(8,128)(2,1)S(1)} %get-tuple-element.19.own_ref, f32[8,128]{1,0:T(8,128)S(1)} %get-tuple-element.20.part_ref, ...), custom_call_target="tpu_custom_call" | custom-call | bytes 1048576 | tf_op jit(solution)/shard_map/early/pallas_call | solution.py:488
  29.7 18.2 %all_to_all.33.stats_ref = f32[16,2,128]{2,1,0:T(2,128)S(1)} all-to-all(f32[16,2,128]{2,1,0:T(2,128)S(1)} %get-tuple-element.23), channel_id=1, replica_groups=mesh['dp'=32,'tm'=16] {'tm'}, dimensions={0} | all-to-all | bytes 32768 | tf_op jit(solution)/shard_map/all_to_all | solution.py:495
  47.9 0.0 copy-done.1
  47.9 0.0 copy-start.2
  47.9 0.0 copy-start.3
  47.9 4.4 %conv1.1 = (bf16[4,8,4,16,128]{4,3,2,1,0:T(8,128)(2,1)S(1)}, bf16[2,8,4,16,128]{4,3,2,1,0:T(8,128)(2,1)S(1)}, f32[16,2,128]{2,1,0:T(2,128)S(1)}) custom-call(s32[1,4]{1,0:T(1,128)S(1)} %get-tuple-element.16.lengths_ref, bf16[4,8,4,16,128]{4,3,2,1,0:T(8,128)(2,1)S(1)} %get-tuple-element.21.early_ref, ...), custom_call_target="tpu_custom_call" | custom-call | flops 2147483648 | bytes 1048576 | tf_op jit(solution)/shard_map/conv1/pallas_call | solution.py:498
  52.3 2.5 %collective-permute-start.1 = (bf16[2,8,4,16,128]{4,3,2,1,0:T(8,128)(2,1)S(1)}, bf16[2,8,4,16,128]{4,3,2,1,0:T(8,128)(2,1)S(1)}, u32[]{:S(2)}, u32[]{:S(2)}) collective-permute-start(bf16[2,8,4,16,128]{4,3,2,1,0:T(8,128)(2,1)S(1)} %get-tuple-element.25), channel_id=1, source_target_pairs={{0,1},{1,2},{2,3},{3,4},{4,5},{5,6},{6,7},{7,8},{8,9},{9,10},{10,1... | collective-permute-start | bytes 786440 | tf_op jit(solution)/shard_map/ppermute | solution.py:506
  54.8 0.0 copy-start
  54.8 10.1 %all_to_all.34.stats_ref = f32[16,2,128]{2,1,0:T(2,128)S(1)} all-to-all(f32[16,2,128]{2,1,0:T(2,128)S(1)} %get-tuple-element.26), channel_id=1, replica_groups=mesh['dp'=32,'tm'=16] {'tm'}, dimensions={0} | all-to-all | bytes 32768 | tf_op jit(solution)/shard_map/all_to_all | solution.py:507
  64.9 0.0 collective-permute-done.1.lead_ref
  64.9 0.0 copy-done.2
  64.9 0.0 copy-done.3
  64.9 0.0 copy-done
  64.9 4.9 %conv2.1 = bf16[256,512]{1,0:T(8,128)(2,1)S(1)} custom-call(s32[1,4]{1,0:T(1,128)S(1)} %get-tuple-element.16.lengths_ref, s32[1,32,32]{2,1,0:T(8,128)S(1)} %copy-done, bf16[4,8,4,16,128]{4,3,2,1,0:T(8,128)(2,1)S(1)} %get-tuple-element.21.early_ref, bf16[2,8,4,16,128]{4,3,2,1,0:T(8,128)(2,1)S(1)} %get-tuple-element.22.late_ref, ...), custom_call_target="tpu_custom_call" | custom-call | flops 2147483648 | bytes 1048576 | tf_op jit(solution)/shard_map/conv2/pallas_call | solution.py:508
  69.9 14.5 %all_to_all.35 = bf16[32,8,512]{2,1,0:T(8,128)(2,1)S(1)} all-to-all(bf16[32,8,512]{2,1,0:T(8,128)(2,1)S(1)} %bitcast.16), channel_id=1, replica_groups=mesh['dp'=32,'tm'=16] {'dp'}, dimensions={0} | all-to-all | bytes 524288 | tf_op jit(solution)/shard_map/all_to_all | solution.py:516
  84.4 1.0 %place.1 = bf16[1,1,32,2048]{3,2,1,0:T(8,128)(2,1)} custom-call(s32[1,32,32]{2,1,0:T(8,128)S(1)} %copy-done, bf16[256,512]{1,0:T(8,128)(2,1)S(1)} %bitcast.12), custom_call_target="tpu_custom_call" | custom-call | bytes 1048576 | tf_op jit(solution)/shard_map/place/pallas_call | solution.py:517
Async XLA Ops:
  0.0 0.7 copy-start.11
  1.2 25.2 %copy-start.4 = (bf16[3,3,3,3,128]{4,3,2,1,0:T(4,128)(2,1)S(1)}, bf16[3,3,3,3,128]{4,3,2,1,0:T(4,128)(2,1)}, u32[]{:S(2)}) copy-start(bf16[3,3,3,3,128]{4,3,2,1,0:T(4,128)(2,1)} %weight_ref.3) | copy-start | bytes 62212
  20.3 8.1 %collective-permute-start = (bf16[256,128]{1,0:T(8,128)(2,1)S(1)}, bf16[256,128]{1,0:T(8,128)(2,1)S(1)}, u32[]{:S(2)}, u32[]{:S(2)}) collective-permute-start(bf16[256,128]{1,0:T(8,128)(2,1)S(1)} %bitcast.13), channel_id=1, source_target_pairs={{0,1},{1,2},{2,3},{3,4},{4,5},{5,6},{6,7},{7,8},{8,9},{9,10},{10,1... | collective-permute-start | bytes 196616 | tf_op jit(solution)/shard_map/ppermute | solution.py:479
  26.3 0.7 copy-start.8
  26.3 0.7 copy-start.9
  26.3 0.7 copy-start.10
  26.4 0.7 copy-start.5
  26.4 0.7 copy-start.6
  26.4 0.7 copy-start.7
  27.7 20.3 %copy-start.1 = (bf16[3,3,3,128,128]{4,3,2,1,0:T(8,128)(2,1)S(1)}, bf16[3,3,3,128,128]{4,3,2,1,0:T(8,128)(2,1)}, u32[]{:S(2)}) copy-start(bf16[3,3,3,128,128]{4,3,2,1,0:T(8,128)(2,1)} %weight_ref.4) | copy-start | bytes 2654212
  47.9 17.0 %copy-start.2 = (bf16[3,3,3,128,128]{4,3,2,1,0:T(8,128)(2,1)S(1)}, bf16[3,3,3,128,128]{4,3,2,1,0:T(8,128)(2,1)}, u32[]{:S(2)}) copy-start(bf16[3,3,3,128,128]{4,3,2,1,0:T(8,128)(2,1)} %weight_ref.5) | copy-start | bytes 2654212
  47.9 17.0 %copy-start.3 = (bf16[3,3,128,128]{3,2,1,0:T(8,128)(2,1)S(1)}, bf16[3,3,128,128]{3,2,1,0:T(8,128)(2,1)}, u32[]{:S(2)}) copy-start(bf16[3,3,128,128]{3,2,1,0:T(8,128)(2,1)} %down_ref.1) | copy-start | bytes 884740
  52.3 12.6 %collective-permute-start.1 = (bf16[2,8,4,16,128]{4,3,2,1,0:T(8,128)(2,1)S(1)}, bf16[2,8,4,16,128]{4,3,2,1,0:T(8,128)(2,1)S(1)}, u32[]{:S(2)}, u32[]{:S(2)}) collective-permute-start(bf16[2,8,4,16,128]{4,3,2,1,0:T(8,128)(2,1)S(1)} %get-tuple-element.25), channel_id=1, source_target_pairs={{0,1},{1,2},{2,3},{3,4},{4,5},{5,6},{6,7},{7,8},{8,9},{9,10},{10,1... | collective-permute-start | bytes 786440 | tf_op jit(solution)/shard_map/ppermute | solution.py:506
  54.8 10.1 %copy-start = (s32[1,32,32]{2,1,0:T(8,128)S(1)}, s32[1,32,32]{2,1,0:T(8,128)}, u32[]{:S(2)}) copy-start(s32[1,32,32]{2,1,0:T(8,128)} %counts_ref.3) | copy-start | bytes 12292

commit v3 on v2

--- a/solution.py
+++ b/solution.py
@@ -44,23 +44,23 @@
     recv = jnp.sum(jnp.where(sub < station, table, 0.0), axis=0, keepdims=True)
     row8 = jnp.broadcast_to(row, (8, NDP))
     start = mm(row8.astype(BF16), onehot(sub < lane))[0:1]
-    spread = (iota((256, NDP), 0) >> 3 == iota((256, NDP), 1)).astype(F32)
+    spread = (iota((128, NDP), 0) >> 2 == iota((128, NDP), 1)).astype(F32)
     count_i = jnp.sum(spread * row, axis=1, keepdims=True)
     start_i = jnp.sum(spread * start, axis=1, keepdims=True)
     recv_i = jnp.sum(spread * recv, axis=1, keepdims=True)
-    i, m = iota((256, 128), 0), iota((256, 128), 1)
-    slot = ((i >> 2) & 1).astype(F32)
-    valid = slot < count_i
-    unit = (m & 31).astype(F32)
-    place = onehot((unit == start_i + slot) & (m >> 5 == (i & 3)) & valid)
+    i, m = iota((128, 64), 0), iota((128, 64), 1)
+    slot = ((i >> 1) & 1).astype(F32)
+    place = onehot(((m & 31).astype(F32) == start_i + slot) & (m >> 5 == (i & 1)) & (slot < count_i))
     src, dst = iota((NDP + 192, 128), 0) - NDP, iota((NDP + 192, 128), 1)
     t = dst & 31
-    wanted = 24 * (dst >> 5) - 3 + t
-    inside = (t < 30) & (dst < 64) & (wanted >= 0) & (wanted < 48)
-    rows = [mm(joined, onehot((src == 48 * q + wanted) & inside)).astype(BF16) for q in range(4)]
+    wanted = 24 * ((dst >> 5) & 1) - 3 + t
+    inside = (t < 30) & (wanted >= 0) & (wanted < 48)
+    wanted = wanted + 48 * (dst >> 6)
+    rows = [mm(joined, onehot((src == 96 * qp + wanted) & inside)).astype(BF16) for qp in range(2)]
     packed = mm(place, jnp.concatenate(rows, axis=0))
-    packed = jnp.where(m == 64, jnp.where(valid, recv_i + slot, 255.0), packed)
-    out_ref[...] = packed.astype(BF16)
+    slot = ((iota((128, 128), 0) >> 1) & 1).astype(F32)
+    packed = jnp.where(iota((128, 128), 1) == 30, jnp.where(slot < count_i, recv_i + slot, 255.0), packed)
+    out_ref[...] = packed.reshape(NDP, 4, 128).astype(BF16)
 
 
 def spread_kernel(weight_ref, lengths_ref, *refs):
@@ -157,26 +157,28 @@
 
 
 def unpack_rows(arrived):
-    lane64 = onehot(iota((8, 128), 1) == 64)
-    pos = lax.dot_general(lane64, arrived, (((1,), (1,)), ((), ())), preferred_element_type=F32)[0:1]
+    lane30 = onehot(iota((8, 128), 1) == 30)
+    pos = lax.dot_general(lane30, arrived, (((1,), (1,)), ((), ())), preferred_element_type=F32)[0:1]
     pos = pos.astype(jnp.int32)
-    q = iota((1, 256), 1) & 3
-    target = jnp.where(pos < 32, (pos >> 3) * 32 + q * 8 + (pos & 7), -1)
-    return mm(onehot(iota((128, 256), 0) == target), arrived)
+    qp = iota((1, 128), 1) & 1
+    target = jnp.where(pos < 32, (pos >> 3) * 16 + qp * 8 + (pos & 7), -1)
+    return mm(onehot(iota((64, 128), 0) == target), arrived)
 
 
 def frame_rows(arrived, x_ref, first):
-    rows = unpack_rows(arrived)
+    rows = unpack_rows(arrived.reshape(128, 128))
     lane = iota((8, 128), 1)
+    move = lambda tile, n: pltpu.roll(tile, n % 128, 1) if n % 128 else tile
     for f in range(FT):
-        tiles = [rows[f * 32 + q * 8 : f * 32 + q * 8 + 8] for q in range(4)]
-        above = [shift_k(tiles[3], 1)] + tiles[:3]
-        below = tiles[1:] + [shift_k(tiles[0], -1)]
+        tiles = [(rows[f * 16 + (q >> 1) * 8 :][:8], 64 * (q & 1)) for q in range(4)]
+        above = [(shift_k(tiles[3][0], 1), tiles[3][1])] + tiles[:3]
+        below = tiles[1:] + [(shift_k(tiles[0][0], -1), tiles[0][1])]
         out = []
         for q in range(4):
-            for a, b, c in ((0, 32, 64), (96, 0, 32)):
+            for h in range(2):
                 a, b, c = (
-                    pltpu.roll(v, n, 1) if n else v for v, n in ((above[q], a), (tiles[q], b), (below[q], c))
+                    move(tile, to - at - 32 * h)
+                    for (tile, at), to in ((above[q], 0), (tiles[q], 32), (below[q], 64))
                 )
                 out.append(jnp.where(lane < 32, a, jnp.where(lane < 64, b, c)))
         x_ref[first + f] = jnp.concatenate(out, axis=0).astype(BF16)
@@ -206,7 +208,34 @@
     return [m.done() for m in moments if m.pivot is not None]
 
 
-def late_kernel(lengths_ref, own_ref, matrix_ref, vectors_ref, base_ref, x_ref, part_ref, lhs_ref):
+def return_routes(counts_ref, place_ref, select_ref):
+    station = lax.axis_index("dp")
+    table = counts_ref[0].astype(F32)
+    narrow = table.astype(BF16)
+    loader, other = iota((256, NDP), 0) >> 3, iota((256, NDP), 1)
+    count_i = pick_lane(mm(onehot(loader == other), narrow), station)
+    start_i = pick_lane(mm(onehot(other < loader), narrow), station)
+    i, m = iota((256, 128), 0), iota((256, 128), 1)
+    slot = ((i >> 2) & 1).astype(F32)
+    place_ref[...] = onehot(
+        ((m & 31).astype(F32) == start_i + slot) & (m >> 5 == (i & 3)) & (slot < count_i)
+    )
+    row = jnp.sum(jnp.where(iota((NDP, NDP), 0) == station, table, 0.0), axis=0, keepdims=True)
+    row8 = jnp.broadcast_to(row, (8, NDP)).astype(BF16)
+    encoder, other = iota((NDP, 256), 1) >> 3, iota((NDP, 256), 0)
+    count_i = mm(row8, onehot(encoder == other))[0:1]
+    start_i = mm(row8, onehot(other < encoder))[0:1]
+    r, i = iota((128, 256), 0), iota((128, 256), 1)
+    slot = ((i >> 2) & 1).astype(F32)
+    select_ref[...] = onehot(
+        ((r & 31).astype(F32) == start_i + slot) & (r >> 5 == (i & 3)) & (slot < count_i)
+    )
+
+
+def late_kernel(
+    lengths_ref, own_ref, matrix_ref, vectors_ref, counts_ref, base_ref, x_ref, part_ref, place_ref, select_ref, lhs_ref
+):
+    return_routes(counts_ref, place_ref, select_ref)
     frame_rows(own_ref[...], x_ref, 0)
     pairs = base_frames(lengths_ref, x_ref, 0, lhs_ref, matrix_ref, vectors_ref, base_ref, 4)
     part_ref[...] = jnp.concatenate([p[0] for p in pairs] * 2 + [p[1] for p in pairs] * 2, axis=0)
@@ -291,7 +320,7 @@
             self.frame(ref, n + i, o + i, [(act_ref, first + i) for act_ref, first in places])
             return carry
 
-        lax.fori_loop(0, count, step, 0)
+        lax.fori_loop(0, count, step, 0, unroll=True)
 
 
 def conv_frames(act_ref, weight_ref, picks):
@@ -362,11 +391,10 @@
 
 
 def conv2_kernel(
-    lengths_ref, counts_ref, early_ref, late_ref, middle_ref, lead_ref, stats_ref, vectors_ref, weight_ref, down_ref,
+    lengths_ref, place_ref, early_ref, late_ref, middle_ref, lead_ref, stats_ref, vectors_ref, weight_ref, down_ref,
     out_ref, low_ref, high_ref, norm_ref, resid_ref, later_ref, latent_ref,
 ):
     column = lax.axis_index("tm")
-    station = lax.axis_index("dp")
     ends = clip_ends(lengths_ref)
     clip_scales(stats_ref, lengths_ref, ends, vectors_ref[3:4, :], norm_ref)
     norm = Norm(norm_ref, ends, column, vectors_ref[4:5, :])
@@ -392,42 +420,28 @@
                 put(half_ref, f, l, tiles)
                 if l == 0:
                     put(half_ref, f, 8, [[tiles[q][1], zero] for q in range(4)])
-        taps = []
-        for row in range(3):
-            for col in range(3):
-                parts = [
-                    half_ref[f, 2 * j + col, 2 * par + row] for f in range(2) for j in range(4) for par in range(2)
-                ]
-                taps.append(jnp.concatenate(parts, axis=0))
-        latent = mm(jnp.concatenate(taps, axis=1), down)
-        for f in range(2):
-            for j in range(4):
-                for w in range(4):
-                    at, to = f * 128 + j * 32 + w * 8, (first + f) * 8
-                    latent_ref[w, to : to + 8, j * CH : (j + 1) * CH] = latent[at : at + 8]
-    table = counts_ref[0].astype(F32).astype(BF16)
-    loader, other = iota((256, NDP), 0) >> 3, iota((256, NDP), 1)
-    count_i = pick_lane(mm(onehot(loader == other), table), station)
-    start_i = pick_lane(mm(onehot(other < loader), table), station)
-    i, m = iota((256, 128), 0), iota((256, 128), 1)
-    slot = ((i >> 2) & 1).astype(F32)
-    place = onehot(((m & 31).astype(F32) == start_i + slot) & (m >> 5 == (i & 3)) & (slot < count_i))
-    out_ref[...] = mm(place, latent_ref[...].reshape(128, 512).astype(BF16)).astype(BF16)
-
-
-def return_kernel(counts_ref, back_ref, out_ref):
-    station = lax.axis_index("dp")
-    table = counts_ref[0].astype(F32)
-    sub, lane = iota((NDP, NDP), 0), iota((NDP, NDP), 1)
-    row = jnp.sum(jnp.where(sub == station, table, 0.0), axis=0, keepdims=True)
-    row8 = jnp.broadcast_to(row, (8, NDP)).astype(BF16)
-    encoder, other = iota((NDP, 256), 1) >> 3, iota((NDP, 256), 0)
-    count_i = mm(row8, onehot(encoder == other))[0:1]
-    start_i = mm(row8, onehot(other < encoder))[0:1]
-    r, i = iota((128, 256), 0), iota((128, 256), 1)
-    slot = ((i >> 2) & 1).astype(F32)
-    select = onehot(((r & 31).astype(F32) == start_i + slot) & (r >> 5 == (i & 3)) & (slot < count_i))
-    units = mm(select, back_ref[...]).astype(BF16)
+    taps = []
+    for row in range(3):
+        for col in range(3):
+            parts = [
+                half_ref[f, 2 * j + col, 2 * par + row]
+                for half_ref in (resid_ref, later_ref)
+                for f in range(2)
+                for j in range(4)
+                for par in range(2)
+            ]
+            taps.append(jnp.concatenate(parts, axis=0))
+    latent = mm(jnp.concatenate(taps, axis=1), down)
+    for f in range(FT):
+        for j in range(4):
+            for w in range(4):
+                at = f * 128 + j * 32 + w * 8
+                latent_ref[w, f * 8 : f * 8 + 8, j * CH : (j + 1) * CH] = latent[at : at + 8]
+    out_ref[...] = mm(place_ref[...], latent_ref[...].reshape(128, 512).astype(BF16)).astype(BF16)
+
+
+def return_kernel(select_ref, back_ref, out_ref):
+    units = mm(select_ref[...], back_ref[...]).astype(BF16)
     for w in range(4):
         out_ref[0, 0, :, w * 512 : (w + 1) * 512] = units[w * 32 : (w + 1) * 32]
 
@@ -465,7 +479,7 @@
 ):
     row = lambda v: v.reshape(1, CH)
     joined = jnp.concatenate([counts[0].astype(BF16), pixels[0, 0]], axis=1)
-    packed = kernel_call(pack_kernel, "pack", [VMEM], [((256, 128), BF16)])(joined)
+    packed = kernel_call(pack_kernel, "pack", [VMEM], [((NDP, 4, 128), BF16)])(joined)
     arrived = lax.all_to_all(packed, "dp", split_axis=0, concat_axis=0, tiled=True)
     matrix, vectors, lengths = kernel_call(
         spread_kernel,
@@ -478,13 +492,13 @@
     onward = [(source, source + 1) for source in range(NTM - 1)]
     before = lax.ppermute(arrived, "tm", onward)
     frames = lambda n: ((n, 8, 4, 16, CH), BF16)
-    late, own, part = kernel_call(
+    late, own, part, place, select = kernel_call(
         late_kernel,
         "late",
-        [VMEM] * 4,
-        [frames(2), ((4, 64, 128), BF16), ((8, CH), F32)],
+        [VMEM] * 5,
+        [frames(2), ((4, 64, 128), BF16), ((8, CH), F32), ((256, 128), BF16), ((128, 256), BF16)],
         [pltpu.VMEM((128, 384), BF16)],
-    )(lengths, arrived, matrix, vectors)
+    )(lengths, arrived, matrix, vectors, counts)
     early, stats = kernel_call(
         early_kernel,
         "early",
@@ -503,8 +517,8 @@
         act + [norm],
         flops=1 << 31,
     )(lengths, early, late, stats, vectors, conv1_weight)
+    stats = lax.all_to_all(stats, "tm", split_axis=0, concat_axis=0, tiled=True)
     lead = lax.ppermute(tail, "tm", onward)
-    stats = lax.all_to_all(stats, "tm", split_axis=0, concat_axis=0, tiled=True)
     packed = kernel_call(
         conv2_kernel,
         "conv2",
@@ -512,9 +526,9 @@
         [((256, 512), BF16)],
         act + [norm] + [pltpu.VMEM((2, 9, 5, 16, CH), BF16)] * 2 + [pltpu.VMEM((4, 32, 512), F32)],
         flops=1 << 31,
-    )(lengths, counts, early, late, middle, lead, stats, vectors, conv2_weight, down_weight)
+    )(lengths, place, early, late, middle, lead, stats, vectors, conv2_weight, down_weight)
     returned = lax.all_to_all(packed, "dp", split_axis=0, concat_axis=0, tiled=True)
-    return kernel_call(return_kernel, "place", [VMEM] * 2, [((1, 1, 32, 2048), BF16)])(counts, returned)
+    return kernel_call(return_kernel, "place", [VMEM] * 2, [((1, 1, 32, 2048), BF16)])(select, returned)
 
 
 def solution(mesh):

time: 86.1 us -> 85.2 us (0.990)
  no operation moved by 1% of the time
where the time goes in v3:
time: 85.2 us; the launch traced here: 84.7 us
  blocking collectives  61.7 us (72%)
  Pallas kernels  12.8 us (15%)
  starting transfers between devices  8.44 us (10%)
    all_to_all x2, blocking collectives, per_device(): lax.all_to_all(packed, 'dp', split_axis=0, concat_axis=0, tiled=True)  33.8 us
    all_to_all x2, blocking collectives, per_device(): stats = lax.all_to_all(stats, 'tm', split_axis=0, concat_axis=0, tiled=True)  27.9 us
    ppermute x1, starting transfers between devices, per_device(): before = lax.ppermute(arrived, 'tm', onward)  5.98 us
    pallas_call x1, Pallas kernels, per_device(): kernel_call(conv2_kernel, 'conv2', [VMEM] * 10, [((256, 512), BF16)], act...  4.76 us
    pallas_call x1, Pallas kernels, per_device(): kernel_call(conv1_kernel, 'conv1', [VMEM] * 6, [frames(4), frames(2), ((N...  4.22 us
    ppermute x1, starting transfers between devices, per_device(): lead = lax.ppermute(tail, 'tm', onward)  2.46 us
  transfers between devices with their start and end apart: 2, of which 0 were waited for; matrix products, arithmetic and copies ran while one was open for 0% of the time, Pallas kernels for 2%

profile of v3, /device:TPU:1, one launch (start us, length us, event | category | flops | bytes accessed | tf_op | source)
XLA Modules:
  0.0 84.7 jit_solution(17531077735342353981)
XLA Ops:
  0.0 0.0 copy-start.11
  0.0 0.7 convert_bitcast_fusion
  0.7 0.0 copy-done.11
  0.7 0.1 pad_maximum_fusion.joined_ref
  0.8 0.4 pack.1
  1.2 0.0 copy-start.4
  1.2 19.0 %all_to_all.26.own_ref = bf16[32,4,128]{2,1,0:T(4,128)(2,1)S(1)} all-to-all(bf16[32,4,128]{2,1,0:T(4,128)(2,1)S(1)} %pack.1), channel_id=1, replica_groups=mesh['dp'=32,'tm'=16] {'dp'}, dimensions={0} | all-to-all | bytes 65536 | tf_op jit(solution)/shard_map/all_to_all | solution.py:483
  20.2 6.0 %collective-permute-start = (bf16[32,4,128]{2,1,0:T(4,128)(2,1)S(1)}, bf16[32,4,128]{2,1,0:T(4,128)(2,1)S(1)}, u32[]{:S(2)}, u32[]{:S(2)}) collective-permute-start(bf16[32,4,128]{2,1,0:T(4,128)(2,1)S(1)} %all_to_all.26.own_ref), channel_id=1, source_target_pairs={{0,1},{1,2},{2,3},{3,4},{4,5},{5,6},{6,7},{7,8},{8,9},{9,10},{10,1... | collective-permute-start | bytes 98312 | tf_op jit(solution)/shard_map/ppermute | solution.py:493
  26.2 0.0 copy-start.8
  26.2 0.0 copy-start.9
  26.2 0.0 copy-start.10
  26.2 0.0 copy-start.5
  26.2 0.0 copy-start.6
  26.2 0.0 copy-start.7
  26.2 0.0 copy-done.4
  26.3 0.6 copy-done.8
  26.8 0.0 copy-done.9
  26.8 0.0 copy-done.10
  26.9 0.0 copy-done.5
  26.9 0.0 copy-done.6
  26.9 0.0 copy-done.7
  26.9 0.0 copy-start
  26.9 0.6 spread.1
  27.5 0.1 copy-done
  27.6 0.0 copy-start.1
  27.6 0.7 late.1
  28.4 0.0 collective-permute-done.prev_ref
  28.4 1.3 %early.1 = (bf16[4,8,4,16,128]{4,3,2,1,0:T(8,128)(2,1)S(1)}, f32[16,2,128]{2,1,0:T(2,128)S(1)}) custom-call(s32[1,4]{1,0:T(1,128)S(1)} %get-tuple-element.18.lengths_ref, bf16[32,4,128]{2,1,0:T(4,128)(2,1)S(1)} %collective-permute-done.prev_ref, bf16[4,64,128]{2,1,0:T(8,128)(2,1)S(1)} %get-tuple-element.23.own_ref, f32[8,128]{1,0:T(8,128)S(1)} %get-tuple-element.24.part_ref, ...), custom_call_target="tpu_custom_call" | custom-call | bytes 1048576 | tf_op jit(solution)/shard_map/early/pallas_call | solution.py:502
  29.6 17.8 %all_to_all.27.stats_ref = f32[16,2,128]{2,1,0:T(2,128)S(1)} all-to-all(f32[16,2,128]{2,1,0:T(2,128)S(1)} %get-tuple-element.27), channel_id=1, replica_groups=mesh['dp'=32,'tm'=16] {'tm'}, dimensions={0} | all-to-all | bytes 32768 | tf_op jit(solution)/shard_map/all_to_all | solution.py:509
  47.4 0.0 copy-done.1
  47.4 0.0 copy-start.2
  47.4 0.0 copy-start.3
  47.4 4.2 %conv1.1 = (bf16[4,8,4,16,128]{4,3,2,1,0:T(8,128)(2,1)S(1)}, bf16[2,8,4,16,128]{4,3,2,1,0:T(8,128)(2,1)S(1)}, f32[16,2,128]{2,1,0:T(2,128)S(1)}) custom-call(s32[1,4]{1,0:T(1,128)S(1)} %get-tuple-element.18.lengths_ref, bf16[4,8,4,16,128]{4,3,2,1,0:T(8,128)(2,1)S(1)} %get-tuple-element.25.early_ref, ...), custom_call_target="tpu_custom_call" | custom-call | flops 2147483648 | bytes 1048576 | tf_op jit(solution)/shard_map/conv1/pallas_call | solution.py:512
  51.6 2.5 %collective-permute-start.1 = (bf16[2,8,4,16,128]{4,3,2,1,0:T(8,128)(2,1)S(1)}, bf16[2,8,4,16,128]{4,3,2,1,0:T(8,128)(2,1)S(1)}, u32[]{:S(2)}, u32[]{:S(2)}) collective-permute-start(bf16[2,8,4,16,128]{4,3,2,1,0:T(8,128)(2,1)S(1)} %get-tuple-element.29), channel_id=1, source_target_pairs={{0,1},{1,2},{2,3},{3,4},{4,5},{5,6},{6,7},{7,8},{8,9},{9,10},{10,1... | collective-permute-start | bytes 786440 | tf_op jit(solution)/shard_map/ppermute | solution.py:521
  54.1 10.1 %all_to_all.28.stats_ref = f32[16,2,128]{2,1,0:T(2,128)S(1)} all-to-all(f32[16,2,128]{2,1,0:T(2,128)S(1)} %get-tuple-element.30), channel_id=1, replica_groups=mesh['dp'=32,'tm'=16] {'tm'}, dimensions={0} | all-to-all | bytes 32768 | tf_op jit(solution)/shard_map/all_to_all | solution.py:520
  64.2 0.0 collective-permute-done.1.lead_ref
  64.2 0.0 copy-done.2
  64.2 0.0 copy-done.3
  64.3 4.8 %conv2.1 = bf16[256,512]{1,0:T(8,128)(2,1)S(1)} custom-call(s32[1,4]{1,0:T(1,128)S(1)} %get-tuple-element.18.lengths_ref, bf16[256,128]{1,0:T(8,128)(2,1)S(1)} %get-tuple-element.22.place_ref, bf16[4,8,4,16,128]{4,3,2,1,0:T(8,128)(2,1)S(1)} %get-tuple-element.25.early_ref, bf16[2,8,4,16,128]{4,3,2,1,0:T(8,128)(2,1)S(1)} %get-tuple-element.26.late_ref, ...), custom_call_target="tpu_custom_call" | custom-call | flops 2147483648 | bytes 1048576 | tf_op jit(solution)/shard_map/conv2/pallas_call | solution.py:522
  69.0 14.8 %all_to_all.29 = bf16[32,8,512]{2,1,0:T(8,128)(2,1)S(1)} all-to-all(bf16[32,8,512]{2,1,0:T(8,128)(2,1)S(1)} %bitcast.11), channel_id=1, replica_groups=mesh['dp'=32,'tm'=16] {'dp'}, dimensions={0} | all-to-all | bytes 524288 | tf_op jit(solution)/shard_map/all_to_all | solution.py:530
  83.8 0.8 place.1
Async XLA Ops:
  0.0 0.7 copy-start.11
  1.2 25.1 %copy-start.4 = (bf16[3,3,3,3,128]{4,3,2,1,0:T(4,128)(2,1)S(1)}, bf16[3,3,3,3,128]{4,3,2,1,0:T(4,128)(2,1)}, u32[]{:S(2)}) copy-start(bf16[3,3,3,3,128]{4,3,2,1,0:T(4,128)(2,1)} %weight_ref.3) | copy-start | bytes 62212
  20.2 8.2 %collective-permute-start = (bf16[32,4,128]{2,1,0:T(4,128)(2,1)S(1)}, bf16[32,4,128]{2,1,0:T(4,128)(2,1)S(1)}, u32[]{:S(2)}, u32[]{:S(2)}) collective-permute-start(bf16[32,4,128]{2,1,0:T(4,128)(2,1)S(1)} %all_to_all.26.own_ref), channel_id=1, source_target_pairs={{0,1},{1,2},{2,3},{3,4},{4,5},{5,6},{6,7},{7,8},{8,9},{9,10},{10,1... | collective-permute-start | bytes 98312 | tf_op jit(solution)/shard_map/ppermute | solution.py:493
  26.2 0.7 copy-start.8
  26.2 0.7 copy-start.9
  26.2 0.7 copy-start.10
  26.2 0.7 copy-start.5
  26.2 0.7 copy-start.6
  26.2 0.7 copy-start.7
  26.9 0.7 copy-start
  27.6 19.8 %copy-start.1 = (bf16[3,3,3,128,128]{4,3,2,1,0:T(8,128)(2,1)S(1)}, bf16[3,3,3,128,128]{4,3,2,1,0:T(8,128)(2,1)}, u32[]{:S(2)}) copy-start(bf16[3,3,3,128,128]{4,3,2,1,0:T(8,128)(2,1)} %weight_ref.4) | copy-start | bytes 2654212
  47.4 16.8 %copy-start.2 = (bf16[3,3,3,128,128]{4,3,2,1,0:T(8,128)(2,1)S(1)}, bf16[3,3,3,128,128]{4,3,2,1,0:T(8,128)(2,1)}, u32[]{:S(2)}) copy-start(bf16[3,3,3,128,128]{4,3,2,1,0:T(8,128)(2,1)} %weight_ref.5) | copy-start | bytes 2654212
  47.4 16.8 %copy-start.3 = (bf16[3,3,128,128]{3,2,1,0:T(8,128)(2,1)S(1)}, bf16[3,3,128,128]{3,2,1,0:T(8,128)(2,1)}, u32[]{:S(2)}) copy-start(bf16[3,3,128,128]{3,2,1,0:T(8,128)(2,1)} %down_ref.1) | copy-start | bytes 884740
  51.6 12.6 %collective-permute-start.1 = (bf16[2,8,4,16,128]{4,3,2,1,0:T(8,128)(2,1)S(1)}, bf16[2,8,4,16,128]{4,3,2,1,0:T(8,128)(2,1)S(1)}, u32[]{:S(2)}, u32[]{:S(2)}) collective-permute-start(bf16[2,8,4,16,128]{4,3,2,1,0:T(8,128)(2,1)S(1)} %get-tuple-element.29), channel_id=1, source_target_pairs={{0,1},{1,2},{2,3},{3,4},{4,5},{5,6},{6,7},{7,8},{8,9},{9,10},{10,1... | collective-permute-start | bytes 786440 | tf_op jit(solution)/shard_map/ppermute | solution.py:521

commit v4 on v3

--- a/solution.py
+++ b/solution.py
@@ -388,6 +388,10 @@
             moments.add(value.astype(F32))
             pairs.append(moments.done())
     put_stats(pairs, stat_ref)
+
+
+def beside_kernel(place_ref, tail_ref, out_ref):
+    out_ref[...] = place_ref[...]
 
 
 def conv2_kernel(
@@ -518,6 +522,7 @@
         flops=1 << 31,
     )(lengths, early, late, stats, vectors, conv1_weight)
     stats = lax.all_to_all(stats, "tm", split_axis=0, concat_axis=0, tiled=True)
+    place = kernel_call(beside_kernel, "beside", [VMEM] * 2, [((256, 128), BF16)], flops=1 << 36)(place, tail)
     lead = lax.ppermute(tail, "tm", onward)
     packed = kernel_call(
         conv2_kernel,

time: 85.2 us -> 84.4 us (level)
  blocking collectives: 61.7 us -> 51.5 us
  starting transfers between devices: 8.44 us -> 13.2 us
  waiting for transfers between devices: 0.01 us -> 3.84 us
    all_to_all x2 -> x1, blocking collectives: 27.9 us -> 17.8 us  [per_device(): stats = lax.all_to_all(stats, 'tm', split_axis=0, concat_axis=0, tiled=True)]
    all_to_all x0 -> x1, waiting for transfers between devices: none -> 3.83 us  [per_device(): stats = lax.all_to_all(stats, 'tm', split_axis=0, concat_axis=0, tiled=True)]
    all_to_all x0 -> x1, starting transfers between devices: none -> 3.68 us  [per_device(): stats = lax.all_to_all(stats, 'tm', split_axis=0, concat_axis=0, tiled=True)]
    ppermute x1, starting transfers between devices: 2.46 us -> 3.53 us  [per_device(): lead = lax.ppermute(tail, 'tm', onward)]
  transfers between devices with their start and end apart: 2 -> 3, of which waited for: 0 -> 1; matrix products, arithmetic and copies ran while one was open for 0% -> 0% of each run, Pallas kernels for 2% -> 2%
where the time goes in v4:
time: 84.4 us; the launch traced here: 83.7 us
  blocking collectives  51.5 us (61%)
  Pallas kernels  13.4 us (16%)
  starting transfers between devices  13.2 us (16%)
  waiting for transfers between devices  3.84 us (5%)
    all_to_all x2, blocking collectives, per_device(): lax.all_to_all(packed, 'dp', split_axis=0, concat_axis=0, tiled=True)  33.7 us
    all_to_all x1, blocking collectives, per_device(): stats = lax.all_to_all(stats, 'tm', split_axis=0, concat_axis=0, tiled=True)  17.8 us
    ppermute x1, starting transfers between devices, per_device(): before = lax.ppermute(arrived, 'tm', onward)  5.98 us
    pallas_call x1, Pallas kernels, per_device(): kernel_call(conv1_kernel, 'conv1', [VMEM] * 6, [frames(4), frames(2), ((N...  4.84 us
    pallas_call x1, Pallas kernels, per_device(): kernel_call(conv2_kernel, 'conv2', [VMEM] * 10, [((256, 512), BF16)], act...  4.78 us
    all_to_all x1, waiting for transfers between devices, per_device(): stats = lax.all_to_all(stats, 'tm', split_axis=0, concat_axis=0, tiled=True)  3.83 us
    all_to_all x1, starting transfers between devices, per_device(): stats = lax.all_to_all(stats, 'tm', split_axis=0, concat_axis=0, tiled=True)  3.68 us
    ppermute x1, starting transfers between devices, per_device(): lead = lax.ppermute(tail, 'tm', onward)  3.53 us
  transfers between devices with their start and end apart: 3, of which 1 were waited for; matrix products, arithmetic and copies ran while one was open for 0% of the time, Pallas kernels for 2%

profile of v4, /device:TPU:1, one launch (start us, length us, event | category | flops | bytes accessed | tf_op | source)
XLA Modules:
  0.0 83.7 jit_solution(17262889824701869926)
XLA Ops:
  0.0 0.0 copy-start.11
  0.0 0.7 convert_bitcast_fusion
  0.7 0.0 copy-done.11
  0.7 0.1 pad_maximum_fusion.joined_ref
  0.8 0.4 pack.1
  1.2 0.0 copy-start.4
  1.2 19.0 %all_to_all.26.own_ref = bf16[32,4,128]{2,1,0:T(4,128)(2,1)S(1)} all-to-all(bf16[32,4,128]{2,1,0:T(4,128)(2,1)S(1)} %pack.1), channel_id=1, replica_groups=mesh['dp'=32,'tm'=16] {'dp'}, dimensions={0} | all-to-all | bytes 65536 | tf_op jit(solution)/shard_map/all_to_all | solution.py:487
  20.2 6.0 %collective-permute-start = (bf16[32,4,128]{2,1,0:T(4,128)(2,1)S(1)}, bf16[32,4,128]{2,1,0:T(4,128)(2,1)S(1)}, u32[]{:S(2)}, u32[]{:S(2)}) collective-permute-start(bf16[32,4,128]{2,1,0:T(4,128)(2,1)S(1)} %all_to_all.26.own_ref), channel_id=1, source_target_pairs={{0,1},{1,2},{2,3},{3,4},{4,5},{5,6},{6,7},{7,8},{8,9},{9,10},{10,1... | collective-permute-start | bytes 98312 | tf_op jit(solution)/shard_map/ppermute | solution.py:497
  26.2 0.0 copy-start.8
  26.2 0.0 copy-start.9
  26.2 0.0 copy-start.10
  26.2 0.0 copy-start.5
  26.2 0.0 copy-start.6
  26.2 0.0 copy-start.7
  26.2 0.0 copy-done.4
  26.3 0.6 copy-done.8
  26.8 0.0 copy-done.9
  26.8 0.0 copy-done.10
  26.9 0.0 copy-done.5
  26.9 0.0 copy-done.6
  26.9 0.0 copy-done.7
  26.9 0.0 copy-start
  26.9 0.6 spread.1
  27.5 0.1 copy-done
  27.6 0.0 copy-start.1
  27.6 0.7 late.1
  28.4 0.0 collective-permute-done.prev_ref
  28.4 1.3 %early.1 = (bf16[4,8,4,16,128]{4,3,2,1,0:T(8,128)(2,1)S(1)}, f32[16,2,128]{2,1,0:T(2,128)S(1)}) custom-call(s32[1,4]{1,0:T(1,128)S(1)} %get-tuple-element.18.lengths_ref, bf16[32,4,128]{2,1,0:T(4,128)(2,1)S(1)} %collective-permute-done.prev_ref, bf16[4,64,128]{2,1,0:T(8,128)(2,1)S(1)} %get-tuple-element.23.own_ref, f32[8,128]{1,0:T(8,128)S(1)} %get-tuple-element.24.part_ref, ...), custom_call_target="tpu_custom_call" | custom-call | bytes 1048576 | tf_op jit(solution)/shard_map/early/pallas_call | solution.py:506
  29.6 17.8 %all_to_all.27.stats_ref = f32[16,2,128]{2,1,0:T(2,128)S(1)} all-to-all(f32[16,2,128]{2,1,0:T(2,128)S(1)} %get-tuple-element.27), channel_id=1, replica_groups=mesh['dp'=32,'tm'=16] {'tm'}, dimensions={0} | all-to-all | bytes 32768 | tf_op jit(solution)/shard_map/all_to_all | solution.py:513
  47.4 0.0 copy-done.1
  47.4 4.8 %conv1.1 = (bf16[4,8,4,16,128]{4,3,2,1,0:T(8,128)(2,1)S(1)}, bf16[2,8,4,16,128]{4,3,2,1,0:T(8,128)(2,1)S(1)}, f32[16,2,128]{2,1,0:T(2,128)}) custom-call(s32[1,4]{1,0:T(1,128)S(1)} %get-tuple-element.18.lengths_ref, bf16[4,8,4,16,128]{4,3,2,1,0:T(8,128)(2,1)S(1)} %get-tuple-element.25.early_ref, bf16[2,8,4,16,128]{4,3,2,1,0:T(8,128)(2,1)S(1)} %get-tuple-element.26.late_ref, ...), custom_call_target="tpu_custom_call" | custom-call | flops 2147483648 | bytes 1048576 | tf_op jit(solution)/shard_map/conv1/pallas_call | solution.py:516
  52.3 3.7 %all-to-all-start.2 = ((f32[16,2,128]{2,1,0:T(2,128)}), f32[16,2,128]{2,1,0:T(2,128)S(1)}, u32[]{:S(2)}, u32[]{:S(2)}) async-start(f32[16,2,128]{2,1,0:T(2,128)} %get-tuple-element.30), calls=%async_computation.2 | async-start | bytes 32768 | tf_op jit(solution)/shard_map/all_to_all | solution.py:524
  55.9 3.5 %collective-permute-start.1 = (bf16[2,8,4,16,128]{4,3,2,1,0:T(8,128)(2,1)S(1)}, bf16[2,8,4,16,128]{4,3,2,1,0:T(8,128)(2,1)S(1)}, u32[]{:S(2)}, u32[]{:S(2)}) collective-permute-start(bf16[2,8,4,16,128]{4,3,2,1,0:T(8,128)(2,1)S(1)} %get-tuple-element.28.tail_ref), channel_id=1, source_target_pairs={{0,1},{1,2},{2,3},{3,4},{4,5},{5,6},{6,7},{7,8},{8,9},{9,10},{10,1... | collective-permute-start | bytes 786440 | tf_op jit(solution)/shard_map/ppermute | solution.py:526
  59.5 0.0 copy-start.2
  59.5 0.0 copy-start.3
  59.5 3.8 %all-to-all-done.2.stats_ref = f32[16,2,128]{2,1,0:T(2,128)S(1)} async-done(((f32[16,2,128]{2,1,0:T(2,128)}), f32[16,2,128]{2,1,0:T(2,128)S(1)}, u32[]{:S(2)}, u32[]{:S(2)}) %all-to-all-start.2) | async-done | bytes 16416 | tf_op jit(solution)/shard_map/all_to_all | solution.py:524
  63.3 0.0 collective-permute-done.1.lead_ref
  63.4 0.0 copy-done.2
  63.4 0.0 copy-done.3
  63.4 4.8 %conv2.1 = bf16[256,512]{1,0:T(8,128)(2,1)S(1)} custom-call(s32[1,4]{1,0:T(1,128)S(1)} %get-tuple-element.18.lengths_ref, bf16[256,128]{1,0:T(8,128)(2,1)S(1)} %beside.1.place_ref, bf16[4,8,4,16,128]{4,3,2,1,0:T(8,128)(2,1)S(1)} %get-tuple-element.25.early_ref, bf16[2,8,4,16,128]{4,3,2,1,0:T(8,128)(2,1)S(1)} %get-tuple-element.26.late_ref, ...), custom_call_target="tpu_custom_call" | custom-call | flops 2147483648 | bytes 1048576 | tf_op jit(solution)/shard_map/conv2/pallas_call | solution.py:527
  68.1 14.8 %all_to_all.28 = bf16[32,8,512]{2,1,0:T(8,128)(2,1)S(1)} all-to-all(bf16[32,8,512]{2,1,0:T(8,128)(2,1)S(1)} %bitcast.11), channel_id=1, replica_groups=mesh['dp'=32,'tm'=16] {'dp'}, dimensions={0} | all-to-all | bytes 524288 | tf_op jit(solution)/shard_map/all_to_all | solution.py:535
  82.9 0.8 %place.1 = bf16[1,1,32,2048]{3,2,1,0:T(8,128)(2,1)} custom-call(bf16[128,256]{1,0:T(8,128)(2,1)S(1)} %get-tuple-element.21.select_ref, bf16[256,512]{1,0:T(8,128)(2,1)S(1)} %bitcast.10), custom_call_target="tpu_custom_call" | custom-call | bytes 1048576 | tf_op jit(solution)/shard_map/place/pallas_call | solution.py:536
  (1 shorter events, 0.0 us)
Async XLA Ops:
  0.0 0.7 copy-start.11
  1.2 25.1 %copy-start.4 = (bf16[3,3,3,3,128]{4,3,2,1,0:T(4,128)(2,1)S(1)}, bf16[3,3,3,3,128]{4,3,2,1,0:T(4,128)(2,1)}, u32[]{:S(2)}) copy-start(bf16[3,3,3,3,128]{4,3,2,1,0:T(4,128)(2,1)} %weight_ref.3) | copy-start | bytes 62212
  20.2 8.2 %collective-permute-start = (bf16[32,4,128]{2,1,0:T(4,128)(2,1)S(1)}, bf16[32,4,128]{2,1,0:T(4,128)(2,1)S(1)}, u32[]{:S(2)}, u32[]{:S(2)}) collective-permute-start(bf16[32,4,128]{2,1,0:T(4,128)(2,1)S(1)} %all_to_all.26.own_ref), channel_id=1, source_target_pairs={{0,1},{1,2},{2,3},{3,4},{4,5},{5,6},{6,7},{7,8},{8,9},{9,10},{10,1... | collective-permute-start | bytes 98312 | tf_op jit(solution)/shard_map/ppermute | solution.py:497
  26.2 0.7 copy-start.8
  26.2 0.7 copy-start.9
  26.2 0.7 copy-start.10
  26.2 0.7 copy-start.5
  26.2 0.7 copy-start.6
  26.2 0.7 copy-start.7
  26.9 0.7 copy-start
  27.6 19.8 %copy-start.1 = (bf16[3,3,3,128,128]{4,3,2,1,0:T(8,128)(2,1)S(1)}, bf16[3,3,3,128,128]{4,3,2,1,0:T(8,128)(2,1)}, u32[]{:S(2)}) copy-start(bf16[3,3,3,128,128]{4,3,2,1,0:T(8,128)(2,1)} %weight_ref.4) | copy-start | bytes 2654212
  52.3 11.1 %all-to-all-start.2 = ((f32[16,2,128]{2,1,0:T(2,128)}), f32[16,2,128]{2,1,0:T(2,128)S(1)}, u32[]{:S(2)}, u32[]{:S(2)}) async-start(f32[16,2,128]{2,1,0:T(2,128)} %get-tuple-element.30), calls=%async_computation.2 | async-start | bytes 32768 | tf_op jit(solution)/shard_map/all_to_all | solution.py:524
  55.9 7.4 %collective-permute-start.1 = (bf16[2,8,4,16,128]{4,3,2,1,0:T(8,128)(2,1)S(1)}, bf16[2,8,4,16,128]{4,3,2,1,0:T(8,128)(2,1)S(1)}, u32[]{:S(2)}, u32[]{:S(2)}) collective-permute-start(bf16[2,8,4,16,128]{4,3,2,1,0:T(8,128)(2,1)S(1)} %get-tuple-element.28.tail_ref), channel_id=1, source_target_pairs={{0,1},{1,2},{2,3},{3,4},{4,5},{5,6},{6,7},{7,8},{8,9},{9,10},{10,1... | collective-permute-start | bytes 786440 | tf_op jit(solution)/shard_map/ppermute | solution.py:526
  59.5 3.9 %copy-start.2 = (bf16[3,3,3,128,128]{4,3,2,1,0:T(8,128)(2,1)S(1)}, bf16[3,3,3,128,128]{4,3,2,1,0:T(8,128)(2,1)}, u32[]{:S(2)}) copy-start(bf16[3,3,3,128,128]{4,3,2,1,0:T(8,128)(2,1)} %weight_ref.5) | copy-start | bytes 2654212
  59.5 3.9 %copy-start.3 = (bf16[3,3,128,128]{3,2,1,0:T(8,128)(2,1)S(1)}, bf16[3,3,128,128]{3,2,1,0:T(8,128)(2,1)}, u32[]{:S(2)}) copy-start(bf16[3,3,128,128]{3,2,1,0:T(8,128)(2,1)} %down_ref.1) | copy-start | bytes 884740

commit v5 on v4

--- a/solution.py
+++ b/solution.py
@@ -35,10 +35,10 @@
     return jnp.sum(jnp.where(iota(values.shape, 1) == lane, values, 0.0), axis=1, keepdims=True)
 
 
-def pack_kernel(joined_ref, out_ref):
+def pack_kernel(counts_ref, pixels_ref, out_ref):
     station = lax.axis_index("dp")
-    joined = joined_ref[...]
-    table = joined[:, :NDP].astype(F32)
+    table = counts_ref[...].astype(F32)
+    pixels = pixels_ref[0, 0]
     sub, lane = iota((NDP, NDP), 0), iota((NDP, NDP), 1)
     row = jnp.sum(jnp.where(sub == station, table, 0.0), axis=0, keepdims=True)
     recv = jnp.sum(jnp.where(sub < station, table, 0.0), axis=0, keepdims=True)
@@ -51,12 +51,12 @@
     i, m = iota((128, 64), 0), iota((128, 64), 1)
     slot = ((i >> 1) & 1).astype(F32)
     place = onehot(((m & 31).astype(F32) == start_i + slot) & (m >> 5 == (i & 1)) & (slot < count_i))
-    src, dst = iota((NDP + 192, 128), 0) - NDP, iota((NDP + 192, 128), 1)
+    src, dst = iota((192, 128), 0), iota((192, 128), 1)
     t = dst & 31
     wanted = 24 * ((dst >> 5) & 1) - 3 + t
     inside = (t < 30) & (wanted >= 0) & (wanted < 48)
     wanted = wanted + 48 * (dst >> 6)
-    rows = [mm(joined, onehot((src == 96 * qp + wanted) & inside)).astype(BF16) for qp in range(2)]
+    rows = [mm(pixels, onehot((src == 96 * qp + wanted) & inside)).astype(BF16) for qp in range(2)]
     packed = mm(place, jnp.concatenate(rows, axis=0))
     slot = ((iota((128, 128), 0) >> 1) & 1).astype(F32)
     packed = jnp.where(iota((128, 128), 1) == 30, jnp.where(slot < count_i, recv_i + slot, 255.0), packed)
@@ -101,11 +101,9 @@
 
 def group_sum(x):
     lane = iota(x.shape, 1)
-    x = x + pltpu.roll(x, 127, 1)
-    x = x + pltpu.roll(x, 126, 1)
-    x = jnp.where(lane & 3 == 0, x, 0.0)
-    x = x + pltpu.roll(x, 1, 1)
-    return x + pltpu.roll(x, 2, 1)
+    for n in (1, 2):
+        x = x + jnp.where(lane & n == 0, pltpu.roll(x, 128 - n, 1), pltpu.roll(x, n, 1))
+    return x
 
 
 def shift_k(tile, step):
@@ -212,24 +210,18 @@
     station = lax.axis_index("dp")
     table = counts_ref[0].astype(F32)
     narrow = table.astype(BF16)
-    loader, other = iota((256, NDP), 0) >> 3, iota((256, NDP), 1)
+    loader, other = iota((64, NDP), 0) >> 1, iota((64, NDP), 1)
     count_i = pick_lane(mm(onehot(loader == other), narrow), station)
     start_i = pick_lane(mm(onehot(other < loader), narrow), station)
-    i, m = iota((256, 128), 0), iota((256, 128), 1)
-    slot = ((i >> 2) & 1).astype(F32)
-    place_ref[...] = onehot(
-        ((m & 31).astype(F32) == start_i + slot) & (m >> 5 == (i & 3)) & (slot < count_i)
-    )
+    slot = (iota((64, NDP), 0) & 1).astype(F32)
+    place_ref[...] = onehot((other.astype(F32) == start_i + slot) & (slot < count_i))
     row = jnp.sum(jnp.where(iota((NDP, NDP), 0) == station, table, 0.0), axis=0, keepdims=True)
     row8 = jnp.broadcast_to(row, (8, NDP)).astype(BF16)
-    encoder, other = iota((NDP, 256), 1) >> 3, iota((NDP, 256), 0)
+    encoder, other = iota((NDP, 64), 1) >> 1, iota((NDP, 64), 0)
     count_i = mm(row8, onehot(encoder == other))[0:1]
     start_i = mm(row8, onehot(other < encoder))[0:1]
-    r, i = iota((128, 256), 0), iota((128, 256), 1)
-    slot = ((i >> 2) & 1).astype(F32)
-    select_ref[...] = onehot(
-        ((r & 31).astype(F32) == start_i + slot) & (r >> 5 == (i & 3)) & (slot < count_i)
-    )
+    slot = (iota((NDP, 64), 1) & 1).astype(F32)
+    select_ref[...] = onehot((other.astype(F32) == start_i + slot) & (slot < count_i))
 
 
 def late_kernel(
@@ -257,19 +249,19 @@
     inside = [frame < ends[0]] + [(frame >= ends[c - 1]) & (frame < ends[c]) for c in range(1, CLIPS)]
     size = [(lengths_ref[0:1, c : c + 1] * FRAME_N).astype(F32) for c in range(CLIPS)]
 
-    def clip_mean(values):
+    def clip_rows(values):
         rows = [
             jnp.sum(jnp.where(inside[c], values[c], 0.0), axis=0, keepdims=True) / size[c] for c in range(CLIPS)
         ]
-        rows = jnp.concatenate(rows, axis=0)
-        rows = rows + pltpu.roll(rows, 32, 1)
-        return rows + pltpu.roll(rows, 64, 1)
-
-    means = clip_mean([sums] * CLIPS)
+        return jnp.concatenate(rows, axis=0)
+
+    parts = clip_rows([sums] * CLIPS)
+    means = parts + pltpu.roll(parts, 32, 1)
+    means = means + pltpu.roll(means, 64, 1)
     offs = [sums * (1.0 / FRAME_N) - means[c : c + 1] for c in range(CLIPS)]
-    scales = lax.rsqrt(clip_mean([devs + FRAME_N * (off * off) for off in offs]) + EPS)
-    wide = exact_mm(jnp.concatenate([means, scales], axis=0), onehot(iota((128, CH), 0) == iota((128, CH), 1) >> 2))
-    norm_ref[...] = jnp.where(iota((8, CH), 0) < CLIPS, wide, wide * (0.5 * gain))
+    rows = jnp.concatenate([parts, clip_rows([devs + FRAME_N * (off * off) for off in offs])], axis=0)
+    wide = exact_mm(rows, onehot(iota((128, CH), 0) & 31 == iota((128, CH), 1) >> 2))
+    norm_ref[...] = jnp.where(iota((8, CH), 0) < CLIPS, wide, lax.rsqrt(wide + EPS) * (0.5 * gain))
 
 
 def clip_norm(norm_ref, ident):
@@ -441,13 +433,13 @@
             for w in range(4):
                 at = f * 128 + j * 32 + w * 8
                 latent_ref[w, f * 8 : f * 8 + 8, j * CH : (j + 1) * CH] = latent[at : at + 8]
-    out_ref[...] = mm(place_ref[...], latent_ref[...].reshape(128, 512).astype(BF16)).astype(BF16)
+    for w in range(4):
+        rows = mm(place_ref[...], latent_ref[w].astype(BF16))
+        out_ref[:, :, w * 512 : (w + 1) * 512] = rows.reshape(NDP, 2, 512).astype(BF16)
 
 
 def return_kernel(select_ref, back_ref, out_ref):
-    units = mm(select_ref[...], back_ref[...]).astype(BF16)
-    for w in range(4):
-        out_ref[0, 0, :, w * 512 : (w + 1) * 512] = units[w * 32 : (w + 1) * 32]
+    out_ref[0, 0] = mm(select_ref[...], back_ref[...].reshape(2 * NDP, 2048)).astype(BF16)
 
 
 VMEM = pl.BlockSpec(memory_space=pltpu.VMEM)
@@ -482,8 +474,7 @@
     down_weight,
 ):
     row = lambda v: v.reshape(1, CH)
-    joined = jnp.concatenate([counts[0].astype(BF16), pixels[0, 0]], axis=1)
-    packed = kernel_call(pack_kernel, "pack", [VMEM], [((NDP, 4, 128), BF16)])(joined)
+    packed = kernel_call(pack_kernel, "pack", [VMEM] * 2, [((NDP, 4, 128), BF16)])(counts[0].astype(BF16), pixels)
     arrived = lax.all_to_all(packed, "dp", split_axis=0, concat_axis=0, tiled=True)
     matrix, vectors, lengths = kernel_call(
         spread_kernel,
@@ -500,7 +491,7 @@
         late_kernel,
         "late",
         [VMEM] * 5,
-        [frames(2), ((4, 64, 128), BF16), ((8, CH), F32), ((256, 128), BF16), ((128, 256), BF16)],
+        [frames(2), ((4, 64, 128), BF16), ((8, CH), F32), ((64, NDP), BF16), ((NDP, 64), BF16)],
         [pltpu.VMEM((128, 384), BF16)],
     )(lengths, arrived, matrix, vectors, counts)
     early, stats = kernel_call(
@@ -522,13 +513,13 @@
         flops=1 << 31,
     )(lengths, early, late, stats, vectors, conv1_weight)
     stats = lax.all_to_all(stats, "tm", split_axis=0, concat_axis=0, tiled=True)
-    place = kernel_call(beside_kernel, "beside", [VMEM] * 2, [((256, 128), BF16)], flops=1 << 36)(place, tail)
+    place = kernel_call(beside_kernel, "beside", [VMEM] * 2, [((64, NDP), BF16)], flops=1 << 36)(place, tail)
     lead = lax.ppermute(tail, "tm", onward)
     packed = kernel_call(
         conv2_kernel,
         "conv2",
         [VMEM] * 10,
-        [((256, 512), BF16)],
+        [((NDP, 2, 2048), BF16)],
         act + [norm] + [pltpu.VMEM((2, 9, 5, 16, CH), BF16)] * 2 + [pltpu.VMEM((4, 32, 512), F32)],
         flops=1 << 31,
     )(lengths, place, early, late, middle, lead, stats, vectors, conv2_weight, down_weight)

time: 84.4 us -> 83.8 us (level)
  no operation moved by 1% of the time
where the time goes in v5:
time: 83.8 us; the launch traced here: 83.2 us
  blocking collectives  51.5 us (61%)
  starting transfers between devices  13.2 us (16%)
  Pallas kernels  12.9 us (15%)
  waiting for transfers between devices  3.84 us (5%)
    all_to_all x2, blocking collectives, per_device(): lax.all_to_all(packed, 'dp', split_axis=0, concat_axis=0, tiled=True)  33.7 us
    all_to_all x1, blocking collectives, per_device(): stats = lax.all_to_all(stats, 'tm', split_axis=0, concat_axis=0, tiled=True)  17.8 us
    ppermute x1, starting transfers between devices, per_device(): before = lax.ppermute(arrived, 'tm', onward)  5.98 us
    pallas_call x1, Pallas kernels, per_device(): kernel_call(conv2_kernel, 'conv2', [VMEM] * 10, [((NDP, 2, 2048), BF16)],...  4.71 us
    pallas_call x1, Pallas kernels, per_device(): kernel_call(conv1_kernel, 'conv1', [VMEM] * 6, [frames(4), frames(2), ((N...  4.57 us
    all_to_all x1, waiting for transfers between devices, per_device(): stats = lax.all_to_all(stats, 'tm', split_axis=0, concat_axis=0, tiled=True)  3.83 us
    all_to_all x1, starting transfers between devices, per_device(): stats = lax.all_to_all(stats, 'tm', split_axis=0, concat_axis=0, tiled=True)  3.68 us
    ppermute x1, starting transfers between devices, per_device(): lead = lax.ppermute(tail, 'tm', onward)  3.53 us
  transfers between devices with their start and end apart: 3, of which 1 were waited for; matrix products, arithmetic and copies ran while one was open for 0% of the time, Pallas kernels for 2%

profile of v5, /device:TPU:1, one launch (start us, length us, event | category | flops | bytes accessed | tf_op | source)
XLA Modules:
  0.0 83.2 jit_solution(16929226864152705447)
XLA Ops:
  0.0 0.0 copy-start.1
  0.0 0.7 convert_bitcast_fusion.counts_ref
  0.7 0.0 copy-done.1
  0.7 0.3 pack.1
  1.1 0.0 copy-start.5
  1.1 19.0 %all_to_all.20.own_ref = bf16[32,4,128]{2,1,0:T(4,128)(2,1)S(1)} all-to-all(bf16[32,4,128]{2,1,0:T(4,128)(2,1)S(1)} %pack.1), channel_id=1, replica_groups=mesh['dp'=32,'tm'=16] {'dp'}, dimensions={0} | all-to-all | bytes 65536 | tf_op jit(solution)/shard_map/all_to_all | solution.py:478
  20.1 6.0 %collective-permute-start = (bf16[32,4,128]{2,1,0:T(4,128)(2,1)S(1)}, bf16[32,4,128]{2,1,0:T(4,128)(2,1)S(1)}, u32[]{:S(2)}, u32[]{:S(2)}) collective-permute-start(bf16[32,4,128]{2,1,0:T(4,128)(2,1)S(1)} %all_to_all.20.own_ref), channel_id=1, source_target_pairs={{0,1},{1,2},{2,3},{3,4},{4,5},{5,6},{6,7},{7,8},{8,9},{9,10},{10,1... | collective-permute-start | bytes 98312 | tf_op jit(solution)/shard_map/ppermute | solution.py:488
  26.1 0.0 copy-start.9
  26.1 0.0 copy-start.10
  26.1 0.0 copy-start.11
  26.1 0.0 copy-start.6
  26.1 0.0 copy-start.7
  26.2 0.0 copy-start.8
  26.2 0.0 copy-done.5
  26.2 0.6 copy-done.9
  26.7 0.0 copy-done.10
  26.8 0.0 copy-done.11
  26.8 0.0 copy-done.6
  26.8 0.0 copy-done.7
  26.8 0.0 copy-done.8
  26.8 0.0 copy-start
  26.8 0.6 spread.1
  27.4 0.1 copy-done
  27.5 0.0 copy-start.2
  27.5 0.7 late.1
  28.3 0.0 collective-permute-done.prev_ref
  28.3 1.1 %early.1 = (bf16[4,8,4,16,128]{4,3,2,1,0:T(8,128)(2,1)S(1)}, f32[16,2,128]{2,1,0:T(2,128)S(1)}) custom-call(s32[1,4]{1,0:T(1,128)S(1)} %get-tuple-element.18.lengths_ref, bf16[32,4,128]{2,1,0:T(4,128)(2,1)S(1)} %collective-permute-done.prev_ref, bf16[4,64,128]{2,1,0:T(8,128)(2,1)S(1)} %get-tuple-element.23.own_ref, f32[8,128]{1,0:T(8,128)S(1)} %get-tuple-element.24.part_ref, ...), custom_call_target="tpu_custom_call" | custom-call | bytes 1048576 | tf_op jit(solution)/shard_map/early/pallas_call | solution.py:497
  29.4 17.8 %all_to_all.21.stats_ref = f32[16,2,128]{2,1,0:T(2,128)S(1)} all-to-all(f32[16,2,128]{2,1,0:T(2,128)S(1)} %get-tuple-element.27), channel_id=1, replica_groups=mesh['dp'=32,'tm'=16] {'tm'}, dimensions={0} | all-to-all | bytes 32768 | tf_op jit(solution)/shard_map/all_to_all | solution.py:504
  47.2 0.0 copy-done.2
  47.2 4.6 %conv1.1 = (bf16[4,8,4,16,128]{4,3,2,1,0:T(8,128)(2,1)S(1)}, bf16[2,8,4,16,128]{4,3,2,1,0:T(8,128)(2,1)S(1)}, f32[16,2,128]{2,1,0:T(2,128)}) custom-call(s32[1,4]{1,0:T(1,128)S(1)} %get-tuple-element.18.lengths_ref, bf16[4,8,4,16,128]{4,3,2,1,0:T(8,128)(2,1)S(1)} %get-tuple-element.25.early_ref, bf16[2,8,4,16,128]{4,3,2,1,0:T(8,128)(2,1)S(1)} %get-tuple-element.26.late_ref, ...), custom_call_target="tpu_custom_call" | custom-call | flops 2147483648 | bytes 1048576 | tf_op jit(solution)/shard_map/conv1/pallas_call | solution.py:507
  51.8 3.7 %all-to-all-start.2 = ((f32[16,2,128]{2,1,0:T(2,128)}), f32[16,2,128]{2,1,0:T(2,128)S(1)}, u32[]{:S(2)}, u32[]{:S(2)}) async-start(f32[16,2,128]{2,1,0:T(2,128)} %get-tuple-element.30), calls=%async_computation.2 | async-start | bytes 32768 | tf_op jit(solution)/shard_map/all_to_all | solution.py:515
  55.4 3.5 %collective-permute-start.1 = (bf16[2,8,4,16,128]{4,3,2,1,0:T(8,128)(2,1)S(1)}, bf16[2,8,4,16,128]{4,3,2,1,0:T(8,128)(2,1)S(1)}, u32[]{:S(2)}, u32[]{:S(2)}) collective-permute-start(bf16[2,8,4,16,128]{4,3,2,1,0:T(8,128)(2,1)S(1)} %get-tuple-element.28.tail_ref), channel_id=1, source_target_pairs={{0,1},{1,2},{2,3},{3,4},{4,5},{5,6},{6,7},{7,8},{8,9},{9,10},{10,1... | collective-permute-start | bytes 786440 | tf_op jit(solution)/shard_map/ppermute | solution.py:517
  59.0 0.0 copy-start.3
  59.0 0.0 copy-start.4
  59.0 3.8 %all-to-all-done.2.stats_ref = f32[16,2,128]{2,1,0:T(2,128)S(1)} async-done(((f32[16,2,128]{2,1,0:T(2,128)}), f32[16,2,128]{2,1,0:T(2,128)S(1)}, u32[]{:S(2)}, u32[]{:S(2)}) %all-to-all-start.2) | async-done | bytes 16416 | tf_op jit(solution)/shard_map/all_to_all | solution.py:515
  62.9 0.0 collective-permute-done.1.lead_ref
  62.9 0.0 copy-done.3
  62.9 0.0 copy-done.4
  62.9 4.7 %conv2.1 = bf16[32,2,2048]{2,1,0:T(2,128)(2,1)S(1)} custom-call(s32[1,4]{1,0:T(1,128)S(1)} %get-tuple-element.18.lengths_ref, bf16[64,32]{1,0:T(8,128)(2,1)S(1)} %beside.1.place_ref, bf16[4,8,4,16,128]{4,3,2,1,0:T(8,128)(2,1)S(1)} %get-tuple-element.25.early_ref, bf16[2,8,4,16,128]{4,3,2,1,0:T(8,128)(2,1)S(1)} %get-tuple-element.26.late_ref, ...), custom_call_target="tpu_custom_call" | custom-call | flops 2147483648 | bytes 1048576 | tf_op jit(solution)/shard_map/conv2/pallas_call | solution.py:518
  67.6 14.8 %all_to_all.22.back_ref = bf16[32,2,2048]{2,1,0:T(2,128)(2,1)S(1)} all-to-all(bf16[32,2,2048]{2,1,0:T(2,128)(2,1)S(1)} %conv2.1), channel_id=1, replica_groups=mesh['dp'=32,'tm'=16] {'dp'}, dimensions={0} | all-to-all | bytes 524288 | tf_op jit(solution)/shard_map/all_to_all | solution.py:526
  82.3 0.8 %place.1 = bf16[1,1,32,2048]{3,2,1,0:T(8,128)(2,1)} custom-call(bf16[32,64]{1,0:T(8,128)(2,1)S(1)} %get-tuple-element.21.select_ref, bf16[32,2,2048]{2,1,0:T(2,128)(2,1)S(1)} %all_to_all.22.back_ref), custom_call_target="tpu_custom_call" | custom-call | bytes 1048576 | tf_op jit(solution)/shard_map/place/pallas_call | solution.py:527
  (1 shorter events, 0.0 us)
Async XLA Ops:
  0.0 0.7 copy-start.1
  1.1 25.1 %copy-start.5 = (bf16[3,3,3,3,128]{4,3,2,1,0:T(4,128)(2,1)S(1)}, bf16[3,3,3,3,128]{4,3,2,1,0:T(4,128)(2,1)}, u32[]{:S(2)}) copy-start(bf16[3,3,3,3,128]{4,3,2,1,0:T(4,128)(2,1)} %weight_ref.3) | copy-start | bytes 62212
  20.1 8.2 %collective-permute-start = (bf16[32,4,128]{2,1,0:T(4,128)(2,1)S(1)}, bf16[32,4,128]{2,1,0:T(4,128)(2,1)S(1)}, u32[]{:S(2)}, u32[]{:S(2)}) collective-permute-start(bf16[32,4,128]{2,1,0:T(4,128)(2,1)S(1)} %all_to_all.20.own_ref), channel_id=1, source_target_pairs={{0,1},{1,2},{2,3},{3,4},{4,5},{5,6},{6,7},{7,8},{8,9},{9,10},{10,1... | collective-permute-start | bytes 98312 | tf_op jit(solution)/shard_map/ppermute | solution.py:488
  26.1 0.7 copy-start.9
  26.1 0.7 copy-start.10
  26.1 0.7 copy-start.11
  26.1 0.7 copy-start.6
  26.1 0.7 copy-start.7
  26.2 0.7 copy-start.8
  26.8 0.7 copy-start
  27.5 19.6 %copy-start.2 = (bf16[3,3,3,128,128]{4,3,2,1,0:T(8,128)(2,1)S(1)}, bf16[3,3,3,128,128]{4,3,2,1,0:T(8,128)(2,1)}, u32[]{:S(2)}) copy-start(bf16[3,3,3,128,128]{4,3,2,1,0:T(8,128)(2,1)} %weight_ref.4) | copy-start | bytes 2654212
  51.8 11.1 %all-to-all-start.2 = ((f32[16,2,128]{2,1,0:T(2,128)}), f32[16,2,128]{2,1,0:T(2,128)S(1)}, u32[]{:S(2)}, u32[]{:S(2)}) async-start(f32[16,2,128]{2,1,0:T(2,128)} %get-tuple-element.30), calls=%async_computation.2 | async-start | bytes 32768 | tf_op jit(solution)/shard_map/all_to_all | solution.py:515
  55.4 7.4 %collective-permute-start.1 = (bf16[2,8,4,16,128]{4,3,2,1,0:T(8,128)(2,1)S(1)}, bf16[2,8,4,16,128]{4,3,2,1,0:T(8,128)(2,1)S(1)}, u32[]{:S(2)}, u32[]{:S(2)}) collective-permute-start(bf16[2,8,4,16,128]{4,3,2,1,0:T(8,128)(2,1)S(1)} %get-tuple-element.28.tail_ref), channel_id=1, source_target_pairs={{0,1},{1,2},{2,3},{3,4},{4,5},{5,6},{6,7},{7,8},{8,9},{9,10},{10,1... | collective-permute-start | bytes 786440 | tf_op jit(solution)/shard_map/ppermute | solution.py:517
  59.0 3.9 %copy-start.3 = (bf16[3,3,3,128,128]{4,3,2,1,0:T(8,128)(2,1)S(1)}, bf16[3,3,3,128,128]{4,3,2,1,0:T(8,128)(2,1)}, u32[]{:S(2)}) copy-start(bf16[3,3,3,128,128]{4,3,2,1,0:T(8,128)(2,1)} %weight_ref.5) | copy-start | bytes 2654212
  59.0 3.9 %copy-start.4 = (bf16[3,3,128,128]{3,2,1,0:T(8,128)(2,1)S(1)}, bf16[3,3,128,128]{3,2,1,0:T(8,128)(2,1)}, u32[]{:S(2)}) copy-start(bf16[3,3,128,128]{3,2,1,0:T(8,128)(2,1)} %down_ref.1) | copy-start | bytes 884740

commit v6 on v5

--- a/solution.py
+++ b/solution.py
@@ -64,8 +64,13 @@
 
 
 def spread_kernel(weight_ref, lengths_ref, *refs):
-    vector_refs, (out_ref, vectors_ref, along_ref, taps_ref) = refs[:5], refs[5:]
+    vector_refs, (out_ref, vectors_ref, along_ref, bounds_ref, taps_ref) = refs[:5], refs[5:]
     along_ref[...] = lengths_ref[...]
+    lengths = [jnp.sum(lengths_ref[0:1, c : c + 1]) for c in range(CLIPS)]
+    for c in range(CLIPS):
+        bounds_ref[c : c + 1, :] = jnp.broadcast_to(sum(lengths[: c + 1]), (1, 128)).astype(F32)
+        size = (lengths[c] * FRAME_N).astype(F32)
+        bounds_ref[c + CLIPS : c + CLIPS + 1, :] = 1.0 / jnp.broadcast_to(size, (1, 128))
     for n, ref in enumerate(vector_refs):
         vectors_ref[n : n + 1, :] = ref[...]
     taps_ref[...] = jnp.zeros_like(taps_ref)
@@ -243,17 +248,17 @@
     put_stats(pairs, stat_ref)
 
 
-def clip_scales(stats_ref, lengths_ref, ends, gain, norm_ref):
+def clip_scales(stats_ref, bounds_ref, gain, norm_ref):
     sums, devs = stats_ref[:, 0, :], stats_ref[:, 1, :]
-    frame = iota((NTM, 128), 0) * FT + (iota((NTM, 128), 1) >> 5)
+    frame = (iota((NTM, 128), 0) * FT + (iota((NTM, 128), 1) >> 5)).astype(F32)
+    ends = [bounds_ref[c : c + 1, :] for c in range(CLIPS)]
     inside = [frame < ends[0]] + [(frame >= ends[c - 1]) & (frame < ends[c]) for c in range(1, CLIPS)]
-    size = [(lengths_ref[0:1, c : c + 1] * FRAME_N).astype(F32) for c in range(CLIPS)]
 
     def clip_rows(values):
         rows = [
-            jnp.sum(jnp.where(inside[c], values[c], 0.0), axis=0, keepdims=True) / size[c] for c in range(CLIPS)
+            jnp.sum(jnp.where(inside[c], values[c], 0.0), axis=0, keepdims=True) for c in range(CLIPS)
         ]
-        return jnp.concatenate(rows, axis=0)
+        return jnp.concatenate(rows, axis=0) * bounds_ref[CLIPS:, :]
 
     parts = clip_rows([sums] * CLIPS)
     means = parts + pltpu.roll(parts, 32, 1)
@@ -360,12 +365,12 @@
 
 
 def conv1_kernel(
-    lengths_ref, early_ref, late_ref, stats_ref, vectors_ref, weight_ref,
+    lengths_ref, early_ref, late_ref, stats_ref, bounds_ref, vectors_ref, weight_ref,
     middle_ref, tail_ref, stat_ref, low_ref, high_ref, norm_ref,
 ):
     column = lax.axis_index("tm")
     ends = clip_ends(lengths_ref)
-    clip_scales(stats_ref, lengths_ref, ends, vectors_ref[1:2, :], norm_ref)
+    clip_scales(stats_ref, bounds_ref, vectors_ref[1:2, :], norm_ref)
     norm = Norm(norm_ref, ends, column, vectors_ref[2:3, :])
     pairs = []
     for first, totals in conv_halves(
@@ -373,9 +378,8 @@
     ):
         for f, total in enumerate(totals, first):
             value = total.astype(BF16)
-            middle_ref[f] = value.reshape(8, 4, 16, CH)
-            if f >= 2:
-                tail_ref[f - 2] = value.reshape(8, 4, 16, CH)
+            half_ref = tail_ref if first else middle_ref
+            half_ref[f & 1] = value.reshape(8, 4, 16, CH)
             moments = Moments()
             moments.add(value.astype(F32))
             pairs.append(moments.done())
@@ -387,12 +391,12 @@
 
 
 def conv2_kernel(
-    lengths_ref, place_ref, early_ref, late_ref, middle_ref, lead_ref, stats_ref, vectors_ref, weight_ref, down_ref,
+    lengths_ref, place_ref, early_ref, late_ref, middle_ref, tail_ref, lead_ref, stats_ref, bounds_ref, vectors_ref, weight_ref, down_ref,
     out_ref, low_ref, high_ref, norm_ref, resid_ref, later_ref, latent_ref,
 ):
     column = lax.axis_index("tm")
     ends = clip_ends(lengths_ref)
-    clip_scales(stats_ref, lengths_ref, ends, vectors_ref[3:4, :], norm_ref)
+    clip_scales(stats_ref, bounds_ref, vectors_ref[3:4, :], norm_ref)
     norm = Norm(norm_ref, ends, column, vectors_ref[4:5, :])
     down = down_ref[...].reshape(9 * CH, CH)
     zero = jnp.zeros((8, CH), F32)
@@ -403,7 +407,7 @@
         ref[f, l] = jnp.concatenate(flat, axis=0).astype(BF16).reshape(5, 16, CH)
 
     for first, totals in conv_halves(
-        norm, [(lead_ref, 0), (middle_ref, 0), (middle_ref, 2)], low_ref, high_ref, weight_ref
+        norm, [(lead_ref, 0), (middle_ref, 0), (tail_ref, 0)], low_ref, high_ref, weight_ref
     ):
         half_ref, base_ref = (later_ref, late_ref) if first else (resid_ref, early_ref)
         for f, total in enumerate(totals):
@@ -476,11 +480,11 @@
     row = lambda v: v.reshape(1, CH)
     packed = kernel_call(pack_kernel, "pack", [VMEM] * 2, [((NDP, 4, 128), BF16)])(counts[0].astype(BF16), pixels)
     arrived = lax.all_to_all(packed, "dp", split_axis=0, concat_axis=0, tiled=True)
-    matrix, vectors, lengths = kernel_call(
+    matrix, vectors, lengths, bounds = kernel_call(
         spread_kernel,
         "spread",
         [VMEM] * 7,
-        [((384, 8 * CH), BF16), ((8, CH), F32), ((1, CLIPS), jnp.int32)],
+        [((384, 8 * CH), BF16), ((8, CH), F32), ((1, CLIPS), jnp.int32), ((8, 128), F32)],
         [pltpu.VMEM((27, 8, CH), F32)],
         flops=1 << 28,
     )(in_weight, clip_lengths, row(in_bias), row(norm1_gain), row(norm1_bias), row(norm2_gain), row(norm2_bias))
@@ -507,22 +511,22 @@
     middle, tail, stats = kernel_call(
         conv1_kernel,
         "conv1",
-        [VMEM] * 6,
-        [frames(4), frames(2), ((NTM, 2, 128), F32)],
+        [VMEM] * 7,
+        [frames(2), frames(2), ((NTM, 2, 128), F32)],
         act + [norm],
         flops=1 << 31,
-    )(lengths, early, late, stats, vectors, conv1_weight)
+    )(lengths, early, late, stats, bounds, vectors, conv1_weight)
     stats = lax.all_to_all(stats, "tm", split_axis=0, concat_axis=0, tiled=True)
     place = kernel_call(beside_kernel, "beside", [VMEM] * 2, [((64, NDP), BF16)], flops=1 << 36)(place, tail)
     lead = lax.ppermute(tail, "tm", onward)
     packed = kernel_call(
         conv2_kernel,
         "conv2",
-        [VMEM] * 10,
+        [VMEM] * 12,
         [((NDP, 2, 2048), BF16)],
         act + [norm] + [pltpu.VMEM((2, 9, 5, 16, CH), BF16)] * 2 + [pltpu.VMEM((4, 32, 512), F32)],
         flops=1 << 31,
-    )(lengths, place, early, late, middle, lead, stats, vectors, conv2_weight, down_weight)
+    )(lengths, place, early, late, middle, tail, lead, stats, bounds, vectors, conv2_weight, down_weight)
     returned = lax.all_to_all(packed, "dp", split_axis=0, concat_axis=0, tiled=True)
     return kernel_call(return_kernel, "place", [VMEM] * 2, [((1, 1, 32, 2048), BF16)])(select, returned)
 

time: 83.8 us -> 83.5 us (level)
  no operation moved by 1% of the time
where the time goes in v6:
time: 83.5 us; the launch traced here: 82.9 us
  blocking collectives  51.5 us (62%)
  starting transfers between devices  13.2 us (16%)
  Pallas kernels  12.7 us (15%)
  waiting for transfers between devices  3.84 us (5%)
    all_to_all x2, blocking collectives, per_device(): lax.all_to_all(packed, 'dp', split_axis=0, concat_axis=0, tiled=True)  33.7 us
    all_to_all x1, blocking collectives, per_device(): stats = lax.all_to_all(stats, 'tm', split_axis=0, concat_axis=0, tiled=True)  17.8 us
    ppermute x1, starting transfers between devices, per_device(): before = lax.ppermute(arrived, 'tm', onward)  5.98 us
    pallas_call x1, Pallas kernels, per_device(): kernel_call(conv2_kernel, 'conv2', [VMEM] * 12, [((NDP, 2, 2048), BF16)],...  4.58 us
    pallas_call x1, Pallas kernels, per_device(): kernel_call(conv1_kernel, 'conv1', [VMEM] * 7, [frames(2), frames(2), ((N...  4.45 us
    all_to_all x1, waiting for transfers between devices, per_device(): stats = lax.all_to_all(stats, 'tm', split_axis=0, concat_axis=0, tiled=True)  3.83 us
    all_to_all x1, starting transfers between devices, per_device(): stats = lax.all_to_all(stats, 'tm', split_axis=0, concat_axis=0, tiled=True)  3.68 us
    ppermute x1, starting transfers between devices, per_device(): lead = lax.ppermute(tail, 'tm', onward)  3.53 us
  transfers between devices with their start and end apart: 3, of which 1 were waited for; matrix products, arithmetic and copies ran while one was open for 0% of the time, Pallas kernels for 2%

profile of v6, /device:TPU:1, one launch (start us, length us, event | category | flops | bytes accessed | tf_op | source)
XLA Modules:
  0.0 82.9 jit_solution(16326924514613559283)
XLA Ops:
  0.0 0.0 copy-start.1
  0.0 0.7 convert_bitcast_fusion.counts_ref
  0.7 0.0 copy-done.1
  0.7 0.3 pack.1
  1.1 0.0 copy-start.5
  1.1 19.0 %all_to_all.20.own_ref = bf16[32,4,128]{2,1,0:T(4,128)(2,1)S(1)} all-to-all(bf16[32,4,128]{2,1,0:T(4,128)(2,1)S(1)} %pack.1), channel_id=1, replica_groups=mesh['dp'=32,'tm'=16] {'dp'}, dimensions={0} | all-to-all | bytes 65536 | tf_op jit(solution)/shard_map/all_to_all | solution.py:482
  20.1 6.0 %collective-permute-start = (bf16[32,4,128]{2,1,0:T(4,128)(2,1)S(1)}, bf16[32,4,128]{2,1,0:T(4,128)(2,1)S(1)}, u32[]{:S(2)}, u32[]{:S(2)}) collective-permute-start(bf16[32,4,128]{2,1,0:T(4,128)(2,1)S(1)} %all_to_all.20.own_ref), channel_id=1, source_target_pairs={{0,1},{1,2},{2,3},{3,4},{4,5},{5,6},{6,7},{7,8},{8,9},{9,10},{10,1... | collective-permute-start | bytes 98312 | tf_op jit(solution)/shard_map/ppermute | solution.py:492
  26.1 0.0 copy-start.9
  26.1 0.0 copy-start.10
  26.1 0.0 copy-start.11
  26.1 0.0 copy-start.6
  26.1 0.0 copy-start.7
  26.2 0.0 copy-start.8
  26.2 0.0 copy-done.5
  26.2 0.6 copy-done.9
  26.7 0.0 copy-done.10
  26.8 0.0 copy-done.11
  26.8 0.0 copy-done.6
  26.8 0.0 copy-done.7
  26.8 0.0 copy-done.8
  26.8 0.0 copy-start
  26.8 0.6 spread.1
  27.4 0.1 copy-done
  27.5 0.0 copy-start.2
  27.5 0.7 late.1
  28.3 0.0 collective-permute-done.prev_ref
  28.3 1.1 %early.1 = (bf16[4,8,4,16,128]{4,3,2,1,0:T(8,128)(2,1)S(1)}, f32[16,2,128]{2,1,0:T(2,128)S(1)}) custom-call(s32[1,4]{1,0:T(1,128)S(1)} %get-tuple-element.19.lengths_ref, bf16[32,4,128]{2,1,0:T(4,128)(2,1)S(1)} %collective-permute-done.prev_ref, bf16[4,64,128]{2,1,0:T(8,128)(2,1)S(1)} %get-tuple-element.24.own_ref, f32[8,128]{1,0:T(8,128)S(1)} %get-tuple-element.25.part_ref, ...), custom_call_target="tpu_custom_call" | custom-call | bytes 1048576 | tf_op jit(solution)/shard_map/early/pallas_call | solution.py:501
  29.4 17.8 %all_to_all.21.stats_ref = f32[16,2,128]{2,1,0:T(2,128)S(1)} all-to-all(f32[16,2,128]{2,1,0:T(2,128)S(1)} %get-tuple-element.28), channel_id=1, replica_groups=mesh['dp'=32,'tm'=16] {'tm'}, dimensions={0} | all-to-all | bytes 32768 | tf_op jit(solution)/shard_map/all_to_all | solution.py:508
  47.2 0.0 copy-done.2
  47.2 4.4 %conv1.1 = (bf16[2,8,4,16,128]{4,3,2,1,0:T(8,128)(2,1)S(1)}, bf16[2,8,4,16,128]{4,3,2,1,0:T(8,128)(2,1)S(1)}, f32[16,2,128]{2,1,0:T(2,128)}) custom-call(s32[1,4]{1,0:T(1,128)S(1)} %get-tuple-element.19.lengths_ref, bf16[4,8,4,16,128]{4,3,2,1,0:T(8,128)(2,1)S(1)} %get-tuple-element.26.early_ref, bf16[2,8,4,16,128]{4,3,2,1,0:T(8,128)(2,1)S(1)} %get-tuple-element.27.late_ref, ...), custom_call_target="tpu_custom_call" | custom-call | flops 2147483648 | bytes 1048576 | tf_op jit(solution)/shard_map/conv1/pallas_call | solution.py:511
  51.6 3.7 %all-to-all-start.2 = ((f32[16,2,128]{2,1,0:T(2,128)}), f32[16,2,128]{2,1,0:T(2,128)S(1)}, u32[]{:S(2)}, u32[]{:S(2)}) async-start(f32[16,2,128]{2,1,0:T(2,128)} %get-tuple-element.32), calls=%async_computation.2 | async-start | bytes 32768 | tf_op jit(solution)/shard_map/all_to_all | solution.py:519
  55.3 3.5 %collective-permute-start.1 = (bf16[2,8,4,16,128]{4,3,2,1,0:T(8,128)(2,1)S(1)}, bf16[2,8,4,16,128]{4,3,2,1,0:T(8,128)(2,1)S(1)}, u32[]{:S(2)}, u32[]{:S(2)}) collective-permute-start(bf16[2,8,4,16,128]{4,3,2,1,0:T(8,128)(2,1)S(1)} %get-tuple-element.30.tail_ref), channel_id=1, source_target_pairs={{0,1},{1,2},{2,3},{3,4},{4,5},{5,6},{6,7},{7,8},{8,9},{9,10},{10,1... | collective-permute-start | bytes 786440 | tf_op jit(solution)/shard_map/ppermute | solution.py:521
  58.9 0.0 copy-start.3
  58.9 0.0 copy-start.4
  58.9 3.8 %all-to-all-done.2.stats_ref = f32[16,2,128]{2,1,0:T(2,128)S(1)} async-done(((f32[16,2,128]{2,1,0:T(2,128)}), f32[16,2,128]{2,1,0:T(2,128)S(1)}, u32[]{:S(2)}, u32[]{:S(2)}) %all-to-all-start.2) | async-done | bytes 16416 | tf_op jit(solution)/shard_map/all_to_all | solution.py:519
  62.7 0.0 collective-permute-done.1.lead_ref
  62.7 0.0 copy-done.3
  62.7 0.0 copy-done.4
  62.7 4.6 %conv2.1 = bf16[32,2,2048]{2,1,0:T(2,128)(2,1)S(1)} custom-call(s32[1,4]{1,0:T(1,128)S(1)} %get-tuple-element.19.lengths_ref, bf16[64,32]{1,0:T(8,128)(2,1)S(1)} %beside.1.place_ref, bf16[4,8,4,16,128]{4,3,2,1,0:T(8,128)(2,1)S(1)} %get-tuple-element.26.early_ref, bf16[2,8,4,16,128]{4,3,2,1,0:T(8,128)(2,1)S(1)} %get-tuple-element.27.late_ref, ...), custom_call_target="tpu_custom_call" | custom-call | flops 2147483648 | bytes 1048576 | tf_op jit(solution)/shard_map/conv2/pallas_call | solution.py:522
  67.3 14.8 %all_to_all.22.back_ref = bf16[32,2,2048]{2,1,0:T(2,128)(2,1)S(1)} all-to-all(bf16[32,2,2048]{2,1,0:T(2,128)(2,1)S(1)} %conv2.1), channel_id=1, replica_groups=mesh['dp'=32,'tm'=16] {'dp'}, dimensions={0} | all-to-all | bytes 524288 | tf_op jit(solution)/shard_map/all_to_all | solution.py:530
  82.1 0.8 %place.1 = bf16[1,1,32,2048]{3,2,1,0:T(8,128)(2,1)} custom-call(bf16[32,64]{1,0:T(8,128)(2,1)S(1)} %get-tuple-element.22.select_ref, bf16[32,2,2048]{2,1,0:T(2,128)(2,1)S(1)} %all_to_all.22.back_ref), custom_call_target="tpu_custom_call" | custom-call | bytes 1048576 | tf_op jit(solution)/shard_map/place/pallas_call | solution.py:531
  (1 shorter events, 0.0 us)
Async XLA Ops:
  0.0 0.7 copy-start.1
  1.1 25.1 %copy-start.5 = (bf16[3,3,3,3,128]{4,3,2,1,0:T(4,128)(2,1)S(1)}, bf16[3,3,3,3,128]{4,3,2,1,0:T(4,128)(2,1)}, u32[]{:S(2)}) copy-start(bf16[3,3,3,3,128]{4,3,2,1,0:T(4,128)(2,1)} %weight_ref.3) | copy-start | bytes 62212
  20.1 8.2 %collective-permute-start = (bf16[32,4,128]{2,1,0:T(4,128)(2,1)S(1)}, bf16[32,4,128]{2,1,0:T(4,128)(2,1)S(1)}, u32[]{:S(2)}, u32[]{:S(2)}) collective-permute-start(bf16[32,4,128]{2,1,0:T(4,128)(2,1)S(1)} %all_to_all.20.own_ref), channel_id=1, source_target_pairs={{0,1},{1,2},{2,3},{3,4},{4,5},{5,6},{6,7},{7,8},{8,9},{9,10},{10,1... | collective-permute-start | bytes 98312 | tf_op jit(solution)/shard_map/ppermute | solution.py:492
  26.1 0.7 copy-start.9
  26.1 0.7 copy-start.10
  26.1 0.7 copy-start.11
  26.1 0.7 copy-start.6
  26.1 0.7 copy-start.7
  26.2 0.7 copy-start.8
  26.8 0.7 copy-start
  27.5 19.6 %copy-start.2 = (bf16[3,3,3,128,128]{4,3,2,1,0:T(8,128)(2,1)S(1)}, bf16[3,3,3,128,128]{4,3,2,1,0:T(8,128)(2,1)}, u32[]{:S(2)}) copy-start(bf16[3,3,3,128,128]{4,3,2,1,0:T(8,128)(2,1)} %weight_ref.4) | copy-start | bytes 2654212
  51.6 11.1 %all-to-all-start.2 = ((f32[16,2,128]{2,1,0:T(2,128)}), f32[16,2,128]{2,1,0:T(2,128)S(1)}, u32[]{:S(2)}, u32[]{:S(2)}) async-start(f32[16,2,128]{2,1,0:T(2,128)} %get-tuple-element.32), calls=%async_computation.2 | async-start | bytes 32768 | tf_op jit(solution)/shard_map/all_to_all | solution.py:519
  55.3 7.4 %collective-permute-start.1 = (bf16[2,8,4,16,128]{4,3,2,1,0:T(8,128)(2,1)S(1)}, bf16[2,8,4,16,128]{4,3,2,1,0:T(8,128)(2,1)S(1)}, u32[]{:S(2)}, u32[]{:S(2)}) collective-permute-start(bf16[2,8,4,16,128]{4,3,2,1,0:T(8,128)(2,1)S(1)} %get-tuple-element.30.tail_ref), channel_id=1, source_target_pairs={{0,1},{1,2},{2,3},{3,4},{4,5},{5,6},{6,7},{7,8},{8,9},{9,10},{10,1... | collective-permute-start | bytes 786440 | tf_op jit(solution)/shard_map/ppermute | solution.py:521
  58.9 3.9 %copy-start.3 = (bf16[3,3,3,128,128]{4,3,2,1,0:T(8,128)(2,1)S(1)}, bf16[3,3,3,128,128]{4,3,2,1,0:T(8,128)(2,1)}, u32[]{:S(2)}) copy-start(bf16[3,3,3,128,128]{4,3,2,1,0:T(8,128)(2,1)} %weight_ref.5) | copy-start | bytes 2654212
  58.9 3.9 %copy-start.4 = (bf16[3,3,128,128]{3,2,1,0:T(8,128)(2,1)S(1)}, bf16[3,3,128,128]{3,2,1,0:T(8,128)(2,1)}, u32[]{:S(2)}) copy-start(bf16[3,3,128,128]{3,2,1,0:T(8,128)(2,1)} %down_ref.1) | copy-start | bytes 884740

commit v7 on v6

--- a/solution.py
+++ b/solution.py
@@ -392,7 +392,7 @@
 
 def conv2_kernel(
     lengths_ref, place_ref, early_ref, late_ref, middle_ref, tail_ref, lead_ref, stats_ref, bounds_ref, vectors_ref, weight_ref, down_ref,
-    out_ref, low_ref, high_ref, norm_ref, resid_ref, later_ref, latent_ref,
+    out_ref, low_ref, high_ref, norm_ref, resid_ref, later_ref,
 ):
     column = lax.axis_index("tm")
     ends = clip_ends(lengths_ref)
@@ -432,13 +432,10 @@
             ]
             taps.append(jnp.concatenate(parts, axis=0))
     latent = mm(jnp.concatenate(taps, axis=1), down)
-    for f in range(FT):
-        for j in range(4):
-            for w in range(4):
-                at = f * 128 + j * 32 + w * 8
-                latent_ref[w, f * 8 : f * 8 + 8, j * CH : (j + 1) * CH] = latent[at : at + 8]
+    piece = lambda f, j, w: latent[f * 128 + j * 32 + w * 8 :][:8]
     for w in range(4):
-        rows = mm(place_ref[...], latent_ref[w].astype(BF16))
+        units = [jnp.concatenate([piece(f, j, w) for f in range(FT)], axis=0) for j in range(4)]
+        rows = mm(place_ref[...], jnp.concatenate(units, axis=1).astype(BF16))
         out_ref[:, :, w * 512 : (w + 1) * 512] = rows.reshape(NDP, 2, 512).astype(BF16)
 
 
@@ -524,7 +521,7 @@
         "conv2",
         [VMEM] * 12,
         [((NDP, 2, 2048), BF16)],
-        act + [norm] + [pltpu.VMEM((2, 9, 5, 16, CH), BF16)] * 2 + [pltpu.VMEM((4, 32, 512), F32)],
+        act + [norm] + [pltpu.VMEM((2, 9, 5, 16, CH), BF16)] * 2,
         flops=1 << 31,
     )(lengths, place, early, late, middle, tail, lead, stats, bounds, vectors, conv2_weight, down_weight)
     returned = lax.all_to_all(packed, "dp", split_axis=0, concat_axis=0, tiled=True)

time: 83.5 us -> 83.5 us (level)
  no operation moved by 1% of the time
where the time goes in v7:
time: 83.5 us; the launch traced here: 82.9 us
  blocking collectives  51.5 us (62%)
  starting transfers between devices  13.2 us (16%)
  Pallas kernels  12.7 us (15%)
  waiting for transfers between devices  3.84 us (5%)
    all_to_all x2, blocking collectives, per_device(): lax.all_to_all(packed, 'dp', split_axis=0, concat_axis=0, tiled=True)  33.7 us
    all_to_all x1, blocking collectives, per_device(): stats = lax.all_to_all(stats, 'tm', split_axis=0, concat_axis=0, tiled=True)  17.8 us
    ppermute x1, starting transfers between devices, per_device(): before = lax.ppermute(arrived, 'tm', onward)  5.98 us
    pallas_call x1, Pallas kernels, per_device(): kernel_call(conv2_kernel, 'conv2', [VMEM] * 12, [((NDP, 2, 2048), BF16)],...  4.58 us
    pallas_call x1, Pallas kernels, per_device(): kernel_call(conv1_kernel, 'conv1', [VMEM] * 7, [frames(2), frames(2), ((N...  4.45 us
    all_to_all x1, waiting for transfers between devices, per_device(): stats = lax.all_to_all(stats, 'tm', split_axis=0, concat_axis=0, tiled=True)  3.83 us
    all_to_all x1, starting transfers between devices, per_device(): stats = lax.all_to_all(stats, 'tm', split_axis=0, concat_axis=0, tiled=True)  3.68 us
    ppermute x1, starting transfers between devices, per_device(): lead = lax.ppermute(tail, 'tm', onward)  3.53 us
  transfers between devices with their start and end apart: 3, of which 1 were waited for; matrix products, arithmetic and copies ran while one was open for 0% of the time, Pallas kernels for 2%

profile of v7, /device:TPU:1, one launch (start us, length us, event | category | flops | bytes accessed | tf_op | source)
XLA Modules:
  0.0 82.9 jit_solution(16326924514613559283)
XLA Ops:
  0.0 0.0 copy-start.1
  0.0 0.7 convert_bitcast_fusion.counts_ref
  0.7 0.0 copy-done.1
  0.7 0.3 pack.1
  1.1 0.0 copy-start.5
  1.1 19.0 %all_to_all.20.own_ref = bf16[32,4,128]{2,1,0:T(4,128)(2,1)S(1)} all-to-all(bf16[32,4,128]{2,1,0:T(4,128)(2,1)S(1)} %pack.1), channel_id=1, replica_groups=mesh['dp'=32,'tm'=16] {'dp'}, dimensions={0} | all-to-all | bytes 65536 | tf_op jit(solution)/shard_map/all_to_all | solution.py:479
  20.1 6.0 %collective-permute-start = (bf16[32,4,128]{2,1,0:T(4,128)(2,1)S(1)}, bf16[32,4,128]{2,1,0:T(4,128)(2,1)S(1)}, u32[]{:S(2)}, u32[]{:S(2)}) collective-permute-start(bf16[32,4,128]{2,1,0:T(4,128)(2,1)S(1)} %all_to_all.20.own_ref), channel_id=1, source_target_pairs={{0,1},{1,2},{2,3},{3,4},{4,5},{5,6},{6,7},{7,8},{8,9},{9,10},{10,1... | collective-permute-start | bytes 98312 | tf_op jit(solution)/shard_map/ppermute | solution.py:489
  26.1 0.0 copy-start.9
  26.1 0.0 copy-start.10
  26.1 0.0 copy-start.11
  26.1 0.0 copy-start.6
  26.1 0.0 copy-start.7
  26.2 0.0 copy-start.8
  26.2 0.0 copy-done.5
  26.2 0.6 copy-done.9
  26.7 0.0 copy-done.10
  26.8 0.0 copy-done.11
  26.8 0.0 copy-done.6
  26.8 0.0 copy-done.7
  26.8 0.0 copy-done.8
  26.8 0.0 copy-start
  26.8 0.6 spread.1
  27.4 0.1 copy-done
  27.5 0.0 copy-start.2
  27.5 0.7 late.1
  28.3 0.0 collective-permute-done.prev_ref
  28.3 1.1 %early.1 = (bf16[4,8,4,16,128]{4,3,2,1,0:T(8,128)(2,1)S(1)}, f32[16,2,128]{2,1,0:T(2,128)S(1)}) custom-call(s32[1,4]{1,0:T(1,128)S(1)} %get-tuple-element.19.lengths_ref, bf16[32,4,128]{2,1,0:T(4,128)(2,1)S(1)} %collective-permute-done.prev_ref, bf16[4,64,128]{2,1,0:T(8,128)(2,1)S(1)} %get-tuple-element.24.own_ref, f32[8,128]{1,0:T(8,128)S(1)} %get-tuple-element.25.part_ref, ...), custom_call_target="tpu_custom_call" | custom-call | bytes 1048576 | tf_op jit(solution)/shard_map/early/pallas_call | solution.py:498
  29.4 17.8 %all_to_all.21.stats_ref = f32[16,2,128]{2,1,0:T(2,128)S(1)} all-to-all(f32[16,2,128]{2,1,0:T(2,128)S(1)} %get-tuple-element.28), channel_id=1, replica_groups=mesh['dp'=32,'tm'=16] {'tm'}, dimensions={0} | all-to-all | bytes 32768 | tf_op jit(solution)/shard_map/all_to_all | solution.py:505
  47.2 0.0 copy-done.2
  47.2 4.4 %conv1.1 = (bf16[2,8,4,16,128]{4,3,2,1,0:T(8,128)(2,1)S(1)}, bf16[2,8,4,16,128]{4,3,2,1,0:T(8,128)(2,1)S(1)}, f32[16,2,128]{2,1,0:T(2,128)}) custom-call(s32[1,4]{1,0:T(1,128)S(1)} %get-tuple-element.19.lengths_ref, bf16[4,8,4,16,128]{4,3,2,1,0:T(8,128)(2,1)S(1)} %get-tuple-element.26.early_ref, bf16[2,8,4,16,128]{4,3,2,1,0:T(8,128)(2,1)S(1)} %get-tuple-element.27.late_ref, ...), custom_call_target="tpu_custom_call" | custom-call | flops 2147483648 | bytes 1048576 | tf_op jit(solution)/shard_map/conv1/pallas_call | solution.py:508
  51.6 3.7 %all-to-all-start.2 = ((f32[16,2,128]{2,1,0:T(2,128)}), f32[16,2,128]{2,1,0:T(2,128)S(1)}, u32[]{:S(2)}, u32[]{:S(2)}) async-start(f32[16,2,128]{2,1,0:T(2,128)} %get-tuple-element.32), calls=%async_computation.2 | async-start | bytes 32768 | tf_op jit(solution)/shard_map/all_to_all | solution.py:516
  55.3 3.5 %collective-permute-start.1 = (bf16[2,8,4,16,128]{4,3,2,1,0:T(8,128)(2,1)S(1)}, bf16[2,8,4,16,128]{4,3,2,1,0:T(8,128)(2,1)S(1)}, u32[]{:S(2)}, u32[]{:S(2)}) collective-permute-start(bf16[2,8,4,16,128]{4,3,2,1,0:T(8,128)(2,1)S(1)} %get-tuple-element.30.tail_ref), channel_id=1, source_target_pairs={{0,1},{1,2},{2,3},{3,4},{4,5},{5,6},{6,7},{7,8},{8,9},{9,10},{10,1... | collective-permute-start | bytes 786440 | tf_op jit(solution)/shard_map/ppermute | solution.py:518
  58.9 0.0 copy-start.3
  58.9 0.0 copy-start.4
  58.9 3.8 %all-to-all-done.2.stats_ref = f32[16,2,128]{2,1,0:T(2,128)S(1)} async-done(((f32[16,2,128]{2,1,0:T(2,128)}), f32[16,2,128]{2,1,0:T(2,128)S(1)}, u32[]{:S(2)}, u32[]{:S(2)}) %all-to-all-start.2) | async-done | bytes 16416 | tf_op jit(solution)/shard_map/all_to_all | solution.py:516
  62.7 0.0 collective-permute-done.1.lead_ref
  62.7 0.0 copy-done.3
  62.7 0.0 copy-done.4
  62.7 4.6 %conv2.1 = bf16[32,2,2048]{2,1,0:T(2,128)(2,1)S(1)} custom-call(s32[1,4]{1,0:T(1,128)S(1)} %get-tuple-element.19.lengths_ref, bf16[64,32]{1,0:T(8,128)(2,1)S(1)} %beside.1.place_ref, bf16[4,8,4,16,128]{4,3,2,1,0:T(8,128)(2,1)S(1)} %get-tuple-element.26.early_ref, bf16[2,8,4,16,128]{4,3,2,1,0:T(8,128)(2,1)S(1)} %get-tuple-element.27.late_ref, ...), custom_call_target="tpu_custom_call" | custom-call | flops 2147483648 | bytes 1048576 | tf_op jit(solution)/shard_map/conv2/pallas_call | solution.py:519
  67.3 14.8 %all_to_all.22.back_ref = bf16[32,2,2048]{2,1,0:T(2,128)(2,1)S(1)} all-to-all(bf16[32,2,2048]{2,1,0:T(2,128)(2,1)S(1)} %conv2.1), channel_id=1, replica_groups=mesh['dp'=32,'tm'=16] {'dp'}, dimensions={0} | all-to-all | bytes 524288 | tf_op jit(solution)/shard_map/all_to_all | solution.py:527
  82.1 0.8 %place.1 = bf16[1,1,32,2048]{3,2,1,0:T(8,128)(2,1)} custom-call(bf16[32,64]{1,0:T(8,128)(2,1)S(1)} %get-tuple-element.22.select_ref, bf16[32,2,2048]{2,1,0:T(2,128)(2,1)S(1)} %all_to_all.22.back_ref), custom_call_target="tpu_custom_call" | custom-call | bytes 1048576 | tf_op jit(solution)/shard_map/place/pallas_call | solution.py:528
  (1 shorter events, 0.0 us)
Async XLA Ops:
  0.0 0.7 copy-start.1
  1.1 25.1 %copy-start.5 = (bf16[3,3,3,3,128]{4,3,2,1,0:T(4,128)(2,1)S(1)}, bf16[3,3,3,3,128]{4,3,2,1,0:T(4,128)(2,1)}, u32[]{:S(2)}) copy-start(bf16[3,3,3,3,128]{4,3,2,1,0:T(4,128)(2,1)} %weight_ref.3) | copy-start | bytes 62212
  20.1 8.2 %collective-permute-start = (bf16[32,4,128]{2,1,0:T(4,128)(2,1)S(1)}, bf16[32,4,128]{2,1,0:T(4,128)(2,1)S(1)}, u32[]{:S(2)}, u32[]{:S(2)}) collective-permute-start(bf16[32,4,128]{2,1,0:T(4,128)(2,1)S(1)} %all_to_all.20.own_ref), channel_id=1, source_target_pairs={{0,1},{1,2},{2,3},{3,4},{4,5},{5,6},{6,7},{7,8},{8,9},{9,10},{10,1... | collective-permute-start | bytes 98312 | tf_op jit(solution)/shard_map/ppermute | solution.py:489
  26.1 0.7 copy-start.9
  26.1 0.7 copy-start.10
  26.1 0.7 copy-start.11
  26.1 0.7 copy-start.6
  26.1 0.7 copy-start.7
  26.2 0.7 copy-start.8
  26.8 0.7 copy-start
  27.5 19.6 %copy-start.2 = (bf16[3,3,3,128,128]{4,3,2,1,0:T(8,128)(2,1)S(1)}, bf16[3,3,3,128,128]{4,3,2,1,0:T(8,128)(2,1)}, u32[]{:S(2)}) copy-start(bf16[3,3,3,128,128]{4,3,2,1,0:T(8,128)(2,1)} %weight_ref.4) | copy-start | bytes 2654212
  51.6 11.1 %all-to-all-start.2 = ((f32[16,2,128]{2,1,0:T(2,128)}), f32[16,2,128]{2,1,0:T(2,128)S(1)}, u32[]{:S(2)}, u32[]{:S(2)}) async-start(f32[16,2,128]{2,1,0:T(2,128)} %get-tuple-element.32), calls=%async_computation.2 | async-start | bytes 32768 | tf_op jit(solution)/shard_map/all_to_all | solution.py:516
  55.3 7.4 %collective-permute-start.1 = (bf16[2,8,4,16,128]{4,3,2,1,0:T(8,128)(2,1)S(1)}, bf16[2,8,4,16,128]{4,3,2,1,0:T(8,128)(2,1)S(1)}, u32[]{:S(2)}, u32[]{:S(2)}) collective-permute-start(bf16[2,8,4,16,128]{4,3,2,1,0:T(8,128)(2,1)S(1)} %get-tuple-element.30.tail_ref), channel_id=1, source_target_pairs={{0,1},{1,2},{2,3},{3,4},{4,5},{5,6},{6,7},{7,8},{8,9},{9,10},{10,1... | collective-permute-start | bytes 786440 | tf_op jit(solution)/shard_map/ppermute | solution.py:518
  58.9 3.9 %copy-start.3 = (bf16[3,3,3,128,128]{4,3,2,1,0:T(8,128)(2,1)S(1)}, bf16[3,3,3,128,128]{4,3,2,1,0:T(8,128)(2,1)}, u32[]{:S(2)}) copy-start(bf16[3,3,3,128,128]{4,3,2,1,0:T(8,128)(2,1)} %weight_ref.5) | copy-start | bytes 2654212
  58.9 3.9 %copy-start.4 = (bf16[3,3,128,128]{3,2,1,0:T(8,128)(2,1)S(1)}, bf16[3,3,128,128]{3,2,1,0:T(8,128)(2,1)}, u32[]{:S(2)}) copy-start(bf16[3,3,128,128]{3,2,1,0:T(8,128)(2,1)} %down_ref.1) | copy-start | bytes 884740
